TPU v7x, 32 devices: a whole 2x2x4 slice. The times are simulated.
32 devices in a mesh: groups: 2 (over y), ctx: 4 (over z), roll: 4 (over x, core).
Axes of the slice: x: 2, y: 2, z: 4, core: 2. Of those that a mesh axis runs over, the one named last changes fastest.
Arguments:
- queries: bfloat16 [4096, 8192], P(('groups', 'ctx', 'roll')), parts along dimension 0, may hold values from -1.6953125 to 1.6953125
- cotangent: bfloat16 [4096, 8192], P(('groups', 'ctx', 'roll')), parts along dimension 0, may hold values from -6 to 6
- out_dot: float32 [4096, 64], P(('groups', 'ctx', 'roll')), parts along dimension 0, may hold values from -48 to 48
- norm_offset: float32 [4096, 64], P(('groups', 'ctx', 'roll')), parts along dimension 0, may hold values from 0.5 to 2.5
- prompt_kv: bfloat16 [2, 512, 1024], P(None, ('groups', 'ctx')), parts along dimension 1, may hold values from -1.6953125 to 1.6953125
- prompt_x: bfloat16 [512, 8192], P(('groups', 'ctx')), parts along dimension 0, may hold values from -6 to 6
- block_ids: int32 [128], P(('groups', 'ctx', 'roll')), parts along dimension 0, may hold values from 0 to 63, each once
- lengths: int32 [32], P('groups'), parts along dimension 0, may hold values from 32 to 128, as said below
- advantages: float32 [32], P('groups'), parts along dimension 0, may hold values from -3 to 3
- adv_index: int32 [32], P('groups'), parts along dimension 0, may hold values from 0 to 15, each once
Outputs:
- query_grad: bfloat16 [4096, 8192], P(('groups', 'ctx', 'roll')), parts along dimension 0
- kv_grad: float32 [2, 512, 1024], P(None, ('groups', 'ctx'), 'roll'), parts along dimension 1
- kv_weight_grad: float32 [2, 16384, 1024], P(None, ('groups', 'ctx'), 'roll'), parts along dimension 1
There are 2 independent parts, one for each index of `groups`. A program takes and returns all parts, laid end to end along the dimension named above; each array names one. Nothing has to cross between parts.
Inputs may be any that keep to these rules, and one draw needn't show every extreme that they name: `lengths`: every rollout has a length of at least 32, and some rollout has length 128. `block_ids`: each id appears once. `adv_index`: each entry appears once.
All inputs are finite; a program needn't handle non-finite values.
Results may differ from a plain program's by a relative error of at most 0.0057.
Values may be sent and summed in bfloat16 or wider, within the bound.
No kernel may reach another device: no remote copies, remote signals or barrier semaphores. Data moves between devices by JAX's collectives and lax.ppermute only.
A program may use at most 128 MiB of HBM per device.

v0:
```python
import math

import jax
import jax.numpy as jnp
from jax import lax
from jax.sharding import PartitionSpec as P

HD = 128
BLOCK = 32


def rollout_weights(block_ids, lengths, advantages, adv_index, blocks_total):
    count = lengths.shape[0]
    per_rollout = blocks_total // count
    resp_max = per_rollout * BLOCK
    rollout = block_ids // per_rollout
    slot = block_ids % per_rollout
    picks = rollout[:, None] == jnp.arange(count, dtype=jnp.int32)[None, :]
    length_of = jnp.sum(jnp.where(picks, lengths[None, :], 0), axis=1)
    table = adv_index[:, None] == jnp.arange(count, dtype=jnp.int32)[None, :]
    adv_rollout = jnp.sum(jnp.where(table, advantages[None, :], jnp.float32(0.0)), axis=1)
    adv_block = jnp.sum(jnp.where(picks, adv_rollout[None, :], jnp.float32(0.0)), axis=1)
    position = slot[:, None] * BLOCK + jnp.arange(BLOCK, dtype=jnp.int32)[None, :]
    scaled = adv_block * resp_max / length_of.astype(jnp.float32)
    weights = jnp.where(position < length_of[:, None], scaled[:, None], jnp.float32(0.0))
    return weights.reshape(-1)


def spread(x, kv_heads):
    tokens = x.shape[0]
    return x.reshape(tokens, kv_heads, -1, HD).transpose(1, 0, 2, 3).reshape(kv_heads, -1, HD)


def spread_small(x, kv_heads):
    tokens = x.shape[0]
    return x.reshape(tokens, kv_heads, -1).transpose(1, 0, 2).reshape(kv_heads, -1)


def piece_grads(heads, piece, scale, slab):
    q_heads, do_heads, d_heads, o_heads = heads
    kv_heads = q_heads.shape[0]
    length = piece.shape[1]
    split = piece.reshape(2, length, kv_heads, HD).transpose(0, 2, 1, 3)
    inner = (((1,), (1,)), ((), ()))
    outer = (((0,), (0,)), ((), ()))

    def one_head(args):
        qg, dog, dg, og, kg, vg = args
        scores = lax.dot_general(qg, kg, inner, preferred_element_type=jnp.float32) * scale
        prob = jnp.exp(scores - og[:, None]) / slab
        prob_low = prob.astype(jnp.bfloat16)
        dprob = lax.dot_general(dog, vg, inner, preferred_element_type=jnp.float32)
        dscore = (prob * (dprob - dg[:, None]) * scale).astype(jnp.bfloat16)
        dq = jnp.dot(dscore, kg, preferred_element_type=jnp.float32)
        dk = lax.dot_general(dscore, qg, outer, preferred_element_type=jnp.float32)
        dv = lax.dot_general(prob_low, dog, outer, preferred_element_type=jnp.float32)
        return (dq, dk, dv)

    dq, dk, dv = lax.map(one_head, (q_heads, do_heads, d_heads, o_heads, split[0], split[1]))
    grads = jnp.stack([dk, dv]).transpose(0, 2, 1, 3).reshape(2, length, kv_heads * HD)
    return (dq, grads)


def unspread(dq_heads, tokens):
    kv_heads = dq_heads.shape[0]
    return dq_heads.reshape(kv_heads, tokens, -1, HD).transpose(1, 0, 2, 3).reshape(tokens, -1)


def on_device(
    queries,
    cotangent,
    out_dot,
    norm_offset,
    prompt_kv,
    prompt_x,
    block_ids,
    lengths,
    advantages,
    adv_index,
):
    ctx_count = lax.axis_size("ctx")
    roll_count = lax.axis_size("roll")
    tokens = queries.shape[0]
    kv_width = prompt_kv.shape[2]
    kv_heads = kv_width // HD
    owned_rows = prompt_kv.shape[1]
    slab = owned_rows * ctx_count
    scale = 1.0 / math.sqrt(HD)
    weights = rollout_weights(
        block_ids, lengths, advantages, adv_index, block_ids.shape[0] * ctx_count * roll_count
    )
    grad_out = (cotangent.astype(jnp.float32) * weights[:, None]).astype(jnp.bfloat16)
    delta = weights[:, None] * out_dot
    heads = (
        spread(queries, kv_heads),
        spread(grad_out, kv_heads),
        spread_small(delta, kv_heads),
        spread_small(norm_offset, kv_heads),
    )
    dq_part, grads = piece_grads(
        heads, lax.all_gather(prompt_kv, "ctx", axis=1, tiled=True), scale, slab
    )
    by_heads = lax.psum_scatter(grads, "roll", scatter_dimension=2, tiled=True)
    owned = lax.psum_scatter(by_heads, "ctx", scatter_dimension=1, tiled=True)
    query_grad = unspread(dq_part, tokens).astype(jnp.bfloat16)
    owned_low = owned.astype(jnp.bfloat16)
    x_local = lax.all_to_all(prompt_x, "ctx", split_axis=1, concat_axis=0, tiled=True)
    summed = jnp.einsum(
        "sd,ksc->dkc",
        x_local,
        lax.all_gather(owned_low, "ctx", axis=1, tiled=True),
        preferred_element_type=jnp.float32,
    )
    weight_grad = summed.transpose(1, 0, 2)
    return (query_grad, owned, weight_grad)


def solution(mesh):
    placed = (
        P(("groups", "ctx", "roll"), None),
        P(("groups", "ctx", "roll"), None),
        P(("groups", "ctx", "roll"), None),
        P(("groups", "ctx", "roll"), None),
        P(None, ("groups", "ctx"), None),
        P(("groups", "ctx"), None),
        P(("groups", "ctx", "roll")),
        P("groups"),
        P("groups"),
        P("groups"),
    )
    return jax.shard_map(
        on_device,
        mesh=mesh,
        in_specs=placed,
        out_specs=(
            P(("groups", "ctx", "roll"), None),
            P(None, ("groups", "ctx"), "roll"),
            P(None, ("groups", "ctx"), "roll"),
        ),
        check_vma=False,
    )
```

profile of v0, /device:TPU:0, one launch (start us, length us, event | category | flops | bytes accessed | tf_op | source)
XLA Modules:
  0.0 190.3 jit_solution(14326844349837195630)
XLA Ops:
  7.2 1.9 %copy.45 = bf16[2,64,1024]{2,0,1:T(2,128)(2,1)} copy(bf16[2,64,1024]{2,1,0:T(8,128)(2,1)} %param.16) | data formatting | bytes 524288 | tf_op args[4]
  11.9 2.2 %fusion.29 = bf16[16,8,64,128]{3,1,2,0:T(8,128)(2,1)S(1)} fusion(bf16[128,8192]{1,0:T(8,128)(2,1)} %param.13, f32[128]{0:T(128)S(1)} %select_n.41), kind=kLoop, calls=%fused_computation.38 | loop fusion | flops 3145728 | bytes 4194816
  14.2 1.9 %copy.61 = bf16[16,8,64,128]{3,2,1,0:T(8,128)(2,1)} copy(bf16[16,8,64,128]{3,1,2,0:T(8,128)(2,1)S(1)} %fusion.29) | data formatting | bytes 4194304
  16.1 1.9 %copy.60 = bf16[16,8,64,128]{3,2,1,0:T(8,128)(2,1)} copy(bf16[16,8,64,128]{3,1,2,0:T(8,128)(2,1)S(1)} %bitcast.127) | data formatting | bytes 4194304
  19.0 4.8 %copy_bitcast_fusion.2 = (bf16[8,1024,128]{2,1,0:T(8,128)(2,1)S(1)}, bf16[8,1024,128]{2,1,0:T(8,128)(2,1)}) fusion(bf16[128,8,8,128]{3,2,1,0:T(8,128)(2,1)} %bitcast.123, bf16[128,8,8,128]{3,2,1,0:T(8,128)(2,1)} %bitcast.124), kind=kLoop, calls=%fused_computation.42 | loop fusion | bytes 8388608 | tf_op jit(solution)/shard_map/reshape | solution.py:31
  23.7 16.5 %all-gather.2.cloned.1.call-done = bf16[2,256,1024]{2,0,1:T(2,128)(2,1)} async-done(((bf16[2,64,1024]{2,0,1:T(2,128)(2,1)}), bf16[2,256,1024]{2,0,1:T(2,128)(2,1)}) %all-gather.2.cloned.1.call-update) | async-done | bytes 1048592 | tf_op jit(solution)/shard_map/all_gather | solution.py:101
  40.2 2.4 %copy.46 = bf16[2,256,1024]{1,2,0:T(8,128)(2,1)S(1)} copy(bf16[2,256,1024]{2,0,1:T(2,128)(2,1)} %all-gather.2.cloned.1.call-done) | data formatting | bytes 2097152 | tf_op jit(solution)/shard_map/all_gather | solution.py:101
  43.7 58.2 %while.14 = (s32[]{:T(128)}, bf16[8,1024,128]{2,1,0:T(8,128)(2,1)}, f32[8,256,128]{2,1,0:T(8,128)}, f32[8,256,128]{2,1,0:T(8,128)}, bf16[8,1024,128]{2,1,0:T(8,1...) while((s32[]{:T(128)}, bf16[8,1024,128]{2,1,0:T(8,128)(2,1)}, ...), condition=%wide.region_4.5_spmd, body=%wide.region_3.4_spmd.sunk | while | flops 337641472 | bytes 6780017 | solution.py:59
  46.2 1.9 fusion.63
  48.0 1.9 %fusion.64 = f32[8,256,128]{2,1,0:T(8,128)} fusion(f32[8,256,128]{2,1,0:T(8,128)} %get-tuple-element.208, s32[]{:T(128)} %get-tuple-element.206, bf16[1024,256]{1,0:T(8,128)(2,1)S(1)} %fusion.62, bf16[8,1024,128]{2,1,0:T(8,128)(2,1)} %get-tuple-element.221), kind=kOutput, calls=%fused_computation.13.clone.1 | convolution fusion | flops 67108864 | bytes 918528 | tf_op jit(solution)/shard_map/while/body/eval_jaxpr/dot_general | solution.py:55
  53.4 1.8 fusion.63
  55.3 1.9 %fusion.64 = f32[8,256,128]{2,1,0:T(8,128)} fusion(f32[8,256,128]{2,1,0:T(8,128)} %get-tuple-element.208, s32[]{:T(128)} %get-tuple-element.206, bf16[1024,256]{1,0:T(8,128)(2,1)S(1)} %fusion.62, bf16[8,1024,128]{2,1,0:T(8,128)(2,1)} %get-tuple-element.221), kind=kOutput, calls=%fused_computation.13.clone.1 | convolution fusion | flops 67108864 | bytes 918528 | tf_op jit(solution)/shard_map/while/body/eval_jaxpr/dot_general | solution.py:55
  60.7 1.9 fusion.63
  62.5 2.0 %fusion.64 = f32[8,256,128]{2,1,0:T(8,128)} fusion(f32[8,256,128]{2,1,0:T(8,128)} %get-tuple-element.208, s32[]{:T(128)} %get-tuple-element.206, bf16[1024,256]{1,0:T(8,128)(2,1)S(1)} %fusion.62, bf16[8,1024,128]{2,1,0:T(8,128)(2,1)} %get-tuple-element.221), kind=kOutput, calls=%fused_computation.13.clone.1 | convolution fusion | flops 67108864 | bytes 918528 | tf_op jit(solution)/shard_map/while/body/eval_jaxpr/dot_general | solution.py:55
  68.0 1.8 fusion.63
  69.8 1.9 %fusion.64 = f32[8,256,128]{2,1,0:T(8,128)} fusion(f32[8,256,128]{2,1,0:T(8,128)} %get-tuple-element.208, s32[]{:T(128)} %get-tuple-element.206, bf16[1024,256]{1,0:T(8,128)(2,1)S(1)} %fusion.62, bf16[8,1024,128]{2,1,0:T(8,128)(2,1)} %get-tuple-element.221), kind=kOutput, calls=%fused_computation.13.clone.1 | convolution fusion | flops 67108864 | bytes 918528 | tf_op jit(solution)/shard_map/while/body/eval_jaxpr/dot_general | solution.py:55
  75.3 1.8 fusion.63
  77.1 1.9 %fusion.64 = f32[8,256,128]{2,1,0:T(8,128)} fusion(f32[8,256,128]{2,1,0:T(8,128)} %get-tuple-element.208, s32[]{:T(128)} %get-tuple-element.206, bf16[1024,256]{1,0:T(8,128)(2,1)S(1)} %fusion.62, bf16[8,1024,128]{2,1,0:T(8,128)(2,1)} %get-tuple-element.221), kind=kOutput, calls=%fused_computation.13.clone.1 | convolution fusion | flops 67108864 | bytes 918528 | tf_op jit(solution)/shard_map/while/body/eval_jaxpr/dot_general | solution.py:55
  82.5 1.9 fusion.63
  84.4 2.0 %fusion.64 = f32[8,256,128]{2,1,0:T(8,128)} fusion(f32[8,256,128]{2,1,0:T(8,128)} %get-tuple-element.208, s32[]{:T(128)} %get-tuple-element.206, bf16[1024,256]{1,0:T(8,128)(2,1)S(1)} %fusion.62, bf16[8,1024,128]{2,1,0:T(8,128)(2,1)} %get-tuple-element.221), kind=kOutput, calls=%fused_computation.13.clone.1 | convolution fusion | flops 67108864 | bytes 918528 | tf_op jit(solution)/shard_map/while/body/eval_jaxpr/dot_general | solution.py:55
  89.8 1.8 fusion.63
  91.7 1.9 %fusion.64 = f32[8,256,128]{2,1,0:T(8,128)} fusion(f32[8,256,128]{2,1,0:T(8,128)} %get-tuple-element.208, s32[]{:T(128)} %get-tuple-element.206, bf16[1024,256]{1,0:T(8,128)(2,1)S(1)} %fusion.62, bf16[8,1024,128]{2,1,0:T(8,128)(2,1)} %get-tuple-element.221), kind=kOutput, calls=%fused_computation.13.clone.1 | convolution fusion | flops 67108864 | bytes 918528 | tf_op jit(solution)/shard_map/while/body/eval_jaxpr/dot_general | solution.py:55
  97.1 1.8 fusion.63
  98.9 2.0 %fusion.64 = f32[8,256,128]{2,1,0:T(8,128)} fusion(f32[8,256,128]{2,1,0:T(8,128)} %get-tuple-element.208, s32[]{:T(128)} %get-tuple-element.206, bf16[1024,256]{1,0:T(8,128)(2,1)S(1)} %fusion.62, bf16[8,1024,128]{2,1,0:T(8,128)(2,1)} %get-tuple-element.221), kind=kOutput, calls=%fused_computation.13.clone.1 | convolution fusion | flops 67108864 | bytes 918528 | tf_op jit(solution)/shard_map/while/body/eval_jaxpr/dot_general | solution.py:55
  101.9 3.1 %copy_bitcast_fusion.1 = f32[2,256,1024]{2,1,0:T(8,128)} fusion(f32[1,8,256,128]{3,2,1,0:T(8,128)} %bitcast.134, f32[1,8,256,128]{3,2,1,0:T(8,128)} %bitcast.133), kind=kLoop, calls=%fused_computation.40 | loop fusion | flops 524288 | bytes 4194304 | tf_op jit(solution)/shard_map/reshape | solution.py:60
  107.3 3.6 %all-to-all-start = ((bf16[64,4,2048]{2,0,1:T(8,128)(2,1)}), bf16[64,4,2048]{2,0,1:T(8,128)(2,1)S(1)}, u32[]{:S(2)}, u32[]{:S(2)}) async-start(bf16[64,4,2048]{2,0,1:T(8,128)(2,1)} %bitcast.93), calls=%async_computation.2 | async-start | bytes 2097152 | tf_op jit(solution)/shard_map/all_to_all | solution.py:107
  110.9 25.2 %reduce-scatter.3.cloned.1.call-done = f32[2,256,256]{2,1,0:T(8,128)} async-done(((f32[2,256,1024]{2,1,0:T(8,128)}), f32[2,256,256]{2,1,0:T(8,128)}) %reduce-scatter.3.cloned.1.call-update) | async-done | bytes 524304 | tf_op jit(solution)/shard_map/reduce_scatter | solution.py:103
  136.7 3.1 %copy.68 = bf16[16,8,64,128]{3,1,2,0:T(8,128)(2,1)} copy(bf16[16,8,64,128]{3,2,1,0:T(8,128)(2,1)S(1)} %bitcast.122) | data formatting | bytes 4194304
  139.8 20.9 %reduce-scatter.5.cloned.1.call-done = f32[2,64,256]{2,1,0:T(8,128)} async-done(((f32[2,256,256]{2,1,0:T(8,128)}), f32[2,64,256]{2,1,0:T(8,128)}) %reduce-scatter.5.cloned.1.call-update) | async-done | bytes 131088 | tf_op jit(solution)/shard_map/reduce_scatter | solution.py:104
  161.6 14.1 %all_gather.7 = bf16[2,256,256]{2,1,0:T(8,128)(2,1)S(1)} all-gather(bf16[2,64,256]{2,1,0:T(8,128)(2,1)S(1)} %convert_element_type.41), channel_id=1, replica_groups=mesh['groups'=2,'ctx'=4,'roll'=4] {'ctx'}, dimensions={1}, use_global_device_ids=true | all-gather | bytes 327680 | tf_op jit(solution)/shard_map/all_gather | solution.py:111
  175.7 2.7 %convolution_bitcast_fusion.3 = f32[2,2048,256]{1,2,0:T(8,128)} fusion(bf16[2,256,256]{2,1,0:T(8,128)(2,1)S(1)} %all_gather.7, bf16[256,2048,1]{1,0,2:T(8,128)(2,1)S(1)} %bitcast.126), kind=kOutput, calls=%fused_computation.37 | convolution fusion | flops 536870912 | bytes 5505024 | tf_op jit(solution)/shard_map/sd,ksc->dkc/dot_general | solution.py:108
  178.4 5.3 %copy.55 = f32[2,2048,256]{2,1,0:T(8,128)} copy(f32[2,2048,256]{1,2,0:T(8,128)} %convolution_bitcast_fusion.3) | data formatting | bytes 8388608
  (68 shorter events, 36.3 us)
Async XLA Ops:
  7.2 33.1 %all-gather.2.cloned.1.call-start = ((), (), s32[]{:S(2)}) async-start(), calls=%async_computation.3 | async-start | bytes 1310720 | tf_op jit(solution)/shard_map/all_gather | solution.py:101
  9.2 126.9 %reduce-scatter.3.cloned.1.call-start = ((), (), s32[]{:S(2)}) async-start(), calls=%async_computation.4 | async-start | bytes 2621440 | tf_op jit(solution)/shard_map/reduce_scatter | solution.py:103
  14.2 1.9 %copy-start = (bf16[128,8192]{1,0:T(8,128)(2,1)S(1)}, bf16[128,8192]{1,0:T(8,128)(2,1)}, u32[]{:S(2)}) copy-start(bf16[128,8192]{1,0:T(8,128)(2,1)} %param.12) | copy-start | bytes 6291460
  16.1 1.9 %copy-start.4 = (f32[128,64]{0,1:T(8,128)S(1)}, f32[128,64]{0,1:T(8,128)}, u32[]{:S(2)}) copy-start(f32[128,64]{0,1:T(8,128)} %param.14) | copy-start | bytes 98308
  16.1 2.4 %copy-start.3 = (f32[128,64]{0,1:T(8,128)S(1)}, f32[128,64]{0,1:T(8,128)}, u32[]{:S(2)}) copy-start(f32[128,64]{0,1:T(8,128)} %param.15) | copy-start | bytes 98308
  105.0 1.2 copy-start.2
  106.2 29.9 %copy-start.1 = (bf16[8,1024,128]{2,1,0:T(8,128)(2,1)S(1)}, bf16[8,1024,128]{2,1,0:T(8,128)(2,1)}, u32[]{:S(2)}) copy-start(bf16[8,1024,128]{2,1,0:T(8,128)(2,1)} %get-tuple-element.57) | copy-start | bytes 6291460
  107.3 68.5 %all-to-all-start = ((bf16[64,4,2048]{2,0,1:T(8,128)(2,1)}), bf16[64,4,2048]{2,0,1:T(8,128)(2,1)S(1)}, u32[]{:S(2)}, u32[]{:S(2)}) async-start(bf16[64,4,2048]{2,0,1:T(8,128)(2,1)} %bitcast.93), calls=%async_computation.2 | async-start | bytes 2097152 | tf_op jit(solution)/shard_map/all_to_all | solution.py:107
  110.9 49.9 %reduce-scatter.5.cloned.1.call-start = ((), (), s32[]{:S(2)}) async-start(), calls=%async_computation.5 | async-start | bytes 655360 | tf_op jit(solution)/shard_map/reduce_scatter | solution.py:104
Sparse Core Ops, SparseCore 0:
  9.6 30.6 all-gather.1
  105.1 30.8 reduce-scatter.2
  139.0 21.6 reduce-scatter.4
where the time goes:
time: 192 us; the launch traced here: 190 us
  waiting for transfers between devices  62.6 us (33%)
  matrix products  60.6 us (32%)
  local copies, waits for them, and re-layouts  26.4 us (14%)
  blocking collectives  14.1 us (7%)
  between operations  13.8 us (7%)
  other arithmetic  8.91 us (5%)
  starting transfers between devices  3.71 us (2%)
    reduce_scatter x1, waiting for transfers between devices, on_device(): by_heads = lax.psum_scatter(grads, 'roll', scatter_dimension=2, tiled=True)  25.2 us
    reduce_scatter x1, waiting for transfers between devices, on_device(): owned = lax.psum_scatter(by_heads, 'ctx', scatter_dimension=1, tiled=True)  20.9 us
    all_gather x1, waiting for transfers between devices, on_device(): lax.all_gather(prompt_kv, 'ctx', axis=1, tiled=True)  16.5 us
    dot_general x8, matrix products, one_head(): dk = lax.dot_general(dscore, qg, outer, preferred_element_type=jnp.float32)  15.6 us
    unnamed x15, local copies, waits for them, and re-layouts  15.4 us
    dot_general x8, matrix products, one_head(): dq = jnp.dot(dscore, kg, preferred_element_type=jnp.float32)  14.8 us
    all_gather x1, blocking collectives, on_device(): lax.all_gather(owned_low, 'ctx', axis=1, tiled=True)  14.1 us
    dot_general x8, matrix products, one_head(): lax.dot_general(qg, kg, inner, preferred_element_type=jnp.float32) * scale  10.4 us
  transfers between devices with their start and end apart: 4, of which 3 were waited for; matrix products, arithmetic and copies ran while one was open for 11% of the time, Pallas kernels for 0%

commit v1 on v0

v1 whole, which is shorter than its diff:
```python
import functools
import math

import jax
import jax.numpy as jnp
from jax import lax
from jax.experimental import pallas as pl
from jax.experimental.pallas import tpu as pltpu
from jax.sharding import PartitionSpec as P

HD = 128
BLOCK = 32
MIB = 2**20
NT = (((1,), (1,)), ((), ()))
TN = (((0,), (0,)), ((), ()))
F32 = jnp.float32
BF16 = jnp.bfloat16


def xor_pairs(count, offset):
    return [(i, i ^ offset) for i in range(count)]


def prep_kernel(per_rollout, slab, ids, lengths, advantages, adv_index, ct_ref, od_ref, no_ref, go_ref, d_ref, o_ref):
    resp_max = per_rollout * BLOCK
    rows = []
    for b in range(ids.shape[0]):
        rollout = ids[b] // per_rollout
        slot = ids[b] % per_rollout
        length = lengths[rollout]
        scaled = jnp.full((BLOCK, HD), advantages[adv_index[rollout]] * resp_max, F32) / jnp.full(
            (BLOCK, HD), length.astype(F32), F32
        )
        position = slot * BLOCK + lax.broadcasted_iota(jnp.int32, (BLOCK, HD), 0)
        rows.append(jnp.where(position < length, scaled, jnp.float32(0.0)))
    weights = jnp.concatenate(rows, 0)
    heads = od_ref.shape[1]

    @pl.when(pl.program_id(0) == 0)
    def _():
        d_ref[...] = jnp.transpose(weights[:, :heads] * od_ref[...])
        o_ref[...] = jnp.transpose(no_ref[...] * math.log2(math.e) + math.log2(slab))

    for c in range(ct_ref.shape[1] // HD):
        cols = slice(c * HD, (c + 1) * HD)
        go_ref[:, cols] = (ct_ref[:, cols].astype(F32) * weights).astype(BF16)


def prep(per_rollout, slab, ids, lengths, advantages, adv_index, cotangent, out_dot, norm_offset):
    tokens, width = cotangent.shape
    heads = out_dot.shape[1]
    step = 2048
    small = pl.BlockSpec((tokens, heads), lambda i, *_: (0, 0))
    turned = pl.BlockSpec((heads, tokens), lambda i, *_: (0, 0))
    wide = pl.BlockSpec((tokens, step), lambda i, *_: (0, i))
    return pl.pallas_call(
        functools.partial(prep_kernel, per_rollout, slab),
        grid_spec=pltpu.PrefetchScalarGridSpec(
            num_scalar_prefetch=4,
            grid=(width // step,),
            in_specs=[wide, small, small],
            out_specs=[wide, turned, turned],
        ),
        out_shape=[
            jax.ShapeDtypeStruct((tokens, width), BF16),
            jax.ShapeDtypeStruct((heads, tokens), F32),
            jax.ShapeDtypeStruct((heads, tokens), F32),
        ],
        compiler_params=pltpu.CompilerParams(vmem_limit_bytes=8 * MIB),
        name="prep",
    )(ids, lengths, advantages, adv_index, cotangent, out_dot, norm_offset)


def heads_kernel(pieces, per_kv, aliased, block_ref, q_ref, go_ref, o_ref, d_ref, *refs):
    kv_refs = refs[:pieces]
    dq_ref, grads_ref = refs[pieces + aliased :]
    tokens = q_ref.shape[0]
    rows = kv_refs[0].shape[1]
    scale = 1.0 / math.sqrt(HD)
    keys = jnp.concatenate([r[0] for r in kv_refs], 0)
    values = jnp.concatenate([r[1] for r in kv_refs], 0)
    cols = [slice(h * HD, (h + 1) * HD) for h in range(per_kv)]
    q = jnp.concatenate([q_ref[:, c] for c in cols], 0)
    go = jnp.concatenate([go_ref[:, c] for c in cols], 0)
    offset = jnp.concatenate([o_ref[h : h + 1, :] for h in range(per_kv)], 1)
    delta = jnp.concatenate([d_ref[h : h + 1, :] for h in range(per_kv)], 1)
    scores = lax.dot_general(keys, q, NT, preferred_element_type=F32)
    prob = jnp.exp2(scores * (scale * math.log2(math.e)) - offset)
    dprob = lax.dot_general(values, go, NT, preferred_element_type=F32)
    dscore = ((prob * scale) * (dprob - delta)).astype(BF16)
    dq = lax.dot_general(dscore, keys, TN, preferred_element_type=F32).astype(BF16)
    for h in range(per_kv):
        dq_ref[:, cols[h]] = dq[h * tokens : (h + 1) * tokens]
    dk = jnp.dot(dscore, q, preferred_element_type=F32)
    dv = jnp.dot(prob.astype(BF16), go, preferred_element_type=F32)
    for c in range(pieces):
        span = slice(c * rows, (c + 1) * rows)
        grads_ref[c, 0] = dk[span].astype(grads_ref.dtype)
        grads_ref[c, 1] = dv[span].astype(grads_ref.dtype)


def head_block(block, kv_width, queries, grad_out, offset, delta, kv, dq, out_type):
    tokens, width = queries.shape
    _, rows, cols = kv[0].shape
    pieces = len(kv)
    count = cols // HD
    per_kv = queries.shape[1] // kv_width
    wide = pl.BlockSpec((tokens, per_kv * HD), lambda g, b: (0, b[0] * count + g))
    small = pl.BlockSpec((per_kv, tokens), lambda g, b: (b[0] * count + g, 0))
    piece = pl.BlockSpec((2, rows, HD), lambda g, b: (0, 0, g))
    aliased = int(dq is not None)
    slab = rows * pieces
    products = 5 * tokens * per_kv * slab * HD * count
    return pl.pallas_call(
        functools.partial(heads_kernel, pieces, per_kv, aliased),
        grid_spec=pltpu.PrefetchScalarGridSpec(
            num_scalar_prefetch=1,
            grid=(count,),
            in_specs=[wide, wide, small, small]
            + [piece] * pieces
            + [pl.BlockSpec(memory_space=pl.ANY)] * aliased,
            out_specs=[wide, pl.BlockSpec((pieces, 2, rows, HD), lambda g, b: (0, 0, 0, g))],
        ),
        out_shape=[
            jax.ShapeDtypeStruct((tokens, width), BF16),
            jax.ShapeDtypeStruct((pieces, 2, rows, cols), out_type),
        ],
        input_output_aliases={5 + pieces: 0} if aliased else {},
        compiler_params=pltpu.CompilerParams(vmem_limit_bytes=12 * MIB + slab * 32 * 1024),
        cost_estimate=pl.CostEstimate(
            flops=2 * products,
            bytes_accessed=tokens * per_kv * HD * count * 6,
            transcendentals=tokens * per_kv * slab * count,
        ),
        name="head_block",
    )(block, queries, grad_out, offset, delta, *kv, *([dq] if aliased else []))


def turn_kernel(pieces, *refs):
    x = jnp.concatenate([r[...] for r in refs[:pieces]], 0)
    refs[pieces][...] = jnp.transpose(x)


def turn(x):
    rows, cols = x[0].shape
    step = min(cols, 512)
    return pl.pallas_call(
        functools.partial(turn_kernel, len(x)),
        grid=(cols // step,),
        in_specs=[pl.BlockSpec((rows, step), lambda i: (0, i))] * len(x),
        out_specs=pl.BlockSpec((step, rows * len(x)), lambda i: (i, 0)),
        out_shape=jax.ShapeDtypeStruct((cols, rows * len(x)), BF16),
        compiler_params=pltpu.CompilerParams(vmem_limit_bytes=12 * MIB),
        name="turn_hidden",
    )(*x)


def weight_kernel(pieces, steps, core_ref, mine_ref, other_ref, *refs):
    low = refs[:pieces]
    out_ref = refs[pieces]
    keys = jnp.concatenate([r[0] for r in low], 0)
    values = jnp.concatenate([r[1] for r in low], 0)

    def write(x):
        out_ref[0] = jnp.dot(x, keys, preferred_element_type=F32)
        out_ref[1] = jnp.dot(x, values, preferred_element_type=F32)

    @pl.when(pl.program_id(0) < steps)
    def _():
        write(mine_ref[...])

    @pl.when(pl.program_id(0) >= steps)
    def _():
        write(other_ref[...])


def weight_grads(core, mine, other, low):
    half, slab = mine.shape
    _, rows, cols = low[0].shape
    step = min(half, 512)
    steps = half // step

    def place(i, core):
        return (0, (i // steps ^ core[0]) * steps + i % steps, 0)

    return pl.pallas_call(
        functools.partial(weight_kernel, len(low), steps),
        grid_spec=pltpu.PrefetchScalarGridSpec(
            num_scalar_prefetch=1,
            grid=(2 * steps,),
            in_specs=[
                pl.BlockSpec((step, slab), lambda i, core: (jnp.minimum(i, steps - 1), 0)),
                pl.BlockSpec((step, slab), lambda i, core: (jnp.maximum(i - steps, 0), 0)),
            ]
            + [pl.BlockSpec((2, rows, cols), lambda i, core: (0, 0, 0))] * len(low),
            out_specs=pl.BlockSpec((2, step, cols), place),
        ),
        out_shape=jax.ShapeDtypeStruct((2, 2 * half, cols), F32),
        compiler_params=pltpu.CompilerParams(vmem_limit_bytes=16 * MIB),
        name="weight_grads",
    )(core, mine, other, *low)


def on_device(
    queries,
    cotangent,
    out_dot,
    norm_offset,
    prompt_kv,
    prompt_x,
    block_ids,
    lengths,
    advantages,
    adv_index,
):
    ctx_count = lax.axis_size("ctx")
    roll_count = lax.axis_size("roll")
    ctx = lax.axis_index("ctx")
    roll = lax.axis_index("roll")
    core = roll % 2
    _, rows, kv_width = prompt_kv.shape
    cols = kv_width // roll_count
    slab = rows * ctx_count

    def to_ctx(x, offset):
        return lax.ppermute(x, "ctx", xor_pairs(ctx_count, offset))

    def to_roll(x, offset):
        return lax.ppermute(x, "roll", xor_pairs(roll_count, offset))

    last = roll_count - 1
    own = lax.dynamic_slice_in_dim(prompt_kv, (roll ^ last) * cols, cols, 2)
    fetched = [own] + [to_ctx(own, k) for k in range(1, ctx_count)]
    kv = {last: fetched}
    stacked = jnp.stack(fetched)
    blocks = {last: stacked}
    blocks[last - 1] = to_roll(stacked, 1)
    for d in range(1, roll_count // 2):
        blocks[last - 2 * d] = to_roll(stacked, 2 * d)
        blocks[last - 2 * d - 1] = to_roll(blocks[last - 2 * d], 1)
    for off in blocks:
        if off != last:
            kv[off] = [blocks[off][c] for c in range(ctx_count)]

    blocks_total = block_ids.shape[0] * ctx_count * roll_count
    grad_out, delta, offset = prep(
        blocks_total // lengths.shape[0], slab, block_ids, lengths, advantages, adv_index, cotangent, out_dot, norm_offset
    )

    width = prompt_x.shape[1] // ctx_count
    half = width // 2
    part = [
        lax.dynamic_slice_in_dim(prompt_x, (ctx ^ k) * width + core * half, half, 1)
        for k in range(ctx_count)
    ]
    x_mine = turn([part[0]] + [to_ctx(part[k], k) for k in range(1, ctx_count)])
    x_other = to_roll(x_mine, 1)

    dq = None
    arrived = []
    for d in reversed(range(roll_count // 2)):
        sums = {}
        for off, kind in ((2 * d + 1, BF16), (2 * d, F32)):
            dq, sums[off] = head_block(
                (roll ^ off)[None].astype(jnp.int32), kv_width, queries, grad_out, offset, delta, kv[off], dq, kind
            )
        total = sums[2 * d] + to_roll(sums[2 * d + 1], 1).astype(F32)
        if d:
            arrived.append(to_roll(total.astype(BF16), 2 * d))
    for part_sum in arrived:
        total = total + part_sum.astype(F32)
    owned = total[0]
    low_total = total.astype(BF16)
    for k in range(1, ctx_count):
        owned = owned + to_ctx(low_total[k], k).astype(F32)
    owned_low = owned.astype(BF16)
    low = [owned_low] + [to_ctx(owned_low, k) for k in range(1, ctx_count)]
    weight_grad = weight_grads(core[None].astype(jnp.int32), x_mine, x_other, low)
    return (dq, owned, weight_grad)


def solution(mesh):
    placed = (
        P(("groups", "ctx", "roll"), None),
        P(("groups", "ctx", "roll"), None),
        P(("groups", "ctx", "roll"), None),
        P(("groups", "ctx", "roll"), None),
        P(None, ("groups", "ctx"), None),
        P(("groups", "ctx"), None),
        P(("groups", "ctx", "roll")),
        P("groups"),
        P("groups"),
        P("groups"),
    )
    return jax.shard_map(
        on_device,
        mesh=mesh,
        in_specs=placed,
        out_specs=(
            P(("groups", "ctx", "roll"), None),
            P(None, ("groups", "ctx"), "roll"),
            P(None, ("groups", "ctx"), "roll"),
        ),
        check_vma=False,
    )
```

time: 192 us -> 64.8 us (0.34)
  matrix products: 60.6 us -> 0 us
  waiting for transfers between devices: 62.6 us -> 17.4 us
  local copies, waits for them, and re-layouts: 26.4 us -> 7.08 us
  starting transfers between devices: 3.71 us -> 22.4 us
  Pallas kernels: 0 us -> 15.8 us
  blocking collectives: 14.1 us -> 0 us
  between operations: 13.8 us -> 0.89 us
  other arithmetic: 8.91 us -> 0.88 us
    dot_general x41 -> x0, matrix products: 60.6 us -> none  [the longest x8 15.6 us: one_head(): dk = lax.dot_general(dscore, qg, outer, preferred_element_type=jnp.float32)]
    reduce_scatter x2 -> x0, waiting for transfers between devices: 46.1 us -> none  [the longest x1 25.2 us: on_device(): by_heads = lax.psum_scatter(grads, 'roll', scatter_dimension=2, tiled=True)]
    ppermute x0 -> x19, starting transfers between devices: none -> 22.4 us  [the longest x12 19.2 us: to_ctx(): return lax.ppermute(x, 'ctx', xor_pairs(ctx_count, offset))]
    ppermute x0 -> x19, waiting for transfers between devices: none -> 17.4 us  [the longest x12 15.6 us: to_ctx(): return lax.ppermute(x, 'ctx', xor_pairs(ctx_count, offset))]
    all_gather x1 -> x0, waiting for transfers between devices: 16.5 us -> none  [on_device(): lax.all_gather(prompt_kv, 'ctx', axis=1, tiled=True)]
    pallas_call x0 -> x7, Pallas kernels: none -> 15.8 us  [the longest x4 10.8 us: head_block(): pl.pallas_call(functools.partial(heads_kernel, pieces, per_kv, aliased),...]
    all_gather x1 -> x0, blocking collectives: 14.1 us -> none  [on_device(): lax.all_gather(owned_low, 'ctx', axis=1, tiled=True)]
    unnamed x15 -> x16, local copies, waits for them, and re-layouts: 15.4 us -> 4.21 us
  transfers between devices with their start and end apart: 4 -> 19, of which waited for: 3 -> 8; matrix products, arithmetic and copies ran while one was open for 11% -> 8% of each run, Pallas kernels for 0% -> 20%
where the time goes in v1:
time: 64.8 us; the launch traced here: 64.4 us
  starting transfers between devices  22.4 us (35%)
  waiting for transfers between devices  17.4 us (27%)
  Pallas kernels  15.8 us (24%)
  local copies, waits for them, and re-layouts  7.08 us (11%)
  between operations  0.89 us (1%)
  other arithmetic  0.88 us (1%)
    ppermute x12, starting transfers between devices, to_ctx(): return lax.ppermute(x, 'ctx', xor_pairs(ctx_count, offset))  19.2 us
    ppermute x12, waiting for transfers between devices, to_ctx(): return lax.ppermute(x, 'ctx', xor_pairs(ctx_count, offset))  15.6 us
    pallas_call x4, Pallas kernels, head_block(): pl.pallas_call(functools.partial(heads_kernel, pieces, per_kv, aliased),...  10.8 us
    unnamed x16, local copies, waits for them, and re-layouts  4.21 us
    ppermute x7, starting transfers between devices, to_roll(): return lax.ppermute(x, 'roll', xor_pairs(roll_count, offset))  3.29 us
    pallas_call x1, Pallas kernels, weight_grads(): pl.pallas_call(functools.partial(weight_kernel, len(low), steps), grid_sp...  2.91 us
    dynamic_slice x1, local copies, waits for them, and re-layouts, on_device(): lax.dynamic_slice_in_dim(prompt_x, (ctx ^ k) * width + core * half, half, 1)  1.86 us
    ppermute x7, waiting for transfers between devices, to_roll(): return lax.ppermute(x, 'roll', xor_pairs(roll_count, offset))  1.72 us
  transfers between devices with their start and end apart: 19, of which 8 were waited for; matrix products, arithmetic and copies ran while one was open for 8% of the time, Pallas kernels for 20%

profile of v1, /device:TPU:0, one launch (start us, length us, event | category | flops | bytes accessed | tf_op | source)
XLA Modules:
  0.0 64.4 jit_solution(4334957959277988343)
XLA Ops:
  0.7 0.9 %copy-done = bf16[2,64,1024]{2,1,0:T(8,128)(2,1)S(1)} copy-done((bf16[2,64,1024]{2,1,0:T(8,128)(2,1)S(1)}, bf16[2,64,1024]{2,1,0:T(8,128)(2,1)}, u32[]{:S(2)}) %copy-start) | copy-done | bytes 262168
  1.6 3.1 %collective-permute-start = (bf16[2,64,256]{2,1,0:T(8,128)(2,1)S(1)}, bf16[2,64,256]{2,1,0:T(8,128)(2,1)S(1)}, u32[]{:S(2)}, u32[]{:S(2)}) collective-permute-start(bf16[2,64,256]{2,1,0:T(8,128)(2,1)S(1)} %constant_dynamic-slice_fusion.4.refs_0_), channel_id=1, source_target_pairs={{0,4},{4,0},{8,12},{12,8},{1,5},{5,1},{9,13},{13,9},{2,6},{6,2},{1... | collective-permute-start | bytes 196616 | tf_op jit(solution)/shard_map/ppermute | solution.py:226
  4.7 2.6 %collective-permute-start.1 = (bf16[2,64,256]{2,1,0:T(8,128)(2,1)S(1)}, bf16[2,64,256]{2,1,0:T(8,128)(2,1)S(1)}, u32[]{:S(2)}, u32[]{:S(2)}) collective-permute-start(bf16[2,64,256]{2,1,0:T(8,128)(2,1)S(1)} %constant_dynamic-slice_fusion.4.refs_0_), channel_id=1, source_target_pairs={{0,8},{4,12},{8,0},{12,4},{1,9},{5,13},{9,1},{13,5},{2,10},{6,14},... | collective-permute-start | bytes 196616 | tf_op jit(solution)/shard_map/ppermute | solution.py:226
  7.3 4.6 %collective-permute-done.1.refs_2_ = bf16[2,64,256]{2,1,0:T(8,128)(2,1)S(1)} collective-permute-done((bf16[2,64,256]{2,1,0:T(8,128)(2,1)S(1)}, bf16[2,64,256]{2,1,0:T(8,128)(2,1)S(1)}, u32[]{:S(2)}, u32[]{:S(2)}) %collective-permute-start.1) | collective-permute-done | bytes 65568 | tf_op jit(solution)/shard_map/ppermute | solution.py:226
  12.0 1.4 %collective-permute-done.2.refs_3_ = bf16[2,64,256]{2,1,0:T(8,128)(2,1)S(1)} collective-permute-done((bf16[2,64,256]{2,1,0:T(8,128)(2,1)S(1)}, bf16[2,64,256]{2,1,0:T(8,128)(2,1)S(1)}, u32[]{:S(2)}, u32[]{:S(2)}) %collective-permute-start.2) | collective-permute-done | bytes 65568 | tf_op jit(solution)/shard_map/ppermute | solution.py:226
  13.5 1.9 %constant_dynamic-slice_fusion = (bf16[64,1024]{1,0:T(8,128)(2,1)}, bf16[64,1024]{1,0:T(8,128)(2,1)}, bf16[64,1024]{1,0:T(8,128)(2,1)S(1)}, bf16[64,1024]{1,0:T(8,128)(2,1)}) fusion(bf16[64,8192]{1,0:T(8,128)(2,1)} %param.15, s32[]{:T(128)S(6)} %select_n.27, s32[]{:T(128)S(6)} %select_n.25, s32[]{:T(128)S(6)} %select_n.24, s32[]{:T(128)S(6)} %select_n.26), kind=kLoop, calls=%fused_computation.22 | loop fusion | bytes 1048592 | tf_op jit(solution)/shard_map/dynamic_slice | solution.py:253
  15.4 2.3 %collective-permute-start.13 = (bf16[64,1024]{1,0:T(8,128)(2,1)}, bf16[64,1024]{1,0:T(8,128)(2,1)S(1)}, u32[]{:S(2)}, u32[]{:S(2)}) collective-permute-start(bf16[64,1024]{1,0:T(8,128)(2,1)} %get-tuple-element.32), channel_id=1, source_target_pairs={{0,8},{4,12},{8,0},{12,4},{1,9},{5,13},{9,1},{13,5},{2,10},{6,14},... | collective-permute-start | bytes 393224 | tf_op jit(solution)/shard_map/ppermute | solution.py:226
  17.7 2.0 %collective-permute-start.14 = (bf16[64,1024]{1,0:T(8,128)(2,1)}, bf16[64,1024]{1,0:T(8,128)(2,1)S(1)}, u32[]{:S(2)}, u32[]{:S(2)}) collective-permute-start(bf16[64,1024]{1,0:T(8,128)(2,1)} %get-tuple-element.29), channel_id=1, source_target_pairs={{0,12},{4,8},{8,4},{12,0},{1,13},{5,9},{9,5},{13,1},{2,14},{6,10},... | collective-permute-start | bytes 393224 | tf_op jit(solution)/shard_map/ppermute | solution.py:226
  19.8 0.8 %copy.16.od_ref = f32[128,64]{1,0:T(8,128)S(1)} copy(f32[128,64]{0,1:T(8,128)} %param.12) | data formatting | bytes 65536 | tf_op args[2]
  20.6 0.9 %copy.17.no_ref = f32[128,64]{1,0:T(8,128)S(1)} copy(f32[128,64]{0,1:T(8,128)} %param.13) | data formatting | bytes 65536 | tf_op args[3]
  21.5 1.6 %copy-done.2 = bf16[128,8192]{1,0:T(8,128)(2,1)S(1)} copy-done((bf16[128,8192]{1,0:T(8,128)(2,1)S(1)}, bf16[128,8192]{1,0:T(8,128)(2,1)}, u32[]{:S(2)}) %copy-start.2) | copy-done | bytes 2097176
  23.1 1.7 %prep.1 = (bf16[128,8192]{1,0:T(8,128)(2,1)S(1)}, f32[64,128]{1,0:T(8,128)S(1)}, f32[64,128]{1,0:T(8,128)S(1)}) custom-call(s32[4]{0:T(128)S(1)} %copy-done.3, s32[16]{0:T(128)S(1)} %copy-done.4, f32[16]{0:T(128)S(1)} %copy-done.5, s32[16]{0:T(128)S(1)} %copy-done.6, bf16[128,8192]{1,0:T(8,128)(2,1)S(1)} %copy-done.2, f32[128,64]{1,0:T(8,128)S(1)} %copy.16.od_ref, ...), custom_call_target="tpu_custom_call" | custom-call | tf_op jit(solution)/shard_map/prep/pallas_call | solution.py:56
  24.8 1.6 %collective-permute-start.3 = (bf16[4,2,64,256]{3,2,1,0:T(8,128)(2,1)S(1)}, bf16[4,2,64,256]{3,2,1,0:T(8,128)(2,1)S(1)}, u32[]{:S(2)}, u32[]{:S(2)}) collective-permute-start(bf16[4,2,64,256]{3,2,1,0:T(8,128)(2,1)S(1)} %pad_maximum_fusion), channel_id=1, source_target_pairs={{0,2},{1,3},{2,0},{3,1},{4,6},{5,7},{6,4},{7,5},{8,10},{9,11},{10,... | collective-permute-start | bytes 786440 | tf_op jit(solution)/shard_map/ppermute | solution.py:229
  26.4 2.7 %head_block.4 = (bf16[128,8192]{1,0:T(8,128)(2,1)}, bf16[4,2,64,256]{3,2,1,0:T(8,128)(2,1)S(1)}) custom-call(s32[1]{0:T(128)} %bitcast.19.block_ref, bf16[128,8192]{1,0:T(8,128)(2,1)S(1)} %copy-done.1, bf16[128,8192]{1,0:T(8,128)(2,1)S(1)} %get-tuple-element.14.go_ref, f32[64,128]{1,0:T(8,128)S(1)} %get-tuple-element.15.o_ref, ...), custom_call_target="tpu_custom_call" | custom-call | flops 671088640 | bytes 1572864 | tf_op jit(solution)/shard_map/head_block/pallas_call | solution.py:114
  29.4 0.6 collective-permute-start.15
  30.0 1.0 %slice_bitcast_fusion.4 = (bf16[2,64,256]{2,1,0:T(8,128)(2,1)S(1)}, bf16[2,64,256]{2,1,0:T(8,128)(2,1)S(1)}, bf16[2,64,256]{2,1,0:T(8,128)(2,1)S(1)}, bf16[2,64,256]{2,1,0:T(8,128)(2,1)S(1)}) fusion(bf16[4,2,64,256]{3,2,1,0:T(8,128)(2,1)} %collective-permute-done.5), kind=kLoop, calls=%fused_computation.10 | loop fusion | bytes 524288 | tf_op jit(solution)/shard_map/squeeze | solution.py:243
  31.0 2.7 %head_block.5 = (bf16[128,8192]{1,0:T(8,128)(2,1)}, f32[4,2,64,256]{3,2,1,0:T(8,128)S(1)}) custom-call(s32[1]{0:T(128)} %bitcast.14.block_ref, bf16[128,8192]{1,0:T(8,128)(2,1)S(1)} %copy-done.1, bf16[128,8192]{1,0:T(8,128)(2,1)S(1)} %get-tuple-element.14.go_ref, f32[64,128]{1,0:T(8,128)S(1)} %get-tuple-element.15.o_ref, ...), custom_call_target="tpu_custom_call", output_to_operand_aliasing={{0}: (9, {})} | custom-call | flops 671088640 | bytes 1572864 | tf_op jit(solution)/shard_map/head_block/pallas_call | solution.py:114
  33.7 0.6 collective-permute-start.8
  34.4 2.7 %head_block.6 = (bf16[128,8192]{1,0:T(8,128)(2,1)}, bf16[4,2,64,256]{3,2,1,0:T(8,128)(2,1)S(1)}) custom-call(s32[1]{0:T(128)} %bitcast.9.block_ref, bf16[128,8192]{1,0:T(8,128)(2,1)S(1)} %copy-done.1, bf16[128,8192]{1,0:T(8,128)(2,1)S(1)} %get-tuple-element.14.go_ref, f32[64,128]{1,0:T(8,128)S(1)} %get-tuple-element.15.o_ref, ...), custom_call_target="tpu_custom_call", output_to_operand_aliasing={{0}: (9, {})} | custom-call | flops 671088640 | bytes 1572864 | tf_op jit(solution)/shard_map/head_block/pallas_call | solution.py:114
  37.6 2.7 %head_block.7 = (bf16[128,8192]{1,0:T(8,128)(2,1)}, f32[4,2,64,256]{3,2,1,0:T(8,128)S(1)}) custom-call(s32[1]{0:T(128)} %bitcast.block_ref, bf16[128,8192]{1,0:T(8,128)(2,1)S(1)} %copy-done.1, bf16[128,8192]{1,0:T(8,128)(2,1)S(1)} %get-tuple-element.14.go_ref, f32[64,128]{1,0:T(8,128)S(1)} %get-tuple-element.15.o_ref, ...), custom_call_target="tpu_custom_call", output_to_operand_aliasing={{0}: (9, {})} | custom-call | flops 671088640 | bytes 1572864 | tf_op jit(solution)/shard_map/head_block/pallas_call | solution.py:114
  40.3 1.7 %collective-permute-done.8 = bf16[4,2,64,256]{3,2,1,0:T(8,128)(2,1)S(1)} collective-permute-done((bf16[4,2,64,256]{3,2,1,0:T(8,128)(2,1)S(1)}, bf16[4,2,64,256]{3,2,1,0:T(8,128)(2,1)S(1)}, u32[]{:S(2)}, u32[]{:S(2)}) %collective-permute-start.8) | collective-permute-done | bytes 262176 | tf_op jit(solution)/shard_map/ppermute | solution.py:229
  42.2 3.6 %collective-permute-start.10 = (bf16[2,64,256]{2,1,0:T(8,128)(2,1)S(1)}, bf16[2,64,256]{2,1,0:T(8,128)(2,1)S(1)}, u32[]{:S(2)}, u32[]{:S(2)}) collective-permute-start(bf16[2,64,256]{2,1,0:T(8,128)(2,1)S(1)} %get-tuple-element.35), channel_id=1, source_target_pairs={{0,8},{4,12},{8,0},{12,4},{1,9},{5,13},{9,1},{13,5},{2,10},{6,14},... | collective-permute-start | bytes 196616 | tf_op jit(solution)/shard_map/ppermute | solution.py:226
  45.8 1.1 %collective-permute-start.11 = (bf16[2,64,256]{2,1,0:T(8,128)(2,1)S(1)}, bf16[2,64,256]{2,1,0:T(8,128)(2,1)S(1)}, u32[]{:S(2)}, u32[]{:S(2)}) collective-permute-start(bf16[2,64,256]{2,1,0:T(8,128)(2,1)S(1)} %get-tuple-element.34), channel_id=1, source_target_pairs={{0,12},{4,8},{8,4},{12,0},{1,13},{5,9},{9,5},{13,1},{2,14},{6,10},... | collective-permute-start | bytes 196616 | tf_op jit(solution)/shard_map/ppermute | solution.py:226
  46.9 3.7 %collective-permute-done.10 = bf16[2,64,256]{2,1,0:T(8,128)(2,1)S(1)} collective-permute-done((bf16[2,64,256]{2,1,0:T(8,128)(2,1)S(1)}, bf16[2,64,256]{2,1,0:T(8,128)(2,1)S(1)}, u32[]{:S(2)}, u32[]{:S(2)}) %collective-permute-start.10) | collective-permute-done | bytes 65568 | tf_op jit(solution)/shard_map/ppermute | solution.py:226
  50.6 1.4 %collective-permute-done.11 = bf16[2,64,256]{2,1,0:T(8,128)(2,1)S(1)} collective-permute-done((bf16[2,64,256]{2,1,0:T(8,128)(2,1)S(1)}, bf16[2,64,256]{2,1,0:T(8,128)(2,1)S(1)}, u32[]{:S(2)}, u32[]{:S(2)}) %collective-permute-start.11) | collective-permute-done | bytes 65568 | tf_op jit(solution)/shard_map/ppermute | solution.py:226
  52.0 0.7 %fusion.3 = (bf16[2,64,256]{2,1,0:T(8,128)(2,1)S(1)}, f32[2,64,256]{2,1,0:T(8,128)}) fusion(bf16[2,64,256]{2,1,0:T(8,128)(2,1)S(1)} %collective-permute-done.11, bf16[2,64,256]{2,1,0:T(8,128)(2,1)S(1)} %collective-permute-done.10, bf16[2,64,256]{2,1,0:T(8,128)(2,1)S(1)} %collective-permute-done.9, f32[4,2,64,256]{3,2,1,0:T(8,128)S(1)} %get-tuple-element.28), kind=kLoop, calls=%fused_computation.27 | loop fusion | flops 229376 | bytes 524288 | tf_op jit(solution)/shard_map/convert_element_type | solution.py:276
  52.7 0.6 collective-permute-start.16
  53.2 2.2 %collective-permute-start.17 = (bf16[2,64,256]{2,1,0:T(8,128)(2,1)S(1)}, bf16[2,64,256]{2,1,0:T(8,128)(2,1)S(1)}, u32[]{:S(2)}, u32[]{:S(2)}) collective-permute-start(bf16[2,64,256]{2,1,0:T(8,128)(2,1)S(1)} %get-tuple-element.25.refs_0_), channel_id=1, source_target_pairs={{0,8},{4,12},{8,0},{12,4},{1,9},{5,13},{9,1},{13,5},{2,10},{6,14},... | collective-permute-start | bytes 196616 | tf_op jit(solution)/shard_map/ppermute | solution.py:226
  55.5 1.6 %collective-permute-start.18 = (bf16[2,64,256]{2,1,0:T(8,128)(2,1)S(1)}, bf16[2,64,256]{2,1,0:T(8,128)(2,1)S(1)}, u32[]{:S(2)}, u32[]{:S(2)}) collective-permute-start(bf16[2,64,256]{2,1,0:T(8,128)(2,1)S(1)} %get-tuple-element.25.refs_0_), channel_id=1, source_target_pairs={{0,12},{4,8},{8,4},{12,0},{1,13},{5,9},{9,5},{13,1},{2,14},{6,10},... | collective-permute-start | bytes 196616 | tf_op jit(solution)/shard_map/ppermute | solution.py:226
  57.4 2.4 %collective-permute-done.17.refs_2_ = bf16[2,64,256]{2,1,0:T(8,128)(2,1)S(1)} collective-permute-done((bf16[2,64,256]{2,1,0:T(8,128)(2,1)S(1)}, bf16[2,64,256]{2,1,0:T(8,128)(2,1)S(1)}, u32[]{:S(2)}, u32[]{:S(2)}) %collective-permute-start.17) | collective-permute-done | bytes 65568 | tf_op jit(solution)/shard_map/ppermute | solution.py:226
  59.7 1.8 %collective-permute-done.18.refs_3_ = bf16[2,64,256]{2,1,0:T(8,128)(2,1)S(1)} collective-permute-done((bf16[2,64,256]{2,1,0:T(8,128)(2,1)S(1)}, bf16[2,64,256]{2,1,0:T(8,128)(2,1)S(1)}, u32[]{:S(2)}, u32[]{:S(2)}) %collective-permute-start.18) | collective-permute-done | bytes 65568 | tf_op jit(solution)/shard_map/ppermute | solution.py:226
  61.5 2.9 %weight_grads.1 = f32[2,2048,256]{2,1,0:T(8,128)} custom-call(s32[1]{0:T(128)} %bitcast.24.core_ref, bf16[1024,256]{1,0:T(8,128)(2,1)S(1)} %turn_hidden.1.mine_ref, bf16[1024,256]{1,0:T(8,128)(2,1)S(1)} %collective-permute-done.15.other_ref, bf16[2,64,256]{2,1,0:T(8,128)(2,1)S(1)} %get-tuple-element.25.refs_0_, ...), custom_call_target="tpu_custom_call" | custom-call | tf_op jit(solution)/shard_map/weight_grads/pallas_call | solution.py:186
  (40 shorter events, 1.6 us)
Async XLA Ops:
  0.6 1.0 %copy-start = (bf16[2,64,1024]{2,1,0:T(8,128)(2,1)S(1)}, bf16[2,64,1024]{2,1,0:T(8,128)(2,1)}, u32[]{:S(2)}) copy-start(bf16[2,64,1024]{2,1,0:T(8,128)(2,1)} %param.14) | copy-start | bytes 786436
  0.6 20.8 %copy-start.3 = (s32[4]{0:T(128)S(1)}, s32[4]{0:T(128)}, u32[]{:S(2)}) copy-start(s32[4]{0:T(128)} %ids.1) | copy-start | bytes 52
  0.7 20.8 %copy-start.4 = (s32[16]{0:T(128)S(1)}, s32[16]{0:T(128)}, u32[]{:S(2)}) copy-start(s32[16]{0:T(128)} %lengths.1) | copy-start | bytes 196
  0.7 20.8 %copy-start.5 = (f32[16]{0:T(128)S(1)}, f32[16]{0:T(128)}, u32[]{:S(2)}) copy-start(f32[16]{0:T(128)} %advantages.1) | copy-start | bytes 196
  0.7 20.8 %copy-start.6 = (s32[16]{0:T(128)S(1)}, s32[16]{0:T(128)}, u32[]{:S(2)}) copy-start(s32[16]{0:T(128)} %adv_index.1) | copy-start | bytes 196
  1.6 24.8 %copy-start.1 = (bf16[128,8192]{1,0:T(8,128)(2,1)S(1)}, bf16[128,8192]{1,0:T(8,128)(2,1)}, u32[]{:S(2)}) copy-start(bf16[128,8192]{1,0:T(8,128)(2,1)} %q_ref.7) | copy-start | bytes 6291460
  1.6 5.7 %collective-permute-start = (bf16[2,64,256]{2,1,0:T(8,128)(2,1)S(1)}, bf16[2,64,256]{2,1,0:T(8,128)(2,1)S(1)}, u32[]{:S(2)}, u32[]{:S(2)}) collective-permute-start(bf16[2,64,256]{2,1,0:T(8,128)(2,1)S(1)} %constant_dynamic-slice_fusion.4.refs_0_), channel_id=1, source_target_pairs={{0,4},{4,0},{8,12},{12,8},{1,5},{5,1},{9,13},{13,9},{2,6},{6,2},{1... | collective-permute-start | bytes 196616 | tf_op jit(solution)/shard_map/ppermute | solution.py:226
  4.7 7.3 %collective-permute-start.1 = (bf16[2,64,256]{2,1,0:T(8,128)(2,1)S(1)}, bf16[2,64,256]{2,1,0:T(8,128)(2,1)S(1)}, u32[]{:S(2)}, u32[]{:S(2)}) collective-permute-start(bf16[2,64,256]{2,1,0:T(8,128)(2,1)S(1)} %constant_dynamic-slice_fusion.4.refs_0_), channel_id=1, source_target_pairs={{0,8},{4,12},{8,0},{12,4},{1,9},{5,13},{9,1},{13,5},{2,10},{6,14},... | collective-permute-start | bytes 196616 | tf_op jit(solution)/shard_map/ppermute | solution.py:226
  7.3 6.1 %collective-permute-start.2 = (bf16[2,64,256]{2,1,0:T(8,128)(2,1)S(1)}, bf16[2,64,256]{2,1,0:T(8,128)(2,1)S(1)}, u32[]{:S(2)}, u32[]{:S(2)}) collective-permute-start(bf16[2,64,256]{2,1,0:T(8,128)(2,1)S(1)} %constant_dynamic-slice_fusion.4.refs_0_), channel_id=1, source_target_pairs={{0,12},{4,8},{8,4},{12,0},{1,13},{5,9},{9,5},{13,1},{2,14},{6,10},... | collective-permute-start | bytes 196616 | tf_op jit(solution)/shard_map/ppermute | solution.py:226
  13.4 16.6 %collective-permute-start.5 = (bf16[4,2,64,256]{3,2,1,0:T(8,128)(2,1)S(1)}, bf16[4,2,64,256]{3,2,1,0:T(8,128)(2,1)}, u32[]{:S(2)}, u32[]{:S(2)}) collective-permute-start(bf16[4,2,64,256]{3,2,1,0:T(8,128)(2,1)S(1)} %pad_maximum_fusion), channel_id=1, source_target_pairs={{0,1},{1,0},{2,3},{3,2},{4,5},{5,4},{6,7},{7,6},{8,9},{9,8},{10,11... | collective-permute-start | bytes 786440 | tf_op jit(solution)/shard_map/ppermute | solution.py:229
  15.4 13.7 %collective-permute-start.12 = (bf16[64,1024]{1,0:T(8,128)(2,1)}, bf16[64,1024]{1,0:T(8,128)(2,1)S(1)}, u32[]{:S(2)}, u32[]{:S(2)}) collective-permute-start(bf16[64,1024]{1,0:T(8,128)(2,1)} %get-tuple-element.30), channel_id=1, source_target_pairs={{0,4},{4,0},{8,12},{12,8},{1,5},{5,1},{9,13},{13,9},{2,6},{6,2},{1... | collective-permute-start | bytes 393224 | tf_op jit(solution)/shard_map/ppermute | solution.py:226
  15.4 13.7 %collective-permute-start.13 = (bf16[64,1024]{1,0:T(8,128)(2,1)}, bf16[64,1024]{1,0:T(8,128)(2,1)S(1)}, u32[]{:S(2)}, u32[]{:S(2)}) collective-permute-start(bf16[64,1024]{1,0:T(8,128)(2,1)} %get-tuple-element.32), channel_id=1, source_target_pairs={{0,8},{4,12},{8,0},{12,4},{1,9},{5,13},{9,1},{13,5},{2,10},{6,14},... | collective-permute-start | bytes 393224 | tf_op jit(solution)/shard_map/ppermute | solution.py:226
  17.7 11.4 %collective-permute-start.14 = (bf16[64,1024]{1,0:T(8,128)(2,1)}, bf16[64,1024]{1,0:T(8,128)(2,1)S(1)}, u32[]{:S(2)}, u32[]{:S(2)}) collective-permute-start(bf16[64,1024]{1,0:T(8,128)(2,1)} %get-tuple-element.29), channel_id=1, source_target_pairs={{0,12},{4,8},{8,4},{12,0},{1,13},{5,9},{9,5},{13,1},{2,14},{6,10},... | collective-permute-start | bytes 393224 | tf_op jit(solution)/shard_map/ppermute | solution.py:226
  21.5 1.6 %copy-start.2 = (bf16[128,8192]{1,0:T(8,128)(2,1)S(1)}, bf16[128,8192]{1,0:T(8,128)(2,1)}, u32[]{:S(2)}) copy-start(bf16[128,8192]{1,0:T(8,128)(2,1)} %ct_ref.1) | copy-start | bytes 6291460
  24.8 9.5 %collective-permute-start.3 = (bf16[4,2,64,256]{3,2,1,0:T(8,128)(2,1)S(1)}, bf16[4,2,64,256]{3,2,1,0:T(8,128)(2,1)S(1)}, u32[]{:S(2)}, u32[]{:S(2)}) collective-permute-start(bf16[4,2,64,256]{3,2,1,0:T(8,128)(2,1)S(1)} %pad_maximum_fusion), channel_id=1, source_target_pairs={{0,2},{1,3},{2,0},{3,1},{4,6},{5,7},{6,4},{7,5},{8,10},{9,11},{10,... | collective-permute-start | bytes 786440 | tf_op jit(solution)/shard_map/ppermute | solution.py:229
  29.1 4.6 %collective-permute-start.7 = (bf16[4,2,64,256]{3,2,1,0:T(8,128)(2,1)S(1)}, bf16[4,2,64,256]{3,2,1,0:T(8,128)(2,1)S(1)}, u32[]{:S(2)}, u32[]{:S(2)}) collective-permute-start(bf16[4,2,64,256]{3,2,1,0:T(8,128)(2,1)S(1)} %get-tuple-element.24), channel_id=1, source_target_pairs={{0,1},{1,0},{2,3},{3,2},{4,5},{5,4},{6,7},{7,6},{8,9},{9,8},{10,11... | collective-permute-start | bytes 786440 | tf_op jit(solution)/shard_map/ppermute | solution.py:229
  29.4 27.6 %collective-permute-start.15 = (bf16[1024,256]{1,0:T(8,128)(2,1)S(1)}, bf16[1024,256]{1,0:T(8,128)(2,1)S(1)}, u32[]{:S(2)}, u32[]{:S(2)}) collective-permute-start(bf16[1024,256]{1,0:T(8,128)(2,1)S(1)} %turn_hidden.1.mine_ref), channel_id=1, source_target_pairs={{0,1},{1,0},{2,3},{3,2},{4,5},{5,4},{6,7},{7,6},{8,9},{9,8},{10,11... | collective-permute-start | bytes 1572872 | tf_op jit(solution)/shard_map/ppermute | solution.py:229
  33.7 8.3 %collective-permute-start.8 = (bf16[4,2,64,256]{3,2,1,0:T(8,128)(2,1)S(1)}, bf16[4,2,64,256]{3,2,1,0:T(8,128)(2,1)S(1)}, u32[]{:S(2)}, u32[]{:S(2)}) collective-permute-start(bf16[4,2,64,256]{3,2,1,0:T(8,128)(2,1)S(1)} %add_convert_fusion), channel_id=1, source_target_pairs={{0,2},{1,3},{2,0},{3,1},{4,6},{5,7},{6,4},{7,5},{8,10},{9,11},{10,... | collective-permute-start | bytes 786440 | tf_op jit(solution)/shard_map/ppermute | solution.py:229
  34.3 3.2 %collective-permute-start.4 = (bf16[4,2,64,256]{3,2,1,0:T(8,128)(2,1)S(1)}, bf16[4,2,64,256]{3,2,1,0:T(8,128)(2,1)S(1)}, u32[]{:S(2)}, u32[]{:S(2)}) collective-permute-start(bf16[4,2,64,256]{3,2,1,0:T(8,128)(2,1)S(1)} %collective-permute-done.3), channel_id=1, source_target_pairs={{0,1},{1,0},{2,3},{3,2},{4,5},{5,4},{6,7},{7,6},{8,9},{9,8},{10,11... | collective-permute-start | bytes 786440 | tf_op jit(solution)/shard_map/ppermute | solution.py:229
  37.1 4.9 %collective-permute-start.6 = (bf16[4,2,64,256]{3,2,1,0:T(8,128)(2,1)S(1)}, bf16[4,2,64,256]{3,2,1,0:T(8,128)(2,1)S(1)}, u32[]{:S(2)}, u32[]{:S(2)}) collective-permute-start(bf16[4,2,64,256]{3,2,1,0:T(8,128)(2,1)S(1)} %get-tuple-element.22), channel_id=1, source_target_pairs={{0,1},{1,0},{2,3},{3,2},{4,5},{5,4},{6,7},{7,6},{8,9},{9,8},{10,11... | collective-permute-start | bytes 786440 | tf_op jit(solution)/shard_map/ppermute | solution.py:229
  42.2 8.4 %collective-permute-start.10 = (bf16[2,64,256]{2,1,0:T(8,128)(2,1)S(1)}, bf16[2,64,256]{2,1,0:T(8,128)(2,1)S(1)}, u32[]{:S(2)}, u32[]{:S(2)}) collective-permute-start(bf16[2,64,256]{2,1,0:T(8,128)(2,1)S(1)} %get-tuple-element.35), channel_id=1, source_target_pairs={{0,8},{4,12},{8,0},{12,4},{1,9},{5,13},{9,1},{13,5},{2,10},{6,14},... | collective-permute-start | bytes 196616 | tf_op jit(solution)/shard_map/ppermute | solution.py:226
  45.8 6.2 %collective-permute-start.11 = (bf16[2,64,256]{2,1,0:T(8,128)(2,1)S(1)}, bf16[2,64,256]{2,1,0:T(8,128)(2,1)S(1)}, u32[]{:S(2)}, u32[]{:S(2)}) collective-permute-start(bf16[2,64,256]{2,1,0:T(8,128)(2,1)S(1)} %get-tuple-element.34), channel_id=1, source_target_pairs={{0,12},{4,8},{8,4},{12,0},{1,13},{5,9},{9,5},{13,1},{2,14},{6,10},... | collective-permute-start | bytes 196616 | tf_op jit(solution)/shard_map/ppermute | solution.py:226
  46.9 5.1 %collective-permute-start.9 = (bf16[2,64,256]{2,1,0:T(8,128)(2,1)S(1)}, bf16[2,64,256]{2,1,0:T(8,128)(2,1)S(1)}, u32[]{:S(2)}, u32[]{:S(2)}) collective-permute-start(bf16[2,64,256]{2,1,0:T(8,128)(2,1)S(1)} %get-tuple-element.33), channel_id=1, source_target_pairs={{0,4},{4,0},{8,12},{12,8},{1,5},{5,1},{9,13},{13,9},{2,6},{6,2},{1... | collective-permute-start | bytes 196616 | tf_op jit(solution)/shard_map/ppermute | solution.py:226
  52.7 4.7 %collective-permute-start.16 = (bf16[2,64,256]{2,1,0:T(8,128)(2,1)S(1)}, bf16[2,64,256]{2,1,0:T(8,128)(2,1)S(1)}, u32[]{:S(2)}, u32[]{:S(2)}) collective-permute-start(bf16[2,64,256]{2,1,0:T(8,128)(2,1)S(1)} %get-tuple-element.25.refs_0_), channel_id=1, source_target_pairs={{0,4},{4,0},{8,12},{12,8},{1,5},{5,1},{9,13},{13,9},{2,6},{6,2},{1... | collective-permute-start | bytes 196616 | tf_op jit(solution)/shard_map/ppermute | solution.py:226
  53.2 6.5 %collective-permute-start.17 = (bf16[2,64,256]{2,1,0:T(8,128)(2,1)S(1)}, bf16[2,64,256]{2,1,0:T(8,128)(2,1)S(1)}, u32[]{:S(2)}, u32[]{:S(2)}) collective-permute-start(bf16[2,64,256]{2,1,0:T(8,128)(2,1)S(1)} %get-tuple-element.25.refs_0_), channel_id=1, source_target_pairs={{0,8},{4,12},{8,0},{12,4},{1,9},{5,13},{9,1},{13,5},{2,10},{6,14},... | collective-permute-start | bytes 196616 | tf_op jit(solution)/shard_map/ppermute | solution.py:226
  55.5 6.1 %collective-permute-start.18 = (bf16[2,64,256]{2,1,0:T(8,128)(2,1)S(1)}, bf16[2,64,256]{2,1,0:T(8,128)(2,1)S(1)}, u32[]{:S(2)}, u32[]{:S(2)}) collective-permute-start(bf16[2,64,256]{2,1,0:T(8,128)(2,1)S(1)} %get-tuple-element.25.refs_0_), channel_id=1, source_target_pairs={{0,12},{4,8},{8,4},{12,0},{1,13},{5,9},{9,5},{13,1},{2,14},{6,10},... | collective-permute-start | bytes 196616 | tf_op jit(solution)/shard_map/ppermute | solution.py:226

commit v2 on v0

v2 whole, which is shorter than its diff:
```python
import functools
import math

import jax
import jax.numpy as jnp
from jax import lax
from jax.experimental import pallas as pl
from jax.experimental.pallas import tpu as pltpu
from jax.sharding import PartitionSpec as P

HD = 128
BLOCK = 32
MIB = 2**20
NT = (((1,), (1,)), ((), ()))
TN = (((0,), (0,)), ((), ()))
F32 = jnp.float32
BF16 = jnp.bfloat16
WHOLE = pl.BlockSpec(memory_space=pltpu.VMEM)


def xor_pairs(count, offset):
    return [(i, i ^ offset) for i in range(count)]


def prep_kernel(per_rollout, slab, ids, lengths, advantages, adv_index, od_ref, no_ref, w_ref, d_ref, o_ref):
    resp_max = per_rollout * BLOCK
    rows = []
    for b in range(ids.shape[0]):
        rollout = ids[b] // per_rollout
        slot = ids[b] % per_rollout
        length = lengths[rollout]
        scaled = jnp.full((BLOCK, HD), advantages[adv_index[rollout]] * resp_max, F32) / jnp.full(
            (BLOCK, HD), length.astype(F32), F32
        )
        position = slot * BLOCK + lax.broadcasted_iota(jnp.int32, (BLOCK, HD), 0)
        rows.append(jnp.where(position < length, scaled, jnp.float32(0.0)))
    weights = jnp.concatenate(rows, 0)
    w_ref[...] = weights
    d_ref[...] = jnp.transpose(weights)[: od_ref.shape[0]] * od_ref[...]
    o_ref[...] = no_ref[...] * math.log2(math.e) + math.log2(slab)


def prep(per_rollout, slab, ids, lengths, advantages, adv_index, out_dot, norm_offset):
    heads, tokens = out_dot.shape
    scalars = pl.BlockSpec(memory_space=pltpu.SMEM)
    return pl.pallas_call(
        functools.partial(prep_kernel, per_rollout, slab),
        in_specs=[scalars] * 4 + [WHOLE] * 2,
        out_specs=[WHOLE] * 3,
        out_shape=[
            jax.ShapeDtypeStruct((tokens, HD), F32),
            jax.ShapeDtypeStruct((heads, tokens), F32),
            jax.ShapeDtypeStruct((heads, tokens), F32),
        ],
        compiler_params=pltpu.CompilerParams(vmem_limit_bytes=4 * MIB),
        cost_estimate=pl.CostEstimate(flops=2**30, bytes_accessed=0, transcendentals=0),
        name="prep",
    )(ids, lengths, advantages, adv_index, out_dot, norm_offset)


def heads_kernel(per_kv, off, q_ref, ct_ref, w_ref, o_ref, d_ref, kv_ref, dq_ref, grads_ref):
    tokens = q_ref.shape[0]
    pieces, _, rows, cols = kv_ref.shape
    count = cols // HD
    span = per_kv * HD
    scale = 1.0 / math.sqrt(HD)
    weights = w_ref[...]
    for g in range(count):
        head = (lax.axis_index("roll") ^ off) * count + g
        here = slice(g * HD, (g + 1) * HD)
        keys = jnp.concatenate([kv_ref[c, 0, :, here] for c in range(pieces)], 0)
        values = jnp.concatenate([kv_ref[c, 1, :, here] for c in range(pieces)], 0)
        places = [pl.ds(pl.multiple_of((head * per_kv + h) * HD, HD), HD) for h in range(per_kv)]
        q = jnp.concatenate([q_ref[:, c] for c in places], 0)
        go = jnp.concatenate([(ct_ref[:, c].astype(F32) * weights).astype(BF16) for c in places], 0)
        lines = pl.ds(pl.multiple_of(head * per_kv, per_kv), per_kv)
        offset = jnp.concatenate([o_ref[lines, :][h : h + 1] for h in range(per_kv)], 1)
        delta = jnp.concatenate([d_ref[lines, :][h : h + 1] for h in range(per_kv)], 1)
        scores = lax.dot_general(keys, q, NT, preferred_element_type=F32)
        prob = jnp.exp2(scores * (scale * math.log2(math.e)) - offset)
        dprob = lax.dot_general(values, go, NT, preferred_element_type=F32)
        dscore = ((prob * scale) * (dprob - delta)).astype(BF16)
        dq = lax.dot_general(dscore, keys, TN, preferred_element_type=F32).astype(BF16)
        for h in range(per_kv):
            dq_ref[:, g * span + h * HD : g * span + (h + 1) * HD] = dq[h * tokens : (h + 1) * tokens]
        dk = jnp.dot(dscore, q, preferred_element_type=F32)
        dv = jnp.dot(prob.astype(BF16), go, preferred_element_type=F32)
        for c in range(pieces):
            part = slice(c * rows, (c + 1) * rows)
            grads_ref[c, 0, :, here] = dk[part].astype(grads_ref.dtype)
            grads_ref[c, 1, :, here] = dv[part].astype(grads_ref.dtype)


def head_block(off, kv_width, queries, cotangent, weights, offset, delta, kv, out_type):
    tokens, width = queries.shape
    pieces, _, rows, cols = kv.shape
    per_kv = width // kv_width
    slab = rows * pieces
    return pl.pallas_call(
        functools.partial(heads_kernel, per_kv, off),
        in_specs=[WHOLE] * 6,
        out_specs=[WHOLE, WHOLE],
        out_shape=[
            jax.ShapeDtypeStruct((tokens, per_kv * cols), BF16),
            jax.ShapeDtypeStruct((pieces, 2, rows, cols), out_type),
        ],
        compiler_params=pltpu.CompilerParams(vmem_limit_bytes=16 * MIB + slab * 32 * 1024),
        cost_estimate=pl.CostEstimate(
            flops=30 * tokens * per_kv * slab * cols, bytes_accessed=0, transcendentals=0
        ),
        name="head_block",
    )(queries, cotangent, weights, offset, delta, kv)


def finish(order, parts, own, received):
    tokens, span = parts[0].shape
    count = len(parts)

    def kernel(*refs):
        own_ref = refs[count]
        received_refs = refs[count + 1 : -4]
        out_ref, owned_ref, total_ref, sems = refs[-4:]
        roll = lax.axis_index("roll")
        copies = [
            pltpu.make_async_copy(
                refs[i],
                out_ref.at[:, pl.ds(pl.multiple_of((roll ^ order[i]) * span, span), span)],
                sems.at[i],
            )
            for i in range(count)
        ]
        for copy in copies:
            copy.start()
        total = own_ref[...]
        for ref in received_refs:
            total = total + ref[...].astype(F32)
        total_ref[...] = total
        copies.append(pltpu.make_async_copy(total_ref, owned_ref, sems.at[count]))
        copies[-1].start()
        for copy in copies:
            copy.wait()

    anywhere = pl.BlockSpec(memory_space=pl.ANY)
    return pl.pallas_call(
        kernel,
        in_specs=[anywhere] * count + [WHOLE] * (1 + len(received)),
        out_specs=[anywhere, anywhere],
        out_shape=[
            jax.ShapeDtypeStruct((tokens, span * count), BF16),
            jax.ShapeDtypeStruct(own.shape, F32),
        ],
        scratch_shapes=[pltpu.VMEM(own.shape, F32), pltpu.SemaphoreType.DMA((count + 1,))],
        compiler_params=pltpu.CompilerParams(vmem_limit_bytes=4 * MIB),
        cost_estimate=pl.CostEstimate(flops=2**30, bytes_accessed=0, transcendentals=0),
        name="finish",
    )(*parts, own, *received)


def add(wide, narrow, out_types, apart):
    count = len(narrow)

    def kernel(wide_ref, *refs):
        for k in range(wide.shape[0]) if apart else [slice(None)]:
            total = wide_ref[k]
            for ref in refs[:count]:
                total = total + ref[k].astype(F32)
            if apart:
                refs[count + k][...] = total.astype(out_types[k])
            else:
                for ref in refs[count:]:
                    ref[...] = total.astype(ref.dtype)

    shape = wide.shape[1:] if apart else wide.shape
    return pl.pallas_call(
        kernel,
        in_specs=[WHOLE] * (1 + count),
        out_specs=[WHOLE] * len(out_types),
        out_shape=[jax.ShapeDtypeStruct(shape, t) for t in out_types],
        compiler_params=pltpu.CompilerParams(vmem_limit_bytes=16 * MIB),
        cost_estimate=pl.CostEstimate(flops=2**28, bytes_accessed=0, transcendentals=0),
        name="add_sums",
    )(wide, *narrow)


def cut(x, count, shares):
    rows, width = x.shape
    span = width // (count * shares)

    def kernel(x_ref, *refs):
        part_refs, sems = refs[:-1], refs[-1]
        ctx = lax.axis_index("ctx")
        share = lax.axis_index("roll") % shares
        copies = [
            pltpu.make_async_copy(
                x_ref.at[:, pl.ds(pl.multiple_of((shares * (ctx ^ k) + share) * span, span), span)],
                part_refs[k],
                sems.at[k],
            )
            for k in range(count)
        ]
        for copy in copies:
            copy.start()
        for copy in copies:
            copy.wait()

    anywhere = pl.BlockSpec(memory_space=pl.ANY)
    return pl.pallas_call(
        kernel,
        in_specs=[anywhere],
        out_specs=[anywhere] * count,
        out_shape=[jax.ShapeDtypeStruct((rows, span), x.dtype)] * count,
        scratch_shapes=[pltpu.SemaphoreType.DMA((count,))],
        compiler_params=pltpu.CompilerParams(vmem_limit_bytes=4 * MIB),
        cost_estimate=pl.CostEstimate(flops=2**30, bytes_accessed=0, transcendentals=0),
        name="cut_hidden",
    )(x)


def turn(x):
    count = len(x)
    rows, cols = x[0].shape

    def kernel(*refs):
        refs[count][...] = jnp.transpose(jnp.concatenate([r[...] for r in refs[:count]], 0))

    return pl.pallas_call(
        kernel,
        in_specs=[WHOLE] * count,
        out_specs=WHOLE,
        out_shape=jax.ShapeDtypeStruct((cols, rows * count), BF16),
        compiler_params=pltpu.CompilerParams(vmem_limit_bytes=12 * MIB),
        cost_estimate=pl.CostEstimate(flops=2**29, bytes_accessed=0, transcendentals=0),
        name="turn_hidden",
    )(*x)


def weight_grads(offsets, shares, low):
    total = len(offsets)
    _, span, slab = shares[0].shape
    _, rows, cols = low[0].shape
    step = min(span, 256)
    steps = span // step
    slots = [(ref, i) for ref, x in enumerate(shares) for i in range(x.shape[0])]

    def kernel(*refs):
        x_refs = refs[: len(shares)]
        low_refs = refs[len(shares) : len(shares) + len(low)]
        out_ref, tiles, sems = refs[len(shares) + len(low) :]
        keys = jnp.concatenate([r[0] for r in low_refs], 0)
        values = jnp.concatenate([r[1] for r in low_refs], 0)
        mine = lax.axis_index("roll") % total
        copies = []
        for offset, (ref, i) in zip(offsets, slots, strict=True):
            for j in range(steps):
                n = len(copies)
                x = x_refs[ref][i, j * step : (j + 1) * step]
                tiles[n, 0] = jnp.dot(x, keys, preferred_element_type=F32)
                tiles[n, 1] = jnp.dot(x, values, preferred_element_type=F32)
                row = pl.multiple_of((mine ^ offset) * span + j * step, step)
                copies.append(
                    pltpu.make_async_copy(tiles.at[n], out_ref.at[:, pl.ds(row, step), :], sems.at[n])
                )
                copies[-1].start()
        for copy in copies:
            copy.wait()

    return pl.pallas_call(
        kernel,
        in_specs=[WHOLE] * (len(shares) + len(low)),
        out_specs=pl.BlockSpec(memory_space=pl.ANY),
        out_shape=jax.ShapeDtypeStruct((2, total * span, cols), F32),
        scratch_shapes=[
            pltpu.VMEM((total * steps, 2, step, cols), F32),
            pltpu.SemaphoreType.DMA((total * steps,)),
        ],
        compiler_params=pltpu.CompilerParams(vmem_limit_bytes=24 * MIB),
        cost_estimate=pl.CostEstimate(flops=2**31, bytes_accessed=0, transcendentals=0),
        name="weight_grads",
    )(*shares, *low)


def on_device(
    queries,
    cotangent,
    out_dot,
    norm_offset,
    prompt_kv,
    prompt_x,
    block_ids,
    lengths,
    advantages,
    adv_index,
):
    ctx_count = lax.axis_size("ctx")
    roll_count = lax.axis_size("roll")
    roll = lax.axis_index("roll")
    _, rows, kv_width = prompt_kv.shape
    cols = kv_width // roll_count
    slab = rows * ctx_count

    def to_ctx(x, offset):
        return lax.ppermute(x, "ctx", xor_pairs(ctx_count, offset))

    def to_roll(x, offset):
        return lax.ppermute(x, "roll", xor_pairs(roll_count, offset))

    last = roll_count - 1
    own = lax.dynamic_slice_in_dim(prompt_kv, (roll ^ last) * cols, cols, 2)
    fetched = jnp.stack([own] + [to_ctx(own, k) for k in range(1, ctx_count)])
    blocks = {last: fetched, last - 1: to_roll(fetched, 1)}
    for d in range(1, roll_count // 2):
        blocks[last - 2 * d] = to_roll(fetched, 2 * d)
        blocks[last - 2 * d - 1] = to_roll(blocks[last - 2 * d], 1)

    shares = roll_count
    while prompt_x.shape[1] // (ctx_count * shares) % HD:
        shares //= 2
    x_cut = cut(prompt_x, ctx_count, shares)
    out_dot, x_cut = lax.optimization_barrier((out_dot, x_cut))
    x_share = turn([x_cut[0]] + [to_ctx(x_cut[k], k) for k in range(1, ctx_count)])[None]

    blocks_total = block_ids.shape[0] * ctx_count * roll_count
    weights, delta, offset = prep(
        blocks_total // lengths.shape[0], slab, block_ids, lengths, advantages, adv_index, out_dot.T, norm_offset.T
    )

    order = list(reversed(range(roll_count)))
    dq = []
    arrived = []
    for off in order:
        kind = BF16 if off % 2 else F32
        part, grads = head_block(
            off, kv_width, queries, cotangent, weights, offset, delta, blocks[off], kind
        )
        dq.append(part)
        if off % 2:
            sibling = to_roll(grads, 1)
        elif off:
            (total,) = add(grads, [sibling], [BF16], False)
            delta, total = lax.optimization_barrier((delta, total))
            arrived.append(to_roll(total, off))
    sums = list(add(grads, [sibling] + arrived, [F32] + [BF16] * (ctx_count - 1), True))
    received = [to_ctx(sums[k], k) for k in range(1, ctx_count)]

    (owned_low,) = add(sums[0], received, [BF16], False)
    offsets, x_parts = [0], [x_share]
    bit = shares // 2
    while bit:
        whole = x_parts[0] if len(x_parts) == 1 else jnp.concatenate(x_parts)
        x_parts.append(to_roll(whole, bit))
        offsets += [offset ^ bit for offset in offsets]
        bit //= 2
        if bit:
            x_parts[-1] = lax.optimization_barrier((x_parts[-1], owned_low))[0]
    low = [owned_low] + [to_ctx(owned_low, k) for k in range(1, ctx_count)]
    dq, sums[0], owned_low = lax.optimization_barrier((dq, sums[0], owned_low))
    query_grad, owned = finish(order, dq, sums[0], received)
    return (query_grad, owned, weight_grads(offsets, x_parts, low))


def solution(mesh):
    placed = (
        P(("groups", "ctx", "roll"), None),
        P(("groups", "ctx", "roll"), None),
        P(("groups", "ctx", "roll"), None),
        P(("groups", "ctx", "roll"), None),
        P(None, ("groups", "ctx"), None),
        P(("groups", "ctx"), None),
        P(("groups", "ctx", "roll")),
        P("groups"),
        P("groups"),
        P("groups"),
    )
    return jax.shard_map(
        on_device,
        mesh=mesh,
        in_specs=placed,
        out_specs=(
            P(("groups", "ctx", "roll"), None),
            P(None, ("groups", "ctx"), "roll"),
            P(None, ("groups", "ctx"), "roll"),
        ),
        check_vma=False,
    )
```

time: 192 us -> 52 us (0.27)
  matrix products: 60.6 us -> 0 us
  waiting for transfers between devices: 62.6 us -> 12.9 us
  local copies, waits for them, and re-layouts: 26.4 us -> 2.22 us
  starting transfers between devices: 3.71 us -> 23.9 us
  blocking collectives: 14.1 us -> 0 us
  between operations: 13.8 us -> 0.92 us
  Pallas kernels: 0 us -> 11.8 us
  other arithmetic: 8.91 us -> 0.09 us
    dot_general x41 -> x0, matrix products: 60.6 us -> none  [the longest x8 15.6 us: one_head(): dk = lax.dot_general(dscore, qg, outer, preferred_element_type=jnp.float32)]
    reduce_scatter x2 -> x0, waiting for transfers between devices: 46.1 us -> none  [the longest x1 25.2 us: on_device(): by_heads = lax.psum_scatter(grads, 'roll', scatter_dimension=2, tiled=True)]
    ppermute x0 -> x20, starting transfers between devices: none -> 23.9 us  [the longest x12 19 us: to_ctx(): return lax.ppermute(x, 'ctx', xor_pairs(ctx_count, offset))]
    all_gather x1 -> x0, waiting for transfers between devices: 16.5 us -> none  [on_device(): lax.all_gather(prompt_kv, 'ctx', axis=1, tiled=True)]
    all_gather x1 -> x0, blocking collectives: 14.1 us -> none  [on_device(): lax.all_gather(owned_low, 'ctx', axis=1, tiled=True)]
    unnamed x15 -> x20, local copies, waits for them, and re-layouts: 15.4 us -> 2.19 us
    ppermute x0 -> x20, waiting for transfers between devices: none -> 12.9 us  [the longest x12 10.7 us: to_ctx(): return lax.ppermute(x, 'ctx', xor_pairs(ctx_count, offset))]
    pallas_call x0 -> x12, Pallas kernels: none -> 11.8 us  [the longest x4 7.09 us: head_block(): pl.pallas_call(functools.partial(heads_kernel, per_kv, off), in_specs=[WH...]
  transfers between devices with their start and end apart: 4 -> 20, of which waited for: 3 -> 7; matrix products, arithmetic and copies ran while one was open for 11% -> 0% of each run, Pallas kernels for 0% -> 18%
where the time goes in v2:
time: 52 us; the launch traced here: 51.8 us
  starting transfers between devices  23.9 us (46%)
  waiting for transfers between devices  12.9 us (25%)
  Pallas kernels  11.8 us (23%)
  local copies, waits for them, and re-layouts  2.22 us (4%)
  between operations  0.92 us (2%)
    ppermute x12, starting transfers between devices, to_ctx(): return lax.ppermute(x, 'ctx', xor_pairs(ctx_count, offset))  19 us
    ppermute x12, waiting for transfers between devices, to_ctx(): return lax.ppermute(x, 'ctx', xor_pairs(ctx_count, offset))  10.7 us
    pallas_call x4, Pallas kernels, head_block(): pl.pallas_call(functools.partial(heads_kernel, per_kv, off), in_specs=[WH...  7.09 us
    ppermute x8, starting transfers between devices, to_roll(): return lax.ppermute(x, 'roll', xor_pairs(roll_count, offset))  4.9 us
    pallas_call x1, Pallas kernels, weight_grads(): pl.pallas_call(kernel, in_specs=[WHOLE] * (len(shares) + len(low)), out_s...  2.31 us
    ppermute x8, waiting for transfers between devices, to_roll(): return lax.ppermute(x, 'roll', xor_pairs(roll_count, offset))  2.2 us
    unnamed x20, local copies, waits for them, and re-layouts  2.19 us
    pallas_call x1, Pallas kernels, finish(): pl.pallas_call(kernel, in_specs=[anywhere] * count + [WHOLE] * (1 + len(r...  1.4 us
  transfers between devices with their start and end apart: 20, of which 7 were waited for; matrix products, arithmetic and copies ran while one was open for 0% of the time, Pallas kernels for 18%

profile of v2, /device:TPU:0, one launch (start us, length us, event | category | flops | bytes accessed | tf_op | source)
XLA Modules:
  0.0 51.8 jit_solution(16124431752459578065)
XLA Ops:
  0.7 0.9 %copy-done = bf16[2,64,1024]{2,1,0:T(8,128)(2,1)S(1)} copy-done((bf16[2,64,1024]{2,1,0:T(8,128)(2,1)S(1)}, bf16[2,64,1024]{2,1,0:T(8,128)(2,1)}, u32[]{:S(2)}) %copy-start) | copy-done | bytes 262168
  1.6 4.1 %collective-permute-start.1 = (bf16[2,64,256]{2,1,0:T(8,128)(2,1)S(1)}, bf16[2,64,256]{2,1,0:T(8,128)(2,1)S(1)}, u32[]{:S(2)}, u32[]{:S(2)}) collective-permute-start(bf16[2,64,256]{2,1,0:T(8,128)(2,1)S(1)} %constant_dynamic-slice_fusion), channel_id=1, source_target_pairs={{0,8},{4,12},{8,0},{12,4},{1,9},{5,13},{9,1},{13,5},{2,10},{6,14},... | collective-permute-start | bytes 196616 | tf_op jit(solution)/shard_map/ppermute | solution.py:302
  5.7 1.6 %collective-permute-start = (bf16[2,64,256]{2,1,0:T(8,128)(2,1)S(1)}, bf16[2,64,256]{2,1,0:T(8,128)(2,1)S(1)}, u32[]{:S(2)}, u32[]{:S(2)}) collective-permute-start(bf16[2,64,256]{2,1,0:T(8,128)(2,1)S(1)} %constant_dynamic-slice_fusion), channel_id=1, source_target_pairs={{0,4},{4,0},{8,12},{12,8},{1,5},{5,1},{9,13},{13,9},{2,6},{6,2},{1... | collective-permute-start | bytes 196616 | tf_op jit(solution)/shard_map/ppermute | solution.py:302
  7.4 1.2 %copy-done.3 = bf16[64,8192]{1,0:T(8,128)(2,1)S(1)} copy-done((bf16[64,8192]{1,0:T(8,128)(2,1)S(1)}, bf16[64,8192]{1,0:T(8,128)(2,1)}, u32[]{:S(2)}) %copy-start.3) | copy-done | bytes 1048600
  8.6 0.1 cut_hidden.1
  8.7 0.7 %prep.1 = (f32[128,128]{1,0:T(8,128)S(1)}, f32[64,128]{1,0:T(8,128)S(1)}, f32[64,128]{1,0:T(8,128)S(1)}) custom-call(s32[4]{0:T(128)S(1)} %copy-done.6, s32[16]{0:T(128)S(1)} %copy-done.7, f32[16]{0:T(128)S(1)} %copy-done.8, s32[16]{0:T(128)S(1)} %copy-done.9, f32[64,128]{1,0:T(8,128)S(1)} %bitcast.11, f32[64,128]{1,0:T(8,128)S(1)} %bitcast.12), custom_call_target="tpu_custom_call" | custom-call | flops 1073741824 | tf_op jit(solution)/shard_map/prep/pallas_call | solution.py:46
  9.4 0.6 %collective-permute-done = bf16[2,64,256]{2,1,0:T(8,128)(2,1)S(1)} collective-permute-done((bf16[2,64,256]{2,1,0:T(8,128)(2,1)S(1)}, bf16[2,64,256]{2,1,0:T(8,128)(2,1)S(1)}, u32[]{:S(2)}, u32[]{:S(2)}) %collective-permute-start) | collective-permute-done | bytes 65568 | tf_op jit(solution)/shard_map/ppermute | solution.py:302
  10.0 3.4 %collective-permute-done.2 = bf16[2,64,256]{2,1,0:T(8,128)(2,1)S(1)} collective-permute-done((bf16[2,64,256]{2,1,0:T(8,128)(2,1)S(1)}, bf16[2,64,256]{2,1,0:T(8,128)(2,1)S(1)}, u32[]{:S(2)}, u32[]{:S(2)}) %collective-permute-start.2) | collective-permute-done | bytes 65568 | tf_op jit(solution)/shard_map/ppermute | solution.py:302
  13.5 1.8 %head_block.4 = (bf16[128,2048]{1,0:T(8,128)(2,1)S(1)}, bf16[4,2,64,256]{3,2,1,0:T(8,128)(2,1)S(1)}) custom-call(bf16[128,8192]{1,0:T(8,128)(2,1)S(1)} %copy-done.1, bf16[128,8192]{1,0:T(8,128)(2,1)S(1)} %copy-done.2, f32[128,128]{1,0:T(8,128)S(1)} %get-tuple-element.42.w_ref, f32[64,128]{1,0:T(8,128)S(1)} %get-tuple-element.43.o_ref, ...), custom_call_target="tpu_custom_call" | custom-call | flops 2013265920 | tf_op jit(solution)/shard_map/head_block/pallas_call | solution.py:99
  15.3 0.5 %collective-permute-start.4 = (bf16[4,2,64,256]{3,2,1,0:T(8,128)(2,1)S(1)}, bf16[4,2,64,256]{3,2,1,0:T(8,128)(2,1)S(1)}, u32[]{:S(2)}, u32[]{:S(2)}) collective-permute-start(bf16[4,2,64,256]{3,2,1,0:T(8,128)(2,1)S(1)} %get-tuple-element.48), channel_id=1, source_target_pairs={{0,1},{1,0},{2,3},{3,2},{4,5},{5,4},{6,7},{7,6},{8,9},{9,8},{10,11... | collective-permute-start | bytes 786440 | tf_op jit(solution)/shard_map/ppermute | solution.py:305
  15.9 1.5 %collective-permute-start.5 = (bf16[4,2,64,256]{3,2,1,0:T(8,128)(2,1)S(1)}, bf16[4,2,64,256]{3,2,1,0:T(8,128)(2,1)S(1)}, u32[]{:S(2)}, u32[]{:S(2)}) collective-permute-start(bf16[4,2,64,256]{3,2,1,0:T(8,128)(2,1)S(1)} %pad_maximum_fusion.1.kv_ref), channel_id=1, source_target_pairs={{0,2},{1,3},{2,0},{3,1},{4,6},{5,7},{6,4},{7,5},{8,10},{9,11},{10,... | collective-permute-start | bytes 786440 | tf_op jit(solution)/shard_map/ppermute | solution.py:305
  17.3 1.8 %collective-permute-start.13 = (bf16[64,512]{1,0:T(8,128)(2,1)S(1)}, bf16[64,512]{1,0:T(8,128)(2,1)S(1)}, u32[]{:S(2)}, u32[]{:S(2)}) collective-permute-start(bf16[64,512]{1,0:T(8,128)(2,1)S(1)} %get-tuple-element.68), channel_id=1, source_target_pairs={{0,8},{4,12},{8,0},{12,4},{1,9},{5,13},{9,1},{13,5},{2,10},{6,14},... | collective-permute-start | bytes 196616 | tf_op jit(solution)/shard_map/ppermute | solution.py:302
  19.2 2.6 %collective-permute-start.14 = (bf16[64,512]{1,0:T(8,128)(2,1)S(1)}, bf16[64,512]{1,0:T(8,128)(2,1)S(1)}, u32[]{:S(2)}, u32[]{:S(2)}) collective-permute-start(bf16[64,512]{1,0:T(8,128)(2,1)S(1)} %get-tuple-element.69), channel_id=1, source_target_pairs={{0,12},{4,8},{8,4},{12,0},{1,13},{5,9},{9,5},{13,1},{2,14},{6,10},... | collective-permute-start | bytes 196616 | tf_op jit(solution)/shard_map/ppermute | solution.py:302
  21.7 1.8 %head_block.5 = (bf16[128,2048]{1,0:T(8,128)(2,1)S(1)}, f32[4,2,64,256]{3,2,1,0:T(8,128)S(1)}) custom-call(bf16[128,8192]{1,0:T(8,128)(2,1)S(1)} %copy-done.1, bf16[128,8192]{1,0:T(8,128)(2,1)S(1)} %copy-done.2, f32[128,128]{1,0:T(8,128)S(1)} %get-tuple-element.42.w_ref, f32[64,128]{1,0:T(8,128)S(1)} %get-tuple-element.43.o_ref, ...), custom_call_target="tpu_custom_call" | custom-call | flops 2013265920 | tf_op jit(solution)/shard_map/head_block/pallas_call | solution.py:99
  23.6 0.6 %collective-permute-start.8 = (bf16[4,2,64,256]{3,2,1,0:T(8,128)(2,1)S(1)}, bf16[4,2,64,256]{3,2,1,0:T(8,128)(2,1)S(1)}, u32[]{:S(2)}, u32[]{:S(2)}) collective-permute-start(bf16[4,2,64,256]{3,2,1,0:T(8,128)(2,1)S(1)} %add_sums.3), channel_id=1, source_target_pairs={{0,2},{1,3},{2,0},{3,1},{4,6},{5,7},{6,4},{7,5},{8,10},{9,11},{10,... | collective-permute-start | bytes 786440 | tf_op jit(solution)/shard_map/ppermute | solution.py:305
  24.2 1.8 %head_block.6 = (bf16[128,2048]{1,0:T(8,128)(2,1)S(1)}, bf16[4,2,64,256]{3,2,1,0:T(8,128)(2,1)S(1)}) custom-call(bf16[128,8192]{1,0:T(8,128)(2,1)S(1)} %copy-done.1, bf16[128,8192]{1,0:T(8,128)(2,1)S(1)} %copy-done.2, f32[128,128]{1,0:T(8,128)S(1)} %get-tuple-element.42.w_ref, f32[64,128]{1,0:T(8,128)S(1)} %get-tuple-element.43.o_ref, ...), custom_call_target="tpu_custom_call" | custom-call | flops 2013265920 | tf_op jit(solution)/shard_map/head_block/pallas_call | solution.py:99
  26.0 0.6 %collective-permute-start.7 = (bf16[4,2,64,256]{3,2,1,0:T(8,128)(2,1)S(1)}, bf16[4,2,64,256]{3,2,1,0:T(8,128)(2,1)S(1)}, u32[]{:S(2)}, u32[]{:S(2)}) collective-permute-start(bf16[4,2,64,256]{3,2,1,0:T(8,128)(2,1)S(1)} %get-tuple-element.53), channel_id=1, source_target_pairs={{0,1},{1,0},{2,3},{3,2},{4,5},{5,4},{6,7},{7,6},{8,9},{9,8},{10,11... | collective-permute-start | bytes 786440 | tf_op jit(solution)/shard_map/ppermute | solution.py:305
  26.6 0.1 turn_hidden.1
  26.7 1.6 %collective-permute-start.15 = (bf16[1,512,256]{2,1,0:T(8,128)(2,1)S(1)}, bf16[1,512,256]{2,1,0:T(8,128)(2,1)S(1)}, u32[]{:S(2)}, u32[]{:S(2)}) collective-permute-start(bf16[1,512,256]{2,1,0:T(8,128)(2,1)S(1)} %bitcast.8), channel_id=1, source_target_pairs={{0,2},{1,3},{2,0},{3,1},{4,6},{5,7},{6,4},{7,5},{8,10},{9,11},{10,... | collective-permute-start | bytes 786440 | tf_op jit(solution)/shard_map/ppermute | solution.py:305
  28.2 1.8 %head_block.7 = (bf16[128,2048]{1,0:T(8,128)(2,1)S(1)}, f32[4,2,64,256]{3,2,1,0:T(8,128)S(1)}) custom-call(bf16[128,8192]{1,0:T(8,128)(2,1)S(1)} %copy-done.1, bf16[128,8192]{1,0:T(8,128)(2,1)S(1)} %copy-done.2, f32[128,128]{1,0:T(8,128)S(1)} %get-tuple-element.42.w_ref, f32[64,128]{1,0:T(8,128)S(1)} %get-tuple-element.43.o_ref, ...), custom_call_target="tpu_custom_call" | custom-call | flops 2013265920 | tf_op jit(solution)/shard_map/head_block/pallas_call | solution.py:99
  30.0 2.2 %collective-permute-done.8.refs_1_ = bf16[4,2,64,256]{3,2,1,0:T(8,128)(2,1)S(1)} collective-permute-done((bf16[4,2,64,256]{3,2,1,0:T(8,128)(2,1)S(1)}, bf16[4,2,64,256]{3,2,1,0:T(8,128)(2,1)S(1)}, u32[]{:S(2)}, u32[]{:S(2)}) %collective-permute-start.8) | collective-permute-done | bytes 262176 | tf_op jit(solution)/shard_map/ppermute | solution.py:305
  32.2 0.1 add_sums.4
  32.4 1.8 %collective-permute-start.10 = (bf16[2,64,256]{2,1,0:T(8,128)(2,1)S(1)}, bf16[2,64,256]{2,1,0:T(8,128)(2,1)S(1)}, u32[]{:S(2)}, u32[]{:S(2)}) collective-permute-start(bf16[2,64,256]{2,1,0:T(8,128)(2,1)S(1)} %get-tuple-element.57), channel_id=1, source_target_pairs={{0,8},{4,12},{8,0},{12,4},{1,9},{5,13},{9,1},{13,5},{2,10},{6,14},... | collective-permute-start | bytes 196616 | tf_op jit(solution)/shard_map/ppermute | solution.py:302
  34.2 2.6 %collective-permute-start.11 = (bf16[2,64,256]{2,1,0:T(8,128)(2,1)S(1)}, bf16[2,64,256]{2,1,0:T(8,128)(2,1)S(1)}, u32[]{:S(2)}, u32[]{:S(2)}) collective-permute-start(bf16[2,64,256]{2,1,0:T(8,128)(2,1)S(1)} %get-tuple-element.58), channel_id=1, source_target_pairs={{0,12},{4,8},{8,4},{12,0},{1,13},{5,9},{9,5},{13,1},{2,14},{6,10},... | collective-permute-start | bytes 196616 | tf_op jit(solution)/shard_map/ppermute | solution.py:302
  36.7 1.3 %collective-permute-done.9.refs_0_.refs_5_ = bf16[2,64,256]{2,1,0:T(8,128)(2,1)S(1)} collective-permute-done((bf16[2,64,256]{2,1,0:T(8,128)(2,1)S(1)}, bf16[2,64,256]{2,1,0:T(8,128)(2,1)S(1)}, u32[]{:S(2)}, u32[]{:S(2)}) %collective-permute-start.9) | collective-permute-done | bytes 65568 | tf_op jit(solution)/shard_map/ppermute | solution.py:302
  38.0 2.2 %collective-permute-done.11.refs_2_.refs_7_ = bf16[2,64,256]{2,1,0:T(8,128)(2,1)S(1)} collective-permute-done((bf16[2,64,256]{2,1,0:T(8,128)(2,1)S(1)}, bf16[2,64,256]{2,1,0:T(8,128)(2,1)S(1)}, u32[]{:S(2)}, u32[]{:S(2)}) %collective-permute-start.11) | collective-permute-done | bytes 65568 | tf_op jit(solution)/shard_map/ppermute | solution.py:302
  40.4 2.6 %collective-permute-start.19 = (bf16[2,64,256]{2,1,0:T(8,128)(2,1)S(1)}, bf16[2,64,256]{2,1,0:T(8,128)(2,1)S(1)}, u32[]{:S(2)}, u32[]{:S(2)}) collective-permute-start(bf16[2,64,256]{2,1,0:T(8,128)(2,1)S(1)} %add_sums.5.refs_3_), channel_id=1, source_target_pairs={{0,12},{4,8},{8,4},{12,0},{1,13},{5,9},{9,5},{13,1},{2,14},{6,10},... | collective-permute-start | bytes 196616 | tf_op jit(solution)/shard_map/ppermute | solution.py:302
  43.0 1.8 %collective-permute-start.17 = (bf16[2,64,256]{2,1,0:T(8,128)(2,1)S(1)}, bf16[2,64,256]{2,1,0:T(8,128)(2,1)S(1)}, u32[]{:S(2)}, u32[]{:S(2)}) collective-permute-start(bf16[2,64,256]{2,1,0:T(8,128)(2,1)S(1)} %add_sums.5.refs_3_), channel_id=1, source_target_pairs={{0,4},{4,0},{8,12},{12,8},{1,5},{5,1},{9,13},{13,9},{2,6},{6,2},{1... | collective-permute-start | bytes 196616 | tf_op jit(solution)/shard_map/ppermute | solution.py:302
  44.9 1.4 %finish.1 = (bf16[128,8192]{1,0:T(8,128)(2,1)}, f32[2,64,256]{2,1,0:T(8,128)}) custom-call(bf16[128,2048]{1,0:T(8,128)(2,1)S(1)} %get-tuple-element.59.refs_0_, bf16[128,2048]{1,0:T(8,128)(2,1)S(1)} %get-tuple-element.60.refs_1_, bf16[128,2048]{1,0:T(8,128)(2,1)S(1)} %get-tuple-element.61.refs_2_, bf16[128,2048]{1,0:T(8,128)(2,1)S(1)} %get-tuple-element.62.refs_3_, ...), custom_call_target="tpu_custom_call" | custom-call | flops 1073741824 | tf_op jit(solution)/shard_map/finish/pallas_call | solution.py:144
  46.3 0.9 %collective-permute-done.19.refs_6_ = bf16[2,64,256]{2,1,0:T(8,128)(2,1)S(1)} collective-permute-done((bf16[2,64,256]{2,1,0:T(8,128)(2,1)S(1)}, bf16[2,64,256]{2,1,0:T(8,128)(2,1)S(1)}, u32[]{:S(2)}, u32[]{:S(2)}) %collective-permute-start.19) | collective-permute-done | bytes 65568 | tf_op jit(solution)/shard_map/ppermute | solution.py:302
  47.2 2.3 %collective-permute-done.18.refs_5_ = bf16[2,64,256]{2,1,0:T(8,128)(2,1)S(1)} collective-permute-done((bf16[2,64,256]{2,1,0:T(8,128)(2,1)S(1)}, bf16[2,64,256]{2,1,0:T(8,128)(2,1)S(1)}, u32[]{:S(2)}, u32[]{:S(2)}) %collective-permute-start.18) | collective-permute-done | bytes 65568 | tf_op jit(solution)/shard_map/ppermute | solution.py:302
  49.5 2.3 %weight_grads.1 = f32[2,2048,256]{2,1,0:T(8,128)} custom-call(bf16[1,512,256]{2,1,0:T(8,128)(2,1)S(1)} %bitcast.10, bf16[1,512,256]{2,1,0:T(8,128)(2,1)S(1)} %collective-permute-done.15.refs_1_, bf16[2,512,256]{2,1,0:T(8,128)(2,1)S(1)} %collective-permute-done.16.refs_2_, bf16[2,64,256]{2,1,0:T(8,128)(2,1)S(1)} %add_sums.5.refs_3_, ...), custom_call_target="tpu_custom_call" | custom-call | flops 2147483648 | tf_op jit(solution)/shard_map/weight_grads/pallas_call | solution.py:267
  (44 shorter events, 0.5 us)
Async XLA Ops:
  0.6 1.0 %copy-start = (bf16[2,64,1024]{2,1,0:T(8,128)(2,1)S(1)}, bf16[2,64,1024]{2,1,0:T(8,128)(2,1)}, u32[]{:S(2)}) copy-start(bf16[2,64,1024]{2,1,0:T(8,128)(2,1)} %param.14) | copy-start | bytes 786436
  1.6 7.1 %copy-start.4 = (f32[128,64]{0,1:T(8,128)S(1)}, f32[128,64]{0,1:T(8,128)}, u32[]{:S(2)}) copy-start(f32[128,64]{0,1:T(8,128)} %param.12) | copy-start | bytes 98308
  1.6 7.1 %copy-start.5 = (f32[128,64]{0,1:T(8,128)S(1)}, f32[128,64]{0,1:T(8,128)}, u32[]{:S(2)}) copy-start(f32[128,64]{0,1:T(8,128)} %param.13) | copy-start | bytes 98308
  1.6 7.1 %copy-start.6 = (s32[4]{0:T(128)S(1)}, s32[4]{0:T(128)}, u32[]{:S(2)}) copy-start(s32[4]{0:T(128)} %ids.1) | copy-start | bytes 52
  1.6 7.1 %copy-start.7 = (s32[16]{0:T(128)S(1)}, s32[16]{0:T(128)}, u32[]{:S(2)}) copy-start(s32[16]{0:T(128)} %lengths.1) | copy-start | bytes 196
  1.6 7.1 %copy-start.8 = (f32[16]{0:T(128)S(1)}, f32[16]{0:T(128)}, u32[]{:S(2)}) copy-start(f32[16]{0:T(128)} %advantages.1) | copy-start | bytes 196
  1.6 7.1 %copy-start.9 = (s32[16]{0:T(128)S(1)}, s32[16]{0:T(128)}, u32[]{:S(2)}) copy-start(s32[16]{0:T(128)} %adv_index.1) | copy-start | bytes 196
  1.6 7.8 %collective-permute-start.1 = (bf16[2,64,256]{2,1,0:T(8,128)(2,1)S(1)}, bf16[2,64,256]{2,1,0:T(8,128)(2,1)S(1)}, u32[]{:S(2)}, u32[]{:S(2)}) collective-permute-start(bf16[2,64,256]{2,1,0:T(8,128)(2,1)S(1)} %constant_dynamic-slice_fusion), channel_id=1, source_target_pairs={{0,8},{4,12},{8,0},{12,4},{1,9},{5,13},{9,1},{13,5},{2,10},{6,14},... | collective-permute-start | bytes 196616 | tf_op jit(solution)/shard_map/ppermute | solution.py:302
  5.7 4.3 %collective-permute-start = (bf16[2,64,256]{2,1,0:T(8,128)(2,1)S(1)}, bf16[2,64,256]{2,1,0:T(8,128)(2,1)S(1)}, u32[]{:S(2)}, u32[]{:S(2)}) collective-permute-start(bf16[2,64,256]{2,1,0:T(8,128)(2,1)S(1)} %constant_dynamic-slice_fusion), channel_id=1, source_target_pairs={{0,4},{4,0},{8,12},{12,8},{1,5},{5,1},{9,13},{13,9},{2,6},{6,2},{1... | collective-permute-start | bytes 196616 | tf_op jit(solution)/shard_map/ppermute | solution.py:302
  7.3 6.1 %collective-permute-start.2 = (bf16[2,64,256]{2,1,0:T(8,128)(2,1)S(1)}, bf16[2,64,256]{2,1,0:T(8,128)(2,1)S(1)}, u32[]{:S(2)}, u32[]{:S(2)}) collective-permute-start(bf16[2,64,256]{2,1,0:T(8,128)(2,1)S(1)} %constant_dynamic-slice_fusion), channel_id=1, source_target_pairs={{0,12},{4,8},{8,4},{12,0},{1,13},{5,9},{9,5},{13,1},{2,14},{6,10},... | collective-permute-start | bytes 196616 | tf_op jit(solution)/shard_map/ppermute | solution.py:302
  7.3 1.2 %copy-start.3 = (bf16[64,8192]{1,0:T(8,128)(2,1)S(1)}, bf16[64,8192]{1,0:T(8,128)(2,1)}, u32[]{:S(2)}) copy-start(bf16[64,8192]{1,0:T(8,128)(2,1)} %x_ref.1) | copy-start | bytes 3145732
  8.7 4.8 %copy-start.1 = (bf16[128,8192]{1,0:T(8,128)(2,1)S(1)}, bf16[128,8192]{1,0:T(8,128)(2,1)}, u32[]{:S(2)}) copy-start(bf16[128,8192]{1,0:T(8,128)(2,1)} %q_ref.7) | copy-start | bytes 6291460
  8.7 4.8 %copy-start.2 = (bf16[128,8192]{1,0:T(8,128)(2,1)S(1)}, bf16[128,8192]{1,0:T(8,128)(2,1)}, u32[]{:S(2)}) copy-start(bf16[128,8192]{1,0:T(8,128)(2,1)} %ct_ref.7) | copy-start | bytes 6291460
  13.4 5.7 %collective-permute-start.3 = (bf16[4,2,64,256]{3,2,1,0:T(8,128)(2,1)S(1)}, bf16[4,2,64,256]{3,2,1,0:T(8,128)(2,1)S(1)}, u32[]{:S(2)}, u32[]{:S(2)}) collective-permute-start(bf16[4,2,64,256]{3,2,1,0:T(8,128)(2,1)S(1)} %pad_maximum_fusion.1.kv_ref), channel_id=1, source_target_pairs={{0,1},{1,0},{2,3},{3,2},{4,5},{5,4},{6,7},{7,6},{8,9},{9,8},{10,11... | collective-permute-start | bytes 786440 | tf_op jit(solution)/shard_map/ppermute | solution.py:305
  15.3 8.2 %collective-permute-start.4 = (bf16[4,2,64,256]{3,2,1,0:T(8,128)(2,1)S(1)}, bf16[4,2,64,256]{3,2,1,0:T(8,128)(2,1)S(1)}, u32[]{:S(2)}, u32[]{:S(2)}) collective-permute-start(bf16[4,2,64,256]{3,2,1,0:T(8,128)(2,1)S(1)} %get-tuple-element.48), channel_id=1, source_target_pairs={{0,1},{1,0},{2,3},{3,2},{4,5},{5,4},{6,7},{7,6},{8,9},{9,8},{10,11... | collective-permute-start | bytes 786440 | tf_op jit(solution)/shard_map/ppermute | solution.py:305
  15.9 8.3 %collective-permute-start.5 = (bf16[4,2,64,256]{3,2,1,0:T(8,128)(2,1)S(1)}, bf16[4,2,64,256]{3,2,1,0:T(8,128)(2,1)S(1)}, u32[]{:S(2)}, u32[]{:S(2)}) collective-permute-start(bf16[4,2,64,256]{3,2,1,0:T(8,128)(2,1)S(1)} %pad_maximum_fusion.1.kv_ref), channel_id=1, source_target_pairs={{0,2},{1,3},{2,0},{3,1},{4,6},{5,7},{6,4},{7,5},{8,10},{9,11},{10,... | collective-permute-start | bytes 786440 | tf_op jit(solution)/shard_map/ppermute | solution.py:305
  17.3 8.6 %collective-permute-start.12 = (bf16[64,512]{1,0:T(8,128)(2,1)S(1)}, bf16[64,512]{1,0:T(8,128)(2,1)S(1)}, u32[]{:S(2)}, u32[]{:S(2)}) collective-permute-start(bf16[64,512]{1,0:T(8,128)(2,1)S(1)} %get-tuple-element.67), channel_id=1, source_target_pairs={{0,4},{4,0},{8,12},{12,8},{1,5},{5,1},{9,13},{13,9},{2,6},{6,2},{1... | collective-permute-start | bytes 196616 | tf_op jit(solution)/shard_map/ppermute | solution.py:302
  17.3 9.2 %collective-permute-start.13 = (bf16[64,512]{1,0:T(8,128)(2,1)S(1)}, bf16[64,512]{1,0:T(8,128)(2,1)S(1)}, u32[]{:S(2)}, u32[]{:S(2)}) collective-permute-start(bf16[64,512]{1,0:T(8,128)(2,1)S(1)} %get-tuple-element.68), channel_id=1, source_target_pairs={{0,8},{4,12},{8,0},{12,4},{1,9},{5,13},{9,1},{13,5},{2,10},{6,14},... | collective-permute-start | bytes 196616 | tf_op jit(solution)/shard_map/ppermute | solution.py:302
  19.2 7.4 %collective-permute-start.14 = (bf16[64,512]{1,0:T(8,128)(2,1)S(1)}, bf16[64,512]{1,0:T(8,128)(2,1)S(1)}, u32[]{:S(2)}, u32[]{:S(2)}) collective-permute-start(bf16[64,512]{1,0:T(8,128)(2,1)S(1)} %get-tuple-element.69), channel_id=1, source_target_pairs={{0,12},{4,8},{8,4},{12,0},{1,13},{5,9},{9,5},{13,1},{2,14},{6,10},... | collective-permute-start | bytes 196616 | tf_op jit(solution)/shard_map/ppermute | solution.py:302
  23.6 8.6 %collective-permute-start.8 = (bf16[4,2,64,256]{3,2,1,0:T(8,128)(2,1)S(1)}, bf16[4,2,64,256]{3,2,1,0:T(8,128)(2,1)S(1)}, u32[]{:S(2)}, u32[]{:S(2)}) collective-permute-start(bf16[4,2,64,256]{3,2,1,0:T(8,128)(2,1)S(1)} %add_sums.3), channel_id=1, source_target_pairs={{0,2},{1,3},{2,0},{3,1},{4,6},{5,7},{6,4},{7,5},{8,10},{9,11},{10,... | collective-permute-start | bytes 786440 | tf_op jit(solution)/shard_map/ppermute | solution.py:305
  24.2 4.1 %collective-permute-start.6 = (bf16[4,2,64,256]{3,2,1,0:T(8,128)(2,1)S(1)}, bf16[4,2,64,256]{3,2,1,0:T(8,128)(2,1)S(1)}, u32[]{:S(2)}, u32[]{:S(2)}) collective-permute-start(bf16[4,2,64,256]{3,2,1,0:T(8,128)(2,1)S(1)} %collective-permute-done.5.kv_ref), channel_id=1, source_target_pairs={{0,1},{1,0},{2,3},{3,2},{4,5},{5,4},{6,7},{7,6},{8,9},{9,8},{10,11... | collective-permute-start | bytes 786440 | tf_op jit(solution)/shard_map/ppermute | solution.py:305
  26.0 6.2 %collective-permute-start.7 = (bf16[4,2,64,256]{3,2,1,0:T(8,128)(2,1)S(1)}, bf16[4,2,64,256]{3,2,1,0:T(8,128)(2,1)S(1)}, u32[]{:S(2)}, u32[]{:S(2)}) collective-permute-start(bf16[4,2,64,256]{3,2,1,0:T(8,128)(2,1)S(1)} %get-tuple-element.53), channel_id=1, source_target_pairs={{0,1},{1,0},{2,3},{3,2},{4,5},{5,4},{6,7},{7,6},{8,9},{9,8},{10,11... | collective-permute-start | bytes 786440 | tf_op jit(solution)/shard_map/ppermute | solution.py:305
  26.7 13.6 %collective-permute-start.15 = (bf16[1,512,256]{2,1,0:T(8,128)(2,1)S(1)}, bf16[1,512,256]{2,1,0:T(8,128)(2,1)S(1)}, u32[]{:S(2)}, u32[]{:S(2)}) collective-permute-start(bf16[1,512,256]{2,1,0:T(8,128)(2,1)S(1)} %bitcast.8), channel_id=1, source_target_pairs={{0,2},{1,3},{2,0},{3,1},{4,6},{5,7},{6,4},{7,5},{8,10},{9,11},{10,... | collective-permute-start | bytes 786440 | tf_op jit(solution)/shard_map/ppermute | solution.py:305
  32.3 5.7 %collective-permute-start.9 = (bf16[2,64,256]{2,1,0:T(8,128)(2,1)S(1)}, bf16[2,64,256]{2,1,0:T(8,128)(2,1)S(1)}, u32[]{:S(2)}, u32[]{:S(2)}) collective-permute-start(bf16[2,64,256]{2,1,0:T(8,128)(2,1)S(1)} %get-tuple-element.56), channel_id=1, source_target_pairs={{0,4},{4,0},{8,12},{12,8},{1,5},{5,1},{9,13},{13,9},{2,6},{6,2},{1... | collective-permute-start | bytes 196616 | tf_op jit(solution)/shard_map/ppermute | solution.py:302
  32.4 5.7 %collective-permute-start.10 = (bf16[2,64,256]{2,1,0:T(8,128)(2,1)S(1)}, bf16[2,64,256]{2,1,0:T(8,128)(2,1)S(1)}, u32[]{:S(2)}, u32[]{:S(2)}) collective-permute-start(bf16[2,64,256]{2,1,0:T(8,128)(2,1)S(1)} %get-tuple-element.57), channel_id=1, source_target_pairs={{0,8},{4,12},{8,0},{12,4},{1,9},{5,13},{9,1},{13,5},{2,10},{6,14},... | collective-permute-start | bytes 196616 | tf_op jit(solution)/shard_map/ppermute | solution.py:302
  34.2 6.1 %collective-permute-start.11 = (bf16[2,64,256]{2,1,0:T(8,128)(2,1)S(1)}, bf16[2,64,256]{2,1,0:T(8,128)(2,1)S(1)}, u32[]{:S(2)}, u32[]{:S(2)}) collective-permute-start(bf16[2,64,256]{2,1,0:T(8,128)(2,1)S(1)} %get-tuple-element.58), channel_id=1, source_target_pairs={{0,12},{4,8},{8,4},{12,0},{1,13},{5,9},{9,5},{13,1},{2,14},{6,10},... | collective-permute-start | bytes 196616 | tf_op jit(solution)/shard_map/ppermute | solution.py:302
  40.3 9.2 %collective-permute-start.16 = (bf16[2,512,256]{2,1,0:T(8,128)(2,1)S(1)}, bf16[2,512,256]{2,1,0:T(8,128)(2,1)S(1)}, u32[]{:S(2)}, u32[]{:S(2)}) collective-permute-start(bf16[2,512,256]{2,1,0:T(8,128)(2,1)S(1)} %pad_maximum_fusion), channel_id=1, source_target_pairs={{0,1},{1,0},{2,3},{3,2},{4,5},{5,4},{6,7},{7,6},{8,9},{9,8},{10,11... | collective-permute-start | bytes 1572872 | tf_op jit(solution)/shard_map/ppermute | solution.py:305
  40.4 6.8 %collective-permute-start.19 = (bf16[2,64,256]{2,1,0:T(8,128)(2,1)S(1)}, bf16[2,64,256]{2,1,0:T(8,128)(2,1)S(1)}, u32[]{:S(2)}, u32[]{:S(2)}) collective-permute-start(bf16[2,64,256]{2,1,0:T(8,128)(2,1)S(1)} %add_sums.5.refs_3_), channel_id=1, source_target_pairs={{0,12},{4,8},{8,4},{12,0},{1,13},{5,9},{9,5},{13,1},{2,14},{6,10},... | collective-permute-start | bytes 196616 | tf_op jit(solution)/shard_map/ppermute | solution.py:302
  43.0 6.5 %collective-permute-start.18 = (bf16[2,64,256]{2,1,0:T(8,128)(2,1)S(1)}, bf16[2,64,256]{2,1,0:T(8,128)(2,1)S(1)}, u32[]{:S(2)}, u32[]{:S(2)}) collective-permute-start(bf16[2,64,256]{2,1,0:T(8,128)(2,1)S(1)} %add_sums.5.refs_3_), channel_id=1, source_target_pairs={{0,8},{4,12},{8,0},{12,4},{1,9},{5,13},{9,1},{13,5},{2,10},{6,14},... | collective-permute-start | bytes 196616 | tf_op jit(solution)/shard_map/ppermute | solution.py:302
  43.0 6.5 %collective-permute-start.17 = (bf16[2,64,256]{2,1,0:T(8,128)(2,1)S(1)}, bf16[2,64,256]{2,1,0:T(8,128)(2,1)S(1)}, u32[]{:S(2)}, u32[]{:S(2)}) collective-permute-start(bf16[2,64,256]{2,1,0:T(8,128)(2,1)S(1)} %add_sums.5.refs_3_), channel_id=1, source_target_pairs={{0,4},{4,0},{8,12},{12,8},{1,5},{5,1},{9,13},{13,9},{2,6},{6,2},{1... | collective-permute-start | bytes 196616 | tf_op jit(solution)/shard_map/ppermute | solution.py:302

commit v3 on v2

--- a/solution.py
+++ b/solution.py
@@ -238,7 +238,7 @@
     total = len(offsets)
     _, span, slab = shares[0].shape
     _, rows, cols = low[0].shape
-    step = min(span, 256)
+    step = min(span, 512)
     steps = span // step
     slots = [(ref, i) for ref, x in enumerate(shares) for i in range(x.shape[0])]
 
@@ -317,7 +317,7 @@
         shares //= 2
     x_cut = cut(prompt_x, ctx_count, shares)
     out_dot, x_cut = lax.optimization_barrier((out_dot, x_cut))
-    x_share = turn([x_cut[0]] + [to_ctx(x_cut[k], k) for k in range(1, ctx_count)])[None]
+    x_pieces = [x_cut[0]] + [to_ctx(x_cut[k], k) for k in range(1, ctx_count)]
 
     blocks_total = block_ids.shape[0] * ctx_count * roll_count
     weights, delta, offset = prep(
@@ -333,6 +333,9 @@
             off, kv_width, queries, cotangent, weights, offset, delta, blocks[off], kind
         )
         dq.append(part)
+        if off == 1:
+            x_pieces = lax.optimization_barrier((x_pieces, grads))[0]
+            x_share = turn(x_pieces)[None]
         if off % 2:
             sibling = to_roll(grads, 1)
         elif off:
@@ -343,6 +346,7 @@
     received = [to_ctx(sums[k], k) for k in range(1, ctx_count)]
 
     (owned_low,) = add(sums[0], received, [BF16], False)
+    x_share = lax.optimization_barrier((x_share, sums[0]))[0]
     offsets, x_parts = [0], [x_share]
     bit = shares // 2
     while bit:

time: 52 us -> 51.3 us (0.987)
  starting transfers between devices: 23.9 us -> 22.9 us
    ppermute x8, starting transfers between devices: 4.9 us -> 3.95 us  [to_roll(): return lax.ppermute(x, 'roll', xor_pairs(roll_count, offset))]
where the time goes in v3:
time: 51.3 us; the launch traced here: 51.1 us
  starting transfers between devices  22.9 us (45%)
  waiting for transfers between devices  13.2 us (26%)
  Pallas kernels  11.9 us (23%)
  local copies, waits for them, and re-layouts  2.22 us (4%)
  between operations  0.92 us (2%)
    ppermute x12, starting transfers between devices, to_ctx(): return lax.ppermute(x, 'ctx', xor_pairs(ctx_count, offset))  18.9 us
    ppermute x12, waiting for transfers between devices, to_ctx(): return lax.ppermute(x, 'ctx', xor_pairs(ctx_count, offset))  10.8 us
    pallas_call x4, Pallas kernels, head_block(): pl.pallas_call(functools.partial(heads_kernel, per_kv, off), in_specs=[WH...  7.11 us
    ppermute x8, starting transfers between devices, to_roll(): return lax.ppermute(x, 'roll', xor_pairs(roll_count, offset))  3.95 us
    ppermute x8, waiting for transfers between devices, to_roll(): return lax.ppermute(x, 'roll', xor_pairs(roll_count, offset))  2.36 us
    pallas_call x1, Pallas kernels, weight_grads(): pl.pallas_call(kernel, in_specs=[WHOLE] * (len(shares) + len(low)), out_s...  2.34 us
    unnamed x20, local copies, waits for them, and re-layouts  2.19 us
    pallas_call x1, Pallas kernels, finish(): pl.pallas_call(kernel, in_specs=[anywhere] * count + [WHOLE] * (1 + len(r...  1.4 us
  transfers between devices with their start and end apart: 20, of which 7 were waited for; matrix products, arithmetic and copies ran while one was open for 0% of the time, Pallas kernels for 18%

profile of v3, /device:TPU:0, one launch (start us, length us, event | category | flops | bytes accessed | tf_op | source)
XLA Modules:
  0.0 51.1 jit_solution(7095512918100829056)
XLA Ops:
  0.7 0.9 %copy-done = bf16[2,64,1024]{2,1,0:T(8,128)(2,1)S(1)} copy-done((bf16[2,64,1024]{2,1,0:T(8,128)(2,1)S(1)}, bf16[2,64,1024]{2,1,0:T(8,128)(2,1)}, u32[]{:S(2)}) %copy-start) | copy-done | bytes 262168
  1.6 4.1 %collective-permute-start.1 = (bf16[2,64,256]{2,1,0:T(8,128)(2,1)S(1)}, bf16[2,64,256]{2,1,0:T(8,128)(2,1)S(1)}, u32[]{:S(2)}, u32[]{:S(2)}) collective-permute-start(bf16[2,64,256]{2,1,0:T(8,128)(2,1)S(1)} %constant_dynamic-slice_fusion), channel_id=1, source_target_pairs={{0,8},{4,12},{8,0},{12,4},{1,9},{5,13},{9,1},{13,5},{2,10},{6,14},... | collective-permute-start | bytes 196616 | tf_op jit(solution)/shard_map/ppermute | solution.py:302
  5.7 1.6 %collective-permute-start = (bf16[2,64,256]{2,1,0:T(8,128)(2,1)S(1)}, bf16[2,64,256]{2,1,0:T(8,128)(2,1)S(1)}, u32[]{:S(2)}, u32[]{:S(2)}) collective-permute-start(bf16[2,64,256]{2,1,0:T(8,128)(2,1)S(1)} %constant_dynamic-slice_fusion), channel_id=1, source_target_pairs={{0,4},{4,0},{8,12},{12,8},{1,5},{5,1},{9,13},{13,9},{2,6},{6,2},{1... | collective-permute-start | bytes 196616 | tf_op jit(solution)/shard_map/ppermute | solution.py:302
  7.4 1.2 %copy-done.3 = bf16[64,8192]{1,0:T(8,128)(2,1)S(1)} copy-done((bf16[64,8192]{1,0:T(8,128)(2,1)S(1)}, bf16[64,8192]{1,0:T(8,128)(2,1)}, u32[]{:S(2)}) %copy-start.3) | copy-done | bytes 1048600
  8.6 0.1 cut_hidden.1
  8.7 0.7 %prep.1 = (f32[128,128]{1,0:T(8,128)S(1)}, f32[64,128]{1,0:T(8,128)S(1)}, f32[64,128]{1,0:T(8,128)S(1)}) custom-call(s32[4]{0:T(128)S(1)} %copy-done.6, s32[16]{0:T(128)S(1)} %copy-done.7, f32[16]{0:T(128)S(1)} %copy-done.8, s32[16]{0:T(128)S(1)} %copy-done.9, f32[64,128]{1,0:T(8,128)S(1)} %bitcast.11, f32[64,128]{1,0:T(8,128)S(1)} %bitcast.12), custom_call_target="tpu_custom_call" | custom-call | flops 1073741824 | tf_op jit(solution)/shard_map/prep/pallas_call | solution.py:46
  9.4 0.6 %collective-permute-done = bf16[2,64,256]{2,1,0:T(8,128)(2,1)S(1)} collective-permute-done((bf16[2,64,256]{2,1,0:T(8,128)(2,1)S(1)}, bf16[2,64,256]{2,1,0:T(8,128)(2,1)S(1)}, u32[]{:S(2)}, u32[]{:S(2)}) %collective-permute-start) | collective-permute-done | bytes 65568 | tf_op jit(solution)/shard_map/ppermute | solution.py:302
  10.0 3.4 %collective-permute-done.2 = bf16[2,64,256]{2,1,0:T(8,128)(2,1)S(1)} collective-permute-done((bf16[2,64,256]{2,1,0:T(8,128)(2,1)S(1)}, bf16[2,64,256]{2,1,0:T(8,128)(2,1)S(1)}, u32[]{:S(2)}, u32[]{:S(2)}) %collective-permute-start.2) | collective-permute-done | bytes 65568 | tf_op jit(solution)/shard_map/ppermute | solution.py:302
  13.5 1.8 %head_block.4 = (bf16[128,2048]{1,0:T(8,128)(2,1)S(1)}, bf16[4,2,64,256]{3,2,1,0:T(8,128)(2,1)S(1)}) custom-call(bf16[128,8192]{1,0:T(8,128)(2,1)S(1)} %copy-done.1, bf16[128,8192]{1,0:T(8,128)(2,1)S(1)} %copy-done.2, f32[128,128]{1,0:T(8,128)S(1)} %get-tuple-element.47.w_ref, f32[64,128]{1,0:T(8,128)S(1)} %get-tuple-element.48.o_ref, ...), custom_call_target="tpu_custom_call" | custom-call | flops 2013265920 | tf_op jit(solution)/shard_map/head_block/pallas_call | solution.py:99
  15.3 0.5 %collective-permute-start.4 = (bf16[4,2,64,256]{3,2,1,0:T(8,128)(2,1)S(1)}, bf16[4,2,64,256]{3,2,1,0:T(8,128)(2,1)S(1)}, u32[]{:S(2)}, u32[]{:S(2)}) collective-permute-start(bf16[4,2,64,256]{3,2,1,0:T(8,128)(2,1)S(1)} %get-tuple-element.53), channel_id=1, source_target_pairs={{0,1},{1,0},{2,3},{3,2},{4,5},{5,4},{6,7},{7,6},{8,9},{9,8},{10,11... | collective-permute-start | bytes 786440 | tf_op jit(solution)/shard_map/ppermute | solution.py:305
  15.9 1.5 %collective-permute-start.5 = (bf16[4,2,64,256]{3,2,1,0:T(8,128)(2,1)S(1)}, bf16[4,2,64,256]{3,2,1,0:T(8,128)(2,1)S(1)}, u32[]{:S(2)}, u32[]{:S(2)}) collective-permute-start(bf16[4,2,64,256]{3,2,1,0:T(8,128)(2,1)S(1)} %pad_maximum_fusion.1.kv_ref), channel_id=1, source_target_pairs={{0,2},{1,3},{2,0},{3,1},{4,6},{5,7},{6,4},{7,5},{8,10},{9,11},{10,... | collective-permute-start | bytes 786440 | tf_op jit(solution)/shard_map/ppermute | solution.py:305
  17.3 1.8 %collective-permute-start.13 = (bf16[64,512]{1,0:T(8,128)(2,1)S(1)}, bf16[64,512]{1,0:T(8,128)(2,1)S(1)}, u32[]{:S(2)}, u32[]{:S(2)}) collective-permute-start(bf16[64,512]{1,0:T(8,128)(2,1)S(1)} %get-tuple-element.73), channel_id=1, source_target_pairs={{0,8},{4,12},{8,0},{12,4},{1,9},{5,13},{9,1},{13,5},{2,10},{6,14},... | collective-permute-start | bytes 196616 | tf_op jit(solution)/shard_map/ppermute | solution.py:302
  19.2 2.6 %collective-permute-start.14 = (bf16[64,512]{1,0:T(8,128)(2,1)S(1)}, bf16[64,512]{1,0:T(8,128)(2,1)S(1)}, u32[]{:S(2)}, u32[]{:S(2)}) collective-permute-start(bf16[64,512]{1,0:T(8,128)(2,1)S(1)} %get-tuple-element.74), channel_id=1, source_target_pairs={{0,12},{4,8},{8,4},{12,0},{1,13},{5,9},{9,5},{13,1},{2,14},{6,10},... | collective-permute-start | bytes 196616 | tf_op jit(solution)/shard_map/ppermute | solution.py:302
  21.7 1.8 %head_block.5 = (bf16[128,2048]{1,0:T(8,128)(2,1)S(1)}, f32[4,2,64,256]{3,2,1,0:T(8,128)S(1)}) custom-call(bf16[128,8192]{1,0:T(8,128)(2,1)S(1)} %copy-done.1, bf16[128,8192]{1,0:T(8,128)(2,1)S(1)} %copy-done.2, f32[128,128]{1,0:T(8,128)S(1)} %get-tuple-element.47.w_ref, f32[64,128]{1,0:T(8,128)S(1)} %get-tuple-element.48.o_ref, ...), custom_call_target="tpu_custom_call" | custom-call | flops 2013265920 | tf_op jit(solution)/shard_map/head_block/pallas_call | solution.py:99
  23.6 0.6 %collective-permute-start.8 = (bf16[4,2,64,256]{3,2,1,0:T(8,128)(2,1)S(1)}, bf16[4,2,64,256]{3,2,1,0:T(8,128)(2,1)S(1)}, u32[]{:S(2)}, u32[]{:S(2)}) collective-permute-start(bf16[4,2,64,256]{3,2,1,0:T(8,128)(2,1)S(1)} %add_sums.3), channel_id=1, source_target_pairs={{0,2},{1,3},{2,0},{3,1},{4,6},{5,7},{6,4},{7,5},{8,10},{9,11},{10,... | collective-permute-start | bytes 786440 | tf_op jit(solution)/shard_map/ppermute | solution.py:305
  24.2 1.8 %head_block.6 = (bf16[128,2048]{1,0:T(8,128)(2,1)S(1)}, bf16[4,2,64,256]{3,2,1,0:T(8,128)(2,1)S(1)}) custom-call(bf16[128,8192]{1,0:T(8,128)(2,1)S(1)} %copy-done.1, bf16[128,8192]{1,0:T(8,128)(2,1)S(1)} %copy-done.2, f32[128,128]{1,0:T(8,128)S(1)} %get-tuple-element.47.w_ref, f32[64,128]{1,0:T(8,128)S(1)} %get-tuple-element.48.o_ref, ...), custom_call_target="tpu_custom_call" | custom-call | flops 2013265920 | tf_op jit(solution)/shard_map/head_block/pallas_call | solution.py:99
  26.0 0.6 %collective-permute-start.7 = (bf16[4,2,64,256]{3,2,1,0:T(8,128)(2,1)S(1)}, bf16[4,2,64,256]{3,2,1,0:T(8,128)(2,1)S(1)}, u32[]{:S(2)}, u32[]{:S(2)}) collective-permute-start(bf16[4,2,64,256]{3,2,1,0:T(8,128)(2,1)S(1)} %get-tuple-element.58), channel_id=1, source_target_pairs={{0,1},{1,0},{2,3},{3,2},{4,5},{5,4},{6,7},{7,6},{8,9},{9,8},{10,11... | collective-permute-start | bytes 786440 | tf_op jit(solution)/shard_map/ppermute | solution.py:305
  26.6 0.1 turn_hidden.1
  26.7 1.8 %head_block.7 = (bf16[128,2048]{1,0:T(8,128)(2,1)S(1)}, f32[4,2,64,256]{3,2,1,0:T(8,128)S(1)}) custom-call(bf16[128,8192]{1,0:T(8,128)(2,1)S(1)} %copy-done.1, bf16[128,8192]{1,0:T(8,128)(2,1)S(1)} %copy-done.2, f32[128,128]{1,0:T(8,128)S(1)} %get-tuple-element.47.w_ref, f32[64,128]{1,0:T(8,128)S(1)} %get-tuple-element.48.o_ref, ...), custom_call_target="tpu_custom_call" | custom-call | flops 2013265920 | tf_op jit(solution)/shard_map/head_block/pallas_call | solution.py:99
  28.5 2.3 %collective-permute-done.8.refs_1_ = bf16[4,2,64,256]{3,2,1,0:T(8,128)(2,1)S(1)} collective-permute-done((bf16[4,2,64,256]{3,2,1,0:T(8,128)(2,1)S(1)}, bf16[4,2,64,256]{3,2,1,0:T(8,128)(2,1)S(1)}, u32[]{:S(2)}, u32[]{:S(2)}) %collective-permute-start.8) | collective-permute-done | bytes 262176 | tf_op jit(solution)/shard_map/ppermute | solution.py:305
  30.8 0.1 add_sums.4
  30.9 0.6 %collective-permute-start.15 = (bf16[1,512,256]{2,1,0:T(8,128)(2,1)S(1)}, bf16[1,512,256]{2,1,0:T(8,128)(2,1)S(1)}, u32[]{:S(2)}, u32[]{:S(2)}) collective-permute-start(bf16[1,512,256]{2,1,0:T(8,128)(2,1)S(1)} %bitcast.8), channel_id=1, source_target_pairs={{0,2},{1,3},{2,0},{3,1},{4,6},{5,7},{6,4},{7,5},{8,10},{9,11},{10,... | collective-permute-start | bytes 786440 | tf_op jit(solution)/shard_map/ppermute | solution.py:305
  31.5 1.8 %collective-permute-start.10 = (bf16[2,64,256]{2,1,0:T(8,128)(2,1)S(1)}, bf16[2,64,256]{2,1,0:T(8,128)(2,1)S(1)}, u32[]{:S(2)}, u32[]{:S(2)}) collective-permute-start(bf16[2,64,256]{2,1,0:T(8,128)(2,1)S(1)} %get-tuple-element.62), channel_id=1, source_target_pairs={{0,8},{4,12},{8,0},{12,4},{1,9},{5,13},{9,1},{13,5},{2,10},{6,14},... | collective-permute-start | bytes 196616 | tf_op jit(solution)/shard_map/ppermute | solution.py:302
  33.3 2.6 %collective-permute-start.11 = (bf16[2,64,256]{2,1,0:T(8,128)(2,1)S(1)}, bf16[2,64,256]{2,1,0:T(8,128)(2,1)S(1)}, u32[]{:S(2)}, u32[]{:S(2)}) collective-permute-start(bf16[2,64,256]{2,1,0:T(8,128)(2,1)S(1)} %get-tuple-element.63), channel_id=1, source_target_pairs={{0,12},{4,8},{8,4},{12,0},{1,13},{5,9},{9,5},{13,1},{2,14},{6,10},... | collective-permute-start | bytes 196616 | tf_op jit(solution)/shard_map/ppermute | solution.py:302
  35.9 2.3 %collective-permute-done.10.refs_1_.refs_6_ = bf16[2,64,256]{2,1,0:T(8,128)(2,1)S(1)} collective-permute-done((bf16[2,64,256]{2,1,0:T(8,128)(2,1)S(1)}, bf16[2,64,256]{2,1,0:T(8,128)(2,1)S(1)}, u32[]{:S(2)}, u32[]{:S(2)}) %collective-permute-start.10) | collective-permute-done | bytes 65568 | tf_op jit(solution)/shard_map/ppermute | solution.py:302
  38.2 1.3 %collective-permute-done.11.refs_2_.refs_7_ = bf16[2,64,256]{2,1,0:T(8,128)(2,1)S(1)} collective-permute-done((bf16[2,64,256]{2,1,0:T(8,128)(2,1)S(1)}, bf16[2,64,256]{2,1,0:T(8,128)(2,1)S(1)}, u32[]{:S(2)}, u32[]{:S(2)}) %collective-permute-start.11) | collective-permute-done | bytes 65568 | tf_op jit(solution)/shard_map/ppermute | solution.py:302
  39.7 2.5 %collective-permute-start.19 = (bf16[2,64,256]{2,1,0:T(8,128)(2,1)S(1)}, bf16[2,64,256]{2,1,0:T(8,128)(2,1)S(1)}, u32[]{:S(2)}, u32[]{:S(2)}) collective-permute-start(bf16[2,64,256]{2,1,0:T(8,128)(2,1)S(1)} %add_sums.5.refs_3_), channel_id=1, source_target_pairs={{0,12},{4,8},{8,4},{12,0},{1,13},{5,9},{9,5},{13,1},{2,14},{6,10},... | collective-permute-start | bytes 196616 | tf_op jit(solution)/shard_map/ppermute | solution.py:302
  42.2 1.9 %collective-permute-start.17 = (bf16[2,64,256]{2,1,0:T(8,128)(2,1)S(1)}, bf16[2,64,256]{2,1,0:T(8,128)(2,1)S(1)}, u32[]{:S(2)}, u32[]{:S(2)}) collective-permute-start(bf16[2,64,256]{2,1,0:T(8,128)(2,1)S(1)} %add_sums.5.refs_3_), channel_id=1, source_target_pairs={{0,4},{4,0},{8,12},{12,8},{1,5},{5,1},{9,13},{13,9},{2,6},{6,2},{1... | collective-permute-start | bytes 196616 | tf_op jit(solution)/shard_map/ppermute | solution.py:302
  44.1 1.4 %finish.1 = (bf16[128,8192]{1,0:T(8,128)(2,1)}, f32[2,64,256]{2,1,0:T(8,128)}) custom-call(bf16[128,2048]{1,0:T(8,128)(2,1)S(1)} %get-tuple-element.64.refs_0_, bf16[128,2048]{1,0:T(8,128)(2,1)S(1)} %get-tuple-element.65.refs_1_, bf16[128,2048]{1,0:T(8,128)(2,1)S(1)} %get-tuple-element.66.refs_2_, bf16[128,2048]{1,0:T(8,128)(2,1)S(1)} %get-tuple-element.67.refs_3_, ...), custom_call_target="tpu_custom_call" | custom-call | flops 1073741824 | tf_op jit(solution)/shard_map/finish/pallas_call | solution.py:144
  45.5 1.0 %collective-permute-done.19.refs_6_ = bf16[2,64,256]{2,1,0:T(8,128)(2,1)S(1)} collective-permute-done((bf16[2,64,256]{2,1,0:T(8,128)(2,1)S(1)}, bf16[2,64,256]{2,1,0:T(8,128)(2,1)S(1)}, u32[]{:S(2)}, u32[]{:S(2)}) %collective-permute-start.19) | collective-permute-done | bytes 65568 | tf_op jit(solution)/shard_map/ppermute | solution.py:302
  46.5 2.3 %collective-permute-done.18.refs_5_ = bf16[2,64,256]{2,1,0:T(8,128)(2,1)S(1)} collective-permute-done((bf16[2,64,256]{2,1,0:T(8,128)(2,1)S(1)}, bf16[2,64,256]{2,1,0:T(8,128)(2,1)S(1)}, u32[]{:S(2)}, u32[]{:S(2)}) %collective-permute-start.18) | collective-permute-done | bytes 65568 | tf_op jit(solution)/shard_map/ppermute | solution.py:302
  48.8 2.3 %weight_grads.1 = f32[2,2048,256]{2,1,0:T(8,128)} custom-call(bf16[1,512,256]{2,1,0:T(8,128)(2,1)S(1)} %bitcast.10, bf16[1,512,256]{2,1,0:T(8,128)(2,1)S(1)} %collective-permute-done.15.refs_1_, bf16[2,512,256]{2,1,0:T(8,128)(2,1)S(1)} %collective-permute-done.16.refs_2_, bf16[2,64,256]{2,1,0:T(8,128)(2,1)S(1)} %add_sums.5.refs_3_, ...), custom_call_target="tpu_custom_call" | custom-call | flops 2147483648 | tf_op jit(solution)/shard_map/weight_grads/pallas_call | solution.py:267
  (44 shorter events, 0.4 us)
Async XLA Ops:
  0.6 1.0 %copy-start = (bf16[2,64,1024]{2,1,0:T(8,128)(2,1)S(1)}, bf16[2,64,1024]{2,1,0:T(8,128)(2,1)}, u32[]{:S(2)}) copy-start(bf16[2,64,1024]{2,1,0:T(8,128)(2,1)} %param.14) | copy-start | bytes 786436
  1.6 7.1 %copy-start.4 = (f32[128,64]{0,1:T(8,128)S(1)}, f32[128,64]{0,1:T(8,128)}, u32[]{:S(2)}) copy-start(f32[128,64]{0,1:T(8,128)} %param.12) | copy-start | bytes 98308
  1.6 7.1 %copy-start.5 = (f32[128,64]{0,1:T(8,128)S(1)}, f32[128,64]{0,1:T(8,128)}, u32[]{:S(2)}) copy-start(f32[128,64]{0,1:T(8,128)} %param.13) | copy-start | bytes 98308
  1.6 7.1 %copy-start.6 = (s32[4]{0:T(128)S(1)}, s32[4]{0:T(128)}, u32[]{:S(2)}) copy-start(s32[4]{0:T(128)} %ids.1) | copy-start | bytes 52
  1.6 7.1 %copy-start.7 = (s32[16]{0:T(128)S(1)}, s32[16]{0:T(128)}, u32[]{:S(2)}) copy-start(s32[16]{0:T(128)} %lengths.1) | copy-start | bytes 196
  1.6 7.1 %copy-start.8 = (f32[16]{0:T(128)S(1)}, f32[16]{0:T(128)}, u32[]{:S(2)}) copy-start(f32[16]{0:T(128)} %advantages.1) | copy-start | bytes 196
  1.6 7.1 %copy-start.9 = (s32[16]{0:T(128)S(1)}, s32[16]{0:T(128)}, u32[]{:S(2)}) copy-start(s32[16]{0:T(128)} %adv_index.1) | copy-start | bytes 196
  1.6 7.8 %collective-permute-start.1 = (bf16[2,64,256]{2,1,0:T(8,128)(2,1)S(1)}, bf16[2,64,256]{2,1,0:T(8,128)(2,1)S(1)}, u32[]{:S(2)}, u32[]{:S(2)}) collective-permute-start(bf16[2,64,256]{2,1,0:T(8,128)(2,1)S(1)} %constant_dynamic-slice_fusion), channel_id=1, source_target_pairs={{0,8},{4,12},{8,0},{12,4},{1,9},{5,13},{9,1},{13,5},{2,10},{6,14},... | collective-permute-start | bytes 196616 | tf_op jit(solution)/shard_map/ppermute | solution.py:302
  5.7 4.3 %collective-permute-start = (bf16[2,64,256]{2,1,0:T(8,128)(2,1)S(1)}, bf16[2,64,256]{2,1,0:T(8,128)(2,1)S(1)}, u32[]{:S(2)}, u32[]{:S(2)}) collective-permute-start(bf16[2,64,256]{2,1,0:T(8,128)(2,1)S(1)} %constant_dynamic-slice_fusion), channel_id=1, source_target_pairs={{0,4},{4,0},{8,12},{12,8},{1,5},{5,1},{9,13},{13,9},{2,6},{6,2},{1... | collective-permute-start | bytes 196616 | tf_op jit(solution)/shard_map/ppermute | solution.py:302
  7.3 6.1 %collective-permute-start.2 = (bf16[2,64,256]{2,1,0:T(8,128)(2,1)S(1)}, bf16[2,64,256]{2,1,0:T(8,128)(2,1)S(1)}, u32[]{:S(2)}, u32[]{:S(2)}) collective-permute-start(bf16[2,64,256]{2,1,0:T(8,128)(2,1)S(1)} %constant_dynamic-slice_fusion), channel_id=1, source_target_pairs={{0,12},{4,8},{8,4},{12,0},{1,13},{5,9},{9,5},{13,1},{2,14},{6,10},... | collective-permute-start | bytes 196616 | tf_op jit(solution)/shard_map/ppermute | solution.py:302
  7.3 1.2 %copy-start.3 = (bf16[64,8192]{1,0:T(8,128)(2,1)S(1)}, bf16[64,8192]{1,0:T(8,128)(2,1)}, u32[]{:S(2)}) copy-start(bf16[64,8192]{1,0:T(8,128)(2,1)} %x_ref.1) | copy-start | bytes 3145732
  8.7 4.8 %copy-start.1 = (bf16[128,8192]{1,0:T(8,128)(2,1)S(1)}, bf16[128,8192]{1,0:T(8,128)(2,1)}, u32[]{:S(2)}) copy-start(bf16[128,8192]{1,0:T(8,128)(2,1)} %q_ref.7) | copy-start | bytes 6291460
  8.7 4.8 %copy-start.2 = (bf16[128,8192]{1,0:T(8,128)(2,1)S(1)}, bf16[128,8192]{1,0:T(8,128)(2,1)}, u32[]{:S(2)}) copy-start(bf16[128,8192]{1,0:T(8,128)(2,1)} %ct_ref.7) | copy-start | bytes 6291460
  13.4 5.7 %collective-permute-start.3 = (bf16[4,2,64,256]{3,2,1,0:T(8,128)(2,1)S(1)}, bf16[4,2,64,256]{3,2,1,0:T(8,128)(2,1)S(1)}, u32[]{:S(2)}, u32[]{:S(2)}) collective-permute-start(bf16[4,2,64,256]{3,2,1,0:T(8,128)(2,1)S(1)} %pad_maximum_fusion.1.kv_ref), channel_id=1, source_target_pairs={{0,1},{1,0},{2,3},{3,2},{4,5},{5,4},{6,7},{7,6},{8,9},{9,8},{10,11... | collective-permute-start | bytes 786440 | tf_op jit(solution)/shard_map/ppermute | solution.py:305
  15.3 8.2 %collective-permute-start.4 = (bf16[4,2,64,256]{3,2,1,0:T(8,128)(2,1)S(1)}, bf16[4,2,64,256]{3,2,1,0:T(8,128)(2,1)S(1)}, u32[]{:S(2)}, u32[]{:S(2)}) collective-permute-start(bf16[4,2,64,256]{3,2,1,0:T(8,128)(2,1)S(1)} %get-tuple-element.53), channel_id=1, source_target_pairs={{0,1},{1,0},{2,3},{3,2},{4,5},{5,4},{6,7},{7,6},{8,9},{9,8},{10,11... | collective-permute-start | bytes 786440 | tf_op jit(solution)/shard_map/ppermute | solution.py:305
  15.9 8.3 %collective-permute-start.5 = (bf16[4,2,64,256]{3,2,1,0:T(8,128)(2,1)S(1)}, bf16[4,2,64,256]{3,2,1,0:T(8,128)(2,1)S(1)}, u32[]{:S(2)}, u32[]{:S(2)}) collective-permute-start(bf16[4,2,64,256]{3,2,1,0:T(8,128)(2,1)S(1)} %pad_maximum_fusion.1.kv_ref), channel_id=1, source_target_pairs={{0,2},{1,3},{2,0},{3,1},{4,6},{5,7},{6,4},{7,5},{8,10},{9,11},{10,... | collective-permute-start | bytes 786440 | tf_op jit(solution)/shard_map/ppermute | solution.py:305
  17.3 8.6 %collective-permute-start.12 = (bf16[64,512]{1,0:T(8,128)(2,1)S(1)}, bf16[64,512]{1,0:T(8,128)(2,1)S(1)}, u32[]{:S(2)}, u32[]{:S(2)}) collective-permute-start(bf16[64,512]{1,0:T(8,128)(2,1)S(1)} %get-tuple-element.72), channel_id=1, source_target_pairs={{0,4},{4,0},{8,12},{12,8},{1,5},{5,1},{9,13},{13,9},{2,6},{6,2},{1... | collective-permute-start | bytes 196616 | tf_op jit(solution)/shard_map/ppermute | solution.py:302
  17.3 9.2 %collective-permute-start.13 = (bf16[64,512]{1,0:T(8,128)(2,1)S(1)}, bf16[64,512]{1,0:T(8,128)(2,1)S(1)}, u32[]{:S(2)}, u32[]{:S(2)}) collective-permute-start(bf16[64,512]{1,0:T(8,128)(2,1)S(1)} %get-tuple-element.73), channel_id=1, source_target_pairs={{0,8},{4,12},{8,0},{12,4},{1,9},{5,13},{9,1},{13,5},{2,10},{6,14},... | collective-permute-start | bytes 196616 | tf_op jit(solution)/shard_map/ppermute | solution.py:302
  19.2 7.4 %collective-permute-start.14 = (bf16[64,512]{1,0:T(8,128)(2,1)S(1)}, bf16[64,512]{1,0:T(8,128)(2,1)S(1)}, u32[]{:S(2)}, u32[]{:S(2)}) collective-permute-start(bf16[64,512]{1,0:T(8,128)(2,1)S(1)} %get-tuple-element.74), channel_id=1, source_target_pairs={{0,12},{4,8},{8,4},{12,0},{1,13},{5,9},{9,5},{13,1},{2,14},{6,10},... | collective-permute-start | bytes 196616 | tf_op jit(solution)/shard_map/ppermute | solution.py:302
  23.6 7.2 %collective-permute-start.8 = (bf16[4,2,64,256]{3,2,1,0:T(8,128)(2,1)S(1)}, bf16[4,2,64,256]{3,2,1,0:T(8,128)(2,1)S(1)}, u32[]{:S(2)}, u32[]{:S(2)}) collective-permute-start(bf16[4,2,64,256]{3,2,1,0:T(8,128)(2,1)S(1)} %add_sums.3), channel_id=1, source_target_pairs={{0,2},{1,3},{2,0},{3,1},{4,6},{5,7},{6,4},{7,5},{8,10},{9,11},{10,... | collective-permute-start | bytes 786440 | tf_op jit(solution)/shard_map/ppermute | solution.py:305
  24.2 2.5 %collective-permute-start.6 = (bf16[4,2,64,256]{3,2,1,0:T(8,128)(2,1)S(1)}, bf16[4,2,64,256]{3,2,1,0:T(8,128)(2,1)S(1)}, u32[]{:S(2)}, u32[]{:S(2)}) collective-permute-start(bf16[4,2,64,256]{3,2,1,0:T(8,128)(2,1)S(1)} %collective-permute-done.5.kv_ref), channel_id=1, source_target_pairs={{0,1},{1,0},{2,3},{3,2},{4,5},{5,4},{6,7},{7,6},{8,9},{9,8},{10,11... | collective-permute-start | bytes 786440 | tf_op jit(solution)/shard_map/ppermute | solution.py:305
  26.0 4.8 %collective-permute-start.7 = (bf16[4,2,64,256]{3,2,1,0:T(8,128)(2,1)S(1)}, bf16[4,2,64,256]{3,2,1,0:T(8,128)(2,1)S(1)}, u32[]{:S(2)}, u32[]{:S(2)}) collective-permute-start(bf16[4,2,64,256]{3,2,1,0:T(8,128)(2,1)S(1)} %get-tuple-element.58), channel_id=1, source_target_pairs={{0,1},{1,0},{2,3},{3,2},{4,5},{5,4},{6,7},{7,6},{8,9},{9,8},{10,11... | collective-permute-start | bytes 786440 | tf_op jit(solution)/shard_map/ppermute | solution.py:305
  30.9 8.6 %collective-permute-start.15 = (bf16[1,512,256]{2,1,0:T(8,128)(2,1)S(1)}, bf16[1,512,256]{2,1,0:T(8,128)(2,1)S(1)}, u32[]{:S(2)}, u32[]{:S(2)}) collective-permute-start(bf16[1,512,256]{2,1,0:T(8,128)(2,1)S(1)} %bitcast.8), channel_id=1, source_target_pairs={{0,2},{1,3},{2,0},{3,1},{4,6},{5,7},{6,4},{7,5},{8,10},{9,11},{10,... | collective-permute-start | bytes 786440 | tf_op jit(solution)/shard_map/ppermute | solution.py:305
  31.5 4.4 %collective-permute-start.9 = (bf16[2,64,256]{2,1,0:T(8,128)(2,1)S(1)}, bf16[2,64,256]{2,1,0:T(8,128)(2,1)S(1)}, u32[]{:S(2)}, u32[]{:S(2)}) collective-permute-start(bf16[2,64,256]{2,1,0:T(8,128)(2,1)S(1)} %get-tuple-element.61), channel_id=1, source_target_pairs={{0,4},{4,0},{8,12},{12,8},{1,5},{5,1},{9,13},{13,9},{2,6},{6,2},{1... | collective-permute-start | bytes 196616 | tf_op jit(solution)/shard_map/ppermute | solution.py:302
  31.5 6.7 %collective-permute-start.10 = (bf16[2,64,256]{2,1,0:T(8,128)(2,1)S(1)}, bf16[2,64,256]{2,1,0:T(8,128)(2,1)S(1)}, u32[]{:S(2)}, u32[]{:S(2)}) collective-permute-start(bf16[2,64,256]{2,1,0:T(8,128)(2,1)S(1)} %get-tuple-element.62), channel_id=1, source_target_pairs={{0,8},{4,12},{8,0},{12,4},{1,9},{5,13},{9,1},{13,5},{2,10},{6,14},... | collective-permute-start | bytes 196616 | tf_op jit(solution)/shard_map/ppermute | solution.py:302
  33.3 6.2 %collective-permute-start.11 = (bf16[2,64,256]{2,1,0:T(8,128)(2,1)S(1)}, bf16[2,64,256]{2,1,0:T(8,128)(2,1)S(1)}, u32[]{:S(2)}, u32[]{:S(2)}) collective-permute-start(bf16[2,64,256]{2,1,0:T(8,128)(2,1)S(1)} %get-tuple-element.63), channel_id=1, source_target_pairs={{0,12},{4,8},{8,4},{12,0},{1,13},{5,9},{9,5},{13,1},{2,14},{6,10},... | collective-permute-start | bytes 196616 | tf_op jit(solution)/shard_map/ppermute | solution.py:302
  39.6 9.2 %collective-permute-start.16 = (bf16[2,512,256]{2,1,0:T(8,128)(2,1)S(1)}, bf16[2,512,256]{2,1,0:T(8,128)(2,1)S(1)}, u32[]{:S(2)}, u32[]{:S(2)}) collective-permute-start(bf16[2,512,256]{2,1,0:T(8,128)(2,1)S(1)} %pad_maximum_fusion), channel_id=1, source_target_pairs={{0,1},{1,0},{2,3},{3,2},{4,5},{5,4},{6,7},{7,6},{8,9},{9,8},{10,11... | collective-permute-start | bytes 1572872 | tf_op jit(solution)/shard_map/ppermute | solution.py:305
  39.7 6.8 %collective-permute-start.19 = (bf16[2,64,256]{2,1,0:T(8,128)(2,1)S(1)}, bf16[2,64,256]{2,1,0:T(8,128)(2,1)S(1)}, u32[]{:S(2)}, u32[]{:S(2)}) collective-permute-start(bf16[2,64,256]{2,1,0:T(8,128)(2,1)S(1)} %add_sums.5.refs_3_), channel_id=1, source_target_pairs={{0,12},{4,8},{8,4},{12,0},{1,13},{5,9},{9,5},{13,1},{2,14},{6,10},... | collective-permute-start | bytes 196616 | tf_op jit(solution)/shard_map/ppermute | solution.py:302
  42.2 6.6 %collective-permute-start.18 = (bf16[2,64,256]{2,1,0:T(8,128)(2,1)S(1)}, bf16[2,64,256]{2,1,0:T(8,128)(2,1)S(1)}, u32[]{:S(2)}, u32[]{:S(2)}) collective-permute-start(bf16[2,64,256]{2,1,0:T(8,128)(2,1)S(1)} %add_sums.5.refs_3_), channel_id=1, source_target_pairs={{0,8},{4,12},{8,0},{12,4},{1,9},{5,13},{9,1},{13,5},{2,10},{6,14},... | collective-permute-start | bytes 196616 | tf_op jit(solution)/shard_map/ppermute | solution.py:302
  42.2 6.6 %collective-permute-start.17 = (bf16[2,64,256]{2,1,0:T(8,128)(2,1)S(1)}, bf16[2,64,256]{2,1,0:T(8,128)(2,1)S(1)}, u32[]{:S(2)}, u32[]{:S(2)}) collective-permute-start(bf16[2,64,256]{2,1,0:T(8,128)(2,1)S(1)} %add_sums.5.refs_3_), channel_id=1, source_target_pairs={{0,4},{4,0},{8,12},{12,8},{1,5},{5,1},{9,13},{13,9},{2,6},{6,2},{1... | collective-permute-start | bytes 196616 | tf_op jit(solution)/shard_map/ppermute | solution.py:302

commit v4 on v3

--- a/solution.py
+++ b/solution.py
@@ -106,7 +106,7 @@
         ],
         compiler_params=pltpu.CompilerParams(vmem_limit_bytes=16 * MIB + slab * 32 * 1024),
         cost_estimate=pl.CostEstimate(
-            flops=30 * tokens * per_kv * slab * cols, bytes_accessed=0, transcendentals=0
+            flops=80 * tokens * per_kv * slab * cols, bytes_accessed=0, transcendentals=0
         ),
         name="head_block",
     )(queries, cotangent, weights, offset, delta, kv)

time: 51.3 us -> 50.7 us (0.988)
  waiting for transfers between devices: 13.2 us -> 11.8 us
  starting transfers between devices: 22.9 us -> 23.6 us
    ppermute x12, waiting for transfers between devices: 10.8 us -> 8.44 us  [to_ctx(): return lax.ppermute(x, 'ctx', xor_pairs(ctx_count, offset))]
    ppermute x8, waiting for transfers between devices: 2.36 us -> 3.35 us  [to_roll(): return lax.ppermute(x, 'roll', xor_pairs(roll_count, offset))]
    ppermute x8, starting transfers between devices: 3.95 us -> 4.59 us  [to_roll(): return lax.ppermute(x, 'roll', xor_pairs(roll_count, offset))]
  transfers between devices with their start and end apart: 20 -> 20, of which waited for: 7 -> 8; matrix products, arithmetic and copies ran while one was open for 0% -> 0% of each run, Pallas kernels for 18% -> 19%
where the time goes in v4:
time: 50.7 us; the launch traced here: 50.5 us
  starting transfers between devices  23.6 us (47%)
  Pallas kernels  11.9 us (23%)
  waiting for transfers between devices  11.8 us (23%)
  local copies, waits for them, and re-layouts  2.23 us (4%)
  between operations  0.91 us (2%)
    ppermute x12, starting transfers between devices, to_ctx(): return lax.ppermute(x, 'ctx', xor_pairs(ctx_count, offset))  19 us
    ppermute x12, waiting for transfers between devices, to_ctx(): return lax.ppermute(x, 'ctx', xor_pairs(ctx_count, offset))  8.44 us
    pallas_call x4, Pallas kernels, head_block(): pl.pallas_call(functools.partial(heads_kernel, per_kv, off), in_specs=[WH...  7.09 us
    ppermute x8, starting transfers between devices, to_roll(): return lax.ppermute(x, 'roll', xor_pairs(roll_count, offset))  4.59 us
    ppermute x8, waiting for transfers between devices, to_roll(): return lax.ppermute(x, 'roll', xor_pairs(roll_count, offset))  3.35 us
    pallas_call x1, Pallas kernels, weight_grads(): pl.pallas_call(kernel, in_specs=[WHOLE] * (len(shares) + len(low)), out_s...  2.34 us
    unnamed x20, local copies, waits for them, and re-layouts  2.2 us
    pallas_call x1, Pallas kernels, finish(): pl.pallas_call(kernel, in_specs=[anywhere] * count + [WHOLE] * (1 + len(r...  1.4 us
  transfers between devices with their start and end apart: 20, of which 8 were waited for; matrix products, arithmetic and copies ran while one was open for 0% of the time, Pallas kernels for 19%

profile of v4, /device:TPU:0, one launch (start us, length us, event | category | flops | bytes accessed | tf_op | source)
XLA Modules:
  0.0 50.5 jit_solution(15486916619605363888)
XLA Ops:
  0.7 0.9 %copy-done = bf16[2,64,1024]{2,1,0:T(8,128)(2,1)S(1)} copy-done((bf16[2,64,1024]{2,1,0:T(8,128)(2,1)S(1)}, bf16[2,64,1024]{2,1,0:T(8,128)(2,1)}, u32[]{:S(2)}) %copy-start) | copy-done | bytes 262168
  1.6 4.1 %collective-permute-start.1 = (bf16[2,64,256]{2,1,0:T(8,128)(2,1)S(1)}, bf16[2,64,256]{2,1,0:T(8,128)(2,1)S(1)}, u32[]{:S(2)}, u32[]{:S(2)}) collective-permute-start(bf16[2,64,256]{2,1,0:T(8,128)(2,1)S(1)} %constant_dynamic-slice_fusion), channel_id=1, source_target_pairs={{0,8},{4,12},{8,0},{12,4},{1,9},{5,13},{9,1},{13,5},{2,10},{6,14},... | collective-permute-start | bytes 196616 | tf_op jit(solution)/shard_map/ppermute | solution.py:302
  5.7 1.6 %collective-permute-start = (bf16[2,64,256]{2,1,0:T(8,128)(2,1)S(1)}, bf16[2,64,256]{2,1,0:T(8,128)(2,1)S(1)}, u32[]{:S(2)}, u32[]{:S(2)}) collective-permute-start(bf16[2,64,256]{2,1,0:T(8,128)(2,1)S(1)} %constant_dynamic-slice_fusion), channel_id=1, source_target_pairs={{0,4},{4,0},{8,12},{12,8},{1,5},{5,1},{9,13},{13,9},{2,6},{6,2},{1... | collective-permute-start | bytes 196616 | tf_op jit(solution)/shard_map/ppermute | solution.py:302
  7.3 1.2 %copy-done.3 = bf16[64,8192]{1,0:T(8,128)(2,1)S(1)} copy-done((bf16[64,8192]{1,0:T(8,128)(2,1)S(1)}, bf16[64,8192]{1,0:T(8,128)(2,1)}, u32[]{:S(2)}) %copy-start.3) | copy-done | bytes 1048600
  8.6 0.1 cut_hidden.1
  8.6 1.0 %collective-permute-start.12 = (bf16[64,512]{1,0:T(8,128)(2,1)S(1)}, bf16[64,512]{1,0:T(8,128)(2,1)S(1)}, u32[]{:S(2)}, u32[]{:S(2)}) collective-permute-start(bf16[64,512]{1,0:T(8,128)(2,1)S(1)} %get-tuple-element.72), channel_id=1, source_target_pairs={{0,4},{4,0},{8,12},{12,8},{1,5},{5,1},{9,13},{13,9},{2,6},{6,2},{1... | collective-permute-start | bytes 196616 | tf_op jit(solution)/shard_map/ppermute | solution.py:302
  9.6 3.5 %collective-permute-start.13 = (bf16[64,512]{1,0:T(8,128)(2,1)S(1)}, bf16[64,512]{1,0:T(8,128)(2,1)S(1)}, u32[]{:S(2)}, u32[]{:S(2)}) collective-permute-start(bf16[64,512]{1,0:T(8,128)(2,1)S(1)} %get-tuple-element.73), channel_id=1, source_target_pairs={{0,8},{4,12},{8,0},{12,4},{1,9},{5,13},{9,1},{13,5},{2,10},{6,14},... | collective-permute-start | bytes 196616 | tf_op jit(solution)/shard_map/ppermute | solution.py:302
  13.2 0.7 %prep.1 = (f32[128,128]{1,0:T(8,128)S(1)}, f32[64,128]{1,0:T(8,128)S(1)}, f32[64,128]{1,0:T(8,128)S(1)}) custom-call(s32[4]{0:T(128)S(1)} %copy-done.6, s32[16]{0:T(128)S(1)} %copy-done.7, f32[16]{0:T(128)S(1)} %copy-done.8, s32[16]{0:T(128)S(1)} %copy-done.9, f32[64,128]{1,0:T(8,128)S(1)} %bitcast.11, f32[64,128]{1,0:T(8,128)S(1)} %bitcast.12), custom_call_target="tpu_custom_call" | custom-call | flops 1073741824 | tf_op jit(solution)/shard_map/prep/pallas_call | solution.py:46
  14.0 0.2 collective-permute-done.2
  14.2 1.6 %collective-permute-start.5 = (bf16[4,2,64,256]{3,2,1,0:T(8,128)(2,1)S(1)}, bf16[4,2,64,256]{3,2,1,0:T(8,128)(2,1)S(1)}, u32[]{:S(2)}, u32[]{:S(2)}) collective-permute-start(bf16[4,2,64,256]{3,2,1,0:T(8,128)(2,1)S(1)} %pad_maximum_fusion.1.kv_ref), channel_id=1, source_target_pairs={{0,2},{1,3},{2,0},{3,1},{4,6},{5,7},{6,4},{7,5},{8,10},{9,11},{10,... | collective-permute-start | bytes 786440 | tf_op jit(solution)/shard_map/ppermute | solution.py:305
  15.8 1.8 %head_block.4 = (bf16[128,2048]{1,0:T(8,128)(2,1)S(1)}, bf16[4,2,64,256]{3,2,1,0:T(8,128)(2,1)S(1)}) custom-call(bf16[128,8192]{1,0:T(8,128)(2,1)S(1)} %copy-done.1, bf16[128,8192]{1,0:T(8,128)(2,1)S(1)} %copy-done.2, f32[128,128]{1,0:T(8,128)S(1)} %get-tuple-element.47.w_ref, f32[64,128]{1,0:T(8,128)S(1)} %get-tuple-element.48.o_ref, ...), custom_call_target="tpu_custom_call" | custom-call | flops 5368709120 | tf_op jit(solution)/shard_map/head_block/pallas_call | solution.py:99
  17.6 0.6 %collective-permute-start.4 = (bf16[4,2,64,256]{3,2,1,0:T(8,128)(2,1)S(1)}, bf16[4,2,64,256]{3,2,1,0:T(8,128)(2,1)S(1)}, u32[]{:S(2)}, u32[]{:S(2)}) collective-permute-start(bf16[4,2,64,256]{3,2,1,0:T(8,128)(2,1)S(1)} %get-tuple-element.53), channel_id=1, source_target_pairs={{0,1},{1,0},{2,3},{3,2},{4,5},{5,4},{6,7},{7,6},{8,9},{9,8},{10,11... | collective-permute-start | bytes 786440 | tf_op jit(solution)/shard_map/ppermute | solution.py:305
  18.2 1.8 %head_block.5 = (bf16[128,2048]{1,0:T(8,128)(2,1)S(1)}, f32[4,2,64,256]{3,2,1,0:T(8,128)S(1)}) custom-call(bf16[128,8192]{1,0:T(8,128)(2,1)S(1)} %copy-done.1, bf16[128,8192]{1,0:T(8,128)(2,1)S(1)} %copy-done.2, f32[128,128]{1,0:T(8,128)S(1)} %get-tuple-element.47.w_ref, f32[64,128]{1,0:T(8,128)S(1)} %get-tuple-element.48.o_ref, ...), custom_call_target="tpu_custom_call" | custom-call | flops 5368709120 | tf_op jit(solution)/shard_map/head_block/pallas_call | solution.py:99
  20.0 0.7 %collective-permute-start.8 = (bf16[4,2,64,256]{3,2,1,0:T(8,128)(2,1)S(1)}, bf16[4,2,64,256]{3,2,1,0:T(8,128)(2,1)S(1)}, u32[]{:S(2)}, u32[]{:S(2)}) collective-permute-start(bf16[4,2,64,256]{3,2,1,0:T(8,128)(2,1)S(1)} %add_sums.3), channel_id=1, source_target_pairs={{0,2},{1,3},{2,0},{3,1},{4,6},{5,7},{6,4},{7,5},{8,10},{9,11},{10,... | collective-permute-start | bytes 786440 | tf_op jit(solution)/shard_map/ppermute | solution.py:305
  20.7 0.2 collective-permute-start.6
  20.9 1.8 %head_block.6 = (bf16[128,2048]{1,0:T(8,128)(2,1)S(1)}, bf16[4,2,64,256]{3,2,1,0:T(8,128)(2,1)S(1)}) custom-call(bf16[128,8192]{1,0:T(8,128)(2,1)S(1)} %copy-done.1, bf16[128,8192]{1,0:T(8,128)(2,1)S(1)} %copy-done.2, f32[128,128]{1,0:T(8,128)S(1)} %get-tuple-element.47.w_ref, f32[64,128]{1,0:T(8,128)S(1)} %get-tuple-element.48.o_ref, ...), custom_call_target="tpu_custom_call" | custom-call | flops 5368709120 | tf_op jit(solution)/shard_map/head_block/pallas_call | solution.py:99
  22.7 0.4 collective-permute-start.7
  23.1 0.1 turn_hidden.1
  23.2 1.8 %head_block.7 = (bf16[128,2048]{1,0:T(8,128)(2,1)S(1)}, f32[4,2,64,256]{3,2,1,0:T(8,128)S(1)}) custom-call(bf16[128,8192]{1,0:T(8,128)(2,1)S(1)} %copy-done.1, bf16[128,8192]{1,0:T(8,128)(2,1)S(1)} %copy-done.2, f32[128,128]{1,0:T(8,128)S(1)} %get-tuple-element.47.w_ref, f32[64,128]{1,0:T(8,128)S(1)} %get-tuple-element.48.o_ref, ...), custom_call_target="tpu_custom_call" | custom-call | flops 5368709120 | tf_op jit(solution)/shard_map/head_block/pallas_call | solution.py:99
  25.0 3.3 %collective-permute-done.8.refs_1_ = bf16[4,2,64,256]{3,2,1,0:T(8,128)(2,1)S(1)} collective-permute-done((bf16[4,2,64,256]{3,2,1,0:T(8,128)(2,1)S(1)}, bf16[4,2,64,256]{3,2,1,0:T(8,128)(2,1)S(1)}, u32[]{:S(2)}, u32[]{:S(2)}) %collective-permute-start.8) | collective-permute-done | bytes 262176 | tf_op jit(solution)/shard_map/ppermute | solution.py:305
  28.4 1.1 %collective-permute-start.15 = (bf16[1,512,256]{2,1,0:T(8,128)(2,1)S(1)}, bf16[1,512,256]{2,1,0:T(8,128)(2,1)S(1)}, u32[]{:S(2)}, u32[]{:S(2)}) collective-permute-start(bf16[1,512,256]{2,1,0:T(8,128)(2,1)S(1)} %bitcast.8), channel_id=1, source_target_pairs={{0,2},{1,3},{2,0},{3,1},{4,6},{5,7},{6,4},{7,5},{8,10},{9,11},{10,... | collective-permute-start | bytes 786440 | tf_op jit(solution)/shard_map/ppermute | solution.py:305
  29.6 3.5 %collective-permute-start.10 = (bf16[2,64,256]{2,1,0:T(8,128)(2,1)S(1)}, bf16[2,64,256]{2,1,0:T(8,128)(2,1)S(1)}, u32[]{:S(2)}, u32[]{:S(2)}) collective-permute-start(bf16[2,64,256]{2,1,0:T(8,128)(2,1)S(1)} %get-tuple-element.62), channel_id=1, source_target_pairs={{0,8},{4,12},{8,0},{12,4},{1,9},{5,13},{9,1},{13,5},{2,10},{6,14},... | collective-permute-start | bytes 196616 | tf_op jit(solution)/shard_map/ppermute | solution.py:302
  33.1 0.8 %collective-permute-start.11 = (bf16[2,64,256]{2,1,0:T(8,128)(2,1)S(1)}, bf16[2,64,256]{2,1,0:T(8,128)(2,1)S(1)}, u32[]{:S(2)}, u32[]{:S(2)}) collective-permute-start(bf16[2,64,256]{2,1,0:T(8,128)(2,1)S(1)} %get-tuple-element.63), channel_id=1, source_target_pairs={{0,12},{4,8},{8,4},{12,0},{1,13},{5,9},{9,5},{13,1},{2,14},{6,10},... | collective-permute-start | bytes 196616 | tf_op jit(solution)/shard_map/ppermute | solution.py:302
  33.9 0.1 collective-permute-done.9.refs_0_.refs_5_
  34.0 3.1 %collective-permute-done.10.refs_1_.refs_6_ = bf16[2,64,256]{2,1,0:T(8,128)(2,1)S(1)} collective-permute-done((bf16[2,64,256]{2,1,0:T(8,128)(2,1)S(1)}, bf16[2,64,256]{2,1,0:T(8,128)(2,1)S(1)}, u32[]{:S(2)}, u32[]{:S(2)}) %collective-permute-start.10) | collective-permute-done | bytes 65568 | tf_op jit(solution)/shard_map/ppermute | solution.py:302
  37.1 2.0 %collective-permute-done.11.refs_2_.refs_7_ = bf16[2,64,256]{2,1,0:T(8,128)(2,1)S(1)} collective-permute-done((bf16[2,64,256]{2,1,0:T(8,128)(2,1)S(1)}, bf16[2,64,256]{2,1,0:T(8,128)(2,1)S(1)}, u32[]{:S(2)}, u32[]{:S(2)}) %collective-permute-start.11) | collective-permute-done | bytes 65568 | tf_op jit(solution)/shard_map/ppermute | solution.py:302
  39.4 0.9 %collective-permute-start.19 = (bf16[2,64,256]{2,1,0:T(8,128)(2,1)S(1)}, bf16[2,64,256]{2,1,0:T(8,128)(2,1)S(1)}, u32[]{:S(2)}, u32[]{:S(2)}) collective-permute-start(bf16[2,64,256]{2,1,0:T(8,128)(2,1)S(1)} %add_sums.5.refs_3_), channel_id=1, source_target_pairs={{0,12},{4,8},{8,4},{12,0},{1,13},{5,9},{9,5},{13,1},{2,14},{6,10},... | collective-permute-start | bytes 196616 | tf_op jit(solution)/shard_map/ppermute | solution.py:302
  40.3 3.5 %collective-permute-start.17 = (bf16[2,64,256]{2,1,0:T(8,128)(2,1)S(1)}, bf16[2,64,256]{2,1,0:T(8,128)(2,1)S(1)}, u32[]{:S(2)}, u32[]{:S(2)}) collective-permute-start(bf16[2,64,256]{2,1,0:T(8,128)(2,1)S(1)} %add_sums.5.refs_3_), channel_id=1, source_target_pairs={{0,4},{4,0},{8,12},{12,8},{1,5},{5,1},{9,13},{13,9},{2,6},{6,2},{1... | collective-permute-start | bytes 196616 | tf_op jit(solution)/shard_map/ppermute | solution.py:302
  43.8 1.4 %finish.1 = (bf16[128,8192]{1,0:T(8,128)(2,1)}, f32[2,64,256]{2,1,0:T(8,128)}) custom-call(bf16[128,2048]{1,0:T(8,128)(2,1)S(1)} %get-tuple-element.64.refs_0_, bf16[128,2048]{1,0:T(8,128)(2,1)S(1)} %get-tuple-element.65.refs_1_, bf16[128,2048]{1,0:T(8,128)(2,1)S(1)} %get-tuple-element.66.refs_2_, bf16[128,2048]{1,0:T(8,128)(2,1)S(1)} %get-tuple-element.67.refs_3_, ...), custom_call_target="tpu_custom_call" | custom-call | flops 1073741824 | tf_op jit(solution)/shard_map/finish/pallas_call | solution.py:144
  45.2 1.0 %collective-permute-done.19.refs_6_ = bf16[2,64,256]{2,1,0:T(8,128)(2,1)S(1)} collective-permute-done((bf16[2,64,256]{2,1,0:T(8,128)(2,1)S(1)}, bf16[2,64,256]{2,1,0:T(8,128)(2,1)S(1)}, u32[]{:S(2)}, u32[]{:S(2)}) %collective-permute-start.19) | collective-permute-done | bytes 65568 | tf_op jit(solution)/shard_map/ppermute | solution.py:302
  46.2 1.9 %collective-permute-done.18.refs_5_ = bf16[2,64,256]{2,1,0:T(8,128)(2,1)S(1)} collective-permute-done((bf16[2,64,256]{2,1,0:T(8,128)(2,1)S(1)}, bf16[2,64,256]{2,1,0:T(8,128)(2,1)S(1)}, u32[]{:S(2)}, u32[]{:S(2)}) %collective-permute-start.18) | collective-permute-done | bytes 65568 | tf_op jit(solution)/shard_map/ppermute | solution.py:302
  48.2 2.3 %weight_grads.1 = f32[2,2048,256]{2,1,0:T(8,128)} custom-call(bf16[1,512,256]{2,1,0:T(8,128)(2,1)S(1)} %bitcast.10, bf16[1,512,256]{2,1,0:T(8,128)(2,1)S(1)} %collective-permute-done.15.refs_1_, bf16[2,512,256]{2,1,0:T(8,128)(2,1)S(1)} %collective-permute-done.16.refs_2_, bf16[2,64,256]{2,1,0:T(8,128)(2,1)S(1)} %add_sums.5.refs_3_, ...), custom_call_target="tpu_custom_call" | custom-call | flops 2147483648 | tf_op jit(solution)/shard_map/weight_grads/pallas_call | solution.py:267
  (44 shorter events, 0.6 us)
Async XLA Ops:
  0.6 1.0 %copy-start = (bf16[2,64,1024]{2,1,0:T(8,128)(2,1)S(1)}, bf16[2,64,1024]{2,1,0:T(8,128)(2,1)}, u32[]{:S(2)}) copy-start(bf16[2,64,1024]{2,1,0:T(8,128)(2,1)} %param.14) | copy-start | bytes 786436
  1.6 11.5 %copy-start.4 = (f32[128,64]{0,1:T(8,128)S(1)}, f32[128,64]{0,1:T(8,128)}, u32[]{:S(2)}) copy-start(f32[128,64]{0,1:T(8,128)} %param.12) | copy-start | bytes 98308
  1.6 11.5 %copy-start.5 = (f32[128,64]{0,1:T(8,128)S(1)}, f32[128,64]{0,1:T(8,128)}, u32[]{:S(2)}) copy-start(f32[128,64]{0,1:T(8,128)} %param.13) | copy-start | bytes 98308
  1.6 11.5 %copy-start.6 = (s32[4]{0:T(128)S(1)}, s32[4]{0:T(128)}, u32[]{:S(2)}) copy-start(s32[4]{0:T(128)} %ids.1) | copy-start | bytes 52
  1.6 11.5 %copy-start.7 = (s32[16]{0:T(128)S(1)}, s32[16]{0:T(128)}, u32[]{:S(2)}) copy-start(s32[16]{0:T(128)} %lengths.1) | copy-start | bytes 196
  1.6 11.6 %copy-start.8 = (f32[16]{0:T(128)S(1)}, f32[16]{0:T(128)}, u32[]{:S(2)}) copy-start(f32[16]{0:T(128)} %advantages.1) | copy-start | bytes 196
  1.6 11.6 %copy-start.9 = (s32[16]{0:T(128)S(1)}, s32[16]{0:T(128)}, u32[]{:S(2)}) copy-start(s32[16]{0:T(128)} %adv_index.1) | copy-start | bytes 196
  1.6 12.2 %collective-permute-start.1 = (bf16[2,64,256]{2,1,0:T(8,128)(2,1)S(1)}, bf16[2,64,256]{2,1,0:T(8,128)(2,1)S(1)}, u32[]{:S(2)}, u32[]{:S(2)}) collective-permute-start(bf16[2,64,256]{2,1,0:T(8,128)(2,1)S(1)} %constant_dynamic-slice_fusion), channel_id=1, source_target_pairs={{0,8},{4,12},{8,0},{12,4},{1,9},{5,13},{9,1},{13,5},{2,10},{6,14},... | collective-permute-start | bytes 196616 | tf_op jit(solution)/shard_map/ppermute | solution.py:302
  5.7 8.2 %collective-permute-start = (bf16[2,64,256]{2,1,0:T(8,128)(2,1)S(1)}, bf16[2,64,256]{2,1,0:T(8,128)(2,1)S(1)}, u32[]{:S(2)}, u32[]{:S(2)}) collective-permute-start(bf16[2,64,256]{2,1,0:T(8,128)(2,1)S(1)} %constant_dynamic-slice_fusion), channel_id=1, source_target_pairs={{0,4},{4,0},{8,12},{12,8},{1,5},{5,1},{9,13},{13,9},{2,6},{6,2},{1... | collective-permute-start | bytes 196616 | tf_op jit(solution)/shard_map/ppermute | solution.py:302
  7.3 6.9 %collective-permute-start.2 = (bf16[2,64,256]{2,1,0:T(8,128)(2,1)S(1)}, bf16[2,64,256]{2,1,0:T(8,128)(2,1)S(1)}, u32[]{:S(2)}, u32[]{:S(2)}) collective-permute-start(bf16[2,64,256]{2,1,0:T(8,128)(2,1)S(1)} %constant_dynamic-slice_fusion), channel_id=1, source_target_pairs={{0,12},{4,8},{8,4},{12,0},{1,13},{5,9},{9,5},{13,1},{2,14},{6,10},... | collective-permute-start | bytes 196616 | tf_op jit(solution)/shard_map/ppermute | solution.py:302
  7.3 1.2 %copy-start.3 = (bf16[64,8192]{1,0:T(8,128)(2,1)S(1)}, bf16[64,8192]{1,0:T(8,128)(2,1)}, u32[]{:S(2)}) copy-start(bf16[64,8192]{1,0:T(8,128)(2,1)} %x_ref.1) | copy-start | bytes 3145732
  8.6 14.0 %collective-permute-start.12 = (bf16[64,512]{1,0:T(8,128)(2,1)S(1)}, bf16[64,512]{1,0:T(8,128)(2,1)S(1)}, u32[]{:S(2)}, u32[]{:S(2)}) collective-permute-start(bf16[64,512]{1,0:T(8,128)(2,1)S(1)} %get-tuple-element.72), channel_id=1, source_target_pairs={{0,4},{4,0},{8,12},{12,8},{1,5},{5,1},{9,13},{13,9},{2,6},{6,2},{1... | collective-permute-start | bytes 196616 | tf_op jit(solution)/shard_map/ppermute | solution.py:302
  9.6 13.5 %collective-permute-start.13 = (bf16[64,512]{1,0:T(8,128)(2,1)S(1)}, bf16[64,512]{1,0:T(8,128)(2,1)S(1)}, u32[]{:S(2)}, u32[]{:S(2)}) collective-permute-start(bf16[64,512]{1,0:T(8,128)(2,1)S(1)} %get-tuple-element.73), channel_id=1, source_target_pairs={{0,8},{4,12},{8,0},{12,4},{1,9},{5,13},{9,1},{13,5},{2,10},{6,14},... | collective-permute-start | bytes 196616 | tf_op jit(solution)/shard_map/ppermute | solution.py:302
  13.2 2.6 %copy-start.1 = (bf16[128,8192]{1,0:T(8,128)(2,1)S(1)}, bf16[128,8192]{1,0:T(8,128)(2,1)}, u32[]{:S(2)}) copy-start(bf16[128,8192]{1,0:T(8,128)(2,1)} %q_ref.7) | copy-start | bytes 6291460
  13.2 2.6 %copy-start.2 = (bf16[128,8192]{1,0:T(8,128)(2,1)S(1)}, bf16[128,8192]{1,0:T(8,128)(2,1)}, u32[]{:S(2)}) copy-start(bf16[128,8192]{1,0:T(8,128)(2,1)} %ct_ref.7) | copy-start | bytes 6291460
  13.9 9.2 %collective-permute-start.14 = (bf16[64,512]{1,0:T(8,128)(2,1)S(1)}, bf16[64,512]{1,0:T(8,128)(2,1)S(1)}, u32[]{:S(2)}, u32[]{:S(2)}) collective-permute-start(bf16[64,512]{1,0:T(8,128)(2,1)S(1)} %get-tuple-element.74), channel_id=1, source_target_pairs={{0,12},{4,8},{8,4},{12,0},{1,13},{5,9},{9,5},{13,1},{2,14},{6,10},... | collective-permute-start | bytes 196616 | tf_op jit(solution)/shard_map/ppermute | solution.py:302
  14.2 6.5 %collective-permute-start.5 = (bf16[4,2,64,256]{3,2,1,0:T(8,128)(2,1)S(1)}, bf16[4,2,64,256]{3,2,1,0:T(8,128)(2,1)S(1)}, u32[]{:S(2)}, u32[]{:S(2)}) collective-permute-start(bf16[4,2,64,256]{3,2,1,0:T(8,128)(2,1)S(1)} %pad_maximum_fusion.1.kv_ref), channel_id=1, source_target_pairs={{0,2},{1,3},{2,0},{3,1},{4,6},{5,7},{6,4},{7,5},{8,10},{9,11},{10,... | collective-permute-start | bytes 786440 | tf_op jit(solution)/shard_map/ppermute | solution.py:305
  15.8 1.8 %collective-permute-start.3 = (bf16[4,2,64,256]{3,2,1,0:T(8,128)(2,1)S(1)}, bf16[4,2,64,256]{3,2,1,0:T(8,128)(2,1)S(1)}, u32[]{:S(2)}, u32[]{:S(2)}) collective-permute-start(bf16[4,2,64,256]{3,2,1,0:T(8,128)(2,1)S(1)} %pad_maximum_fusion.1.kv_ref), channel_id=1, source_target_pairs={{0,1},{1,0},{2,3},{3,2},{4,5},{5,4},{6,7},{7,6},{8,9},{9,8},{10,11... | collective-permute-start | bytes 786440 | tf_op jit(solution)/shard_map/ppermute | solution.py:305
  17.6 2.3 %collective-permute-start.4 = (bf16[4,2,64,256]{3,2,1,0:T(8,128)(2,1)S(1)}, bf16[4,2,64,256]{3,2,1,0:T(8,128)(2,1)S(1)}, u32[]{:S(2)}, u32[]{:S(2)}) collective-permute-start(bf16[4,2,64,256]{3,2,1,0:T(8,128)(2,1)S(1)} %get-tuple-element.53), channel_id=1, source_target_pairs={{0,1},{1,0},{2,3},{3,2},{4,5},{5,4},{6,7},{7,6},{8,9},{9,8},{10,11... | collective-permute-start | bytes 786440 | tf_op jit(solution)/shard_map/ppermute | solution.py:305
  20.0 8.3 %collective-permute-start.8 = (bf16[4,2,64,256]{3,2,1,0:T(8,128)(2,1)S(1)}, bf16[4,2,64,256]{3,2,1,0:T(8,128)(2,1)S(1)}, u32[]{:S(2)}, u32[]{:S(2)}) collective-permute-start(bf16[4,2,64,256]{3,2,1,0:T(8,128)(2,1)S(1)} %add_sums.3), channel_id=1, source_target_pairs={{0,2},{1,3},{2,0},{3,1},{4,6},{5,7},{6,4},{7,5},{8,10},{9,11},{10,... | collective-permute-start | bytes 786440 | tf_op jit(solution)/shard_map/ppermute | solution.py:305
  20.7 2.5 %collective-permute-start.6 = (bf16[4,2,64,256]{3,2,1,0:T(8,128)(2,1)S(1)}, bf16[4,2,64,256]{3,2,1,0:T(8,128)(2,1)S(1)}, u32[]{:S(2)}, u32[]{:S(2)}) collective-permute-start(bf16[4,2,64,256]{3,2,1,0:T(8,128)(2,1)S(1)} %collective-permute-done.5.kv_ref), channel_id=1, source_target_pairs={{0,1},{1,0},{2,3},{3,2},{4,5},{5,4},{6,7},{7,6},{8,9},{9,8},{10,11... | collective-permute-start | bytes 786440 | tf_op jit(solution)/shard_map/ppermute | solution.py:305
  22.7 5.6 %collective-permute-start.7 = (bf16[4,2,64,256]{3,2,1,0:T(8,128)(2,1)S(1)}, bf16[4,2,64,256]{3,2,1,0:T(8,128)(2,1)S(1)}, u32[]{:S(2)}, u32[]{:S(2)}) collective-permute-start(bf16[4,2,64,256]{3,2,1,0:T(8,128)(2,1)S(1)} %get-tuple-element.58), channel_id=1, source_target_pairs={{0,1},{1,0},{2,3},{3,2},{4,5},{5,4},{6,7},{7,6},{8,9},{9,8},{10,11... | collective-permute-start | bytes 786440 | tf_op jit(solution)/shard_map/ppermute | solution.py:305
  28.4 10.8 %collective-permute-start.15 = (bf16[1,512,256]{2,1,0:T(8,128)(2,1)S(1)}, bf16[1,512,256]{2,1,0:T(8,128)(2,1)S(1)}, u32[]{:S(2)}, u32[]{:S(2)}) collective-permute-start(bf16[1,512,256]{2,1,0:T(8,128)(2,1)S(1)} %bitcast.8), channel_id=1, source_target_pairs={{0,2},{1,3},{2,0},{3,1},{4,6},{5,7},{6,4},{7,5},{8,10},{9,11},{10,... | collective-permute-start | bytes 786440 | tf_op jit(solution)/shard_map/ppermute | solution.py:305
  29.5 4.5 %collective-permute-start.9 = (bf16[2,64,256]{2,1,0:T(8,128)(2,1)S(1)}, bf16[2,64,256]{2,1,0:T(8,128)(2,1)S(1)}, u32[]{:S(2)}, u32[]{:S(2)}) collective-permute-start(bf16[2,64,256]{2,1,0:T(8,128)(2,1)S(1)} %get-tuple-element.61), channel_id=1, source_target_pairs={{0,4},{4,0},{8,12},{12,8},{1,5},{5,1},{9,13},{13,9},{2,6},{6,2},{1... | collective-permute-start | bytes 196616 | tf_op jit(solution)/shard_map/ppermute | solution.py:302
  29.6 7.5 %collective-permute-start.10 = (bf16[2,64,256]{2,1,0:T(8,128)(2,1)S(1)}, bf16[2,64,256]{2,1,0:T(8,128)(2,1)S(1)}, u32[]{:S(2)}, u32[]{:S(2)}) collective-permute-start(bf16[2,64,256]{2,1,0:T(8,128)(2,1)S(1)} %get-tuple-element.62), channel_id=1, source_target_pairs={{0,8},{4,12},{8,0},{12,4},{1,9},{5,13},{9,1},{13,5},{2,10},{6,14},... | collective-permute-start | bytes 196616 | tf_op jit(solution)/shard_map/ppermute | solution.py:302
  33.1 6.1 %collective-permute-start.11 = (bf16[2,64,256]{2,1,0:T(8,128)(2,1)S(1)}, bf16[2,64,256]{2,1,0:T(8,128)(2,1)S(1)}, u32[]{:S(2)}, u32[]{:S(2)}) collective-permute-start(bf16[2,64,256]{2,1,0:T(8,128)(2,1)S(1)} %get-tuple-element.63), channel_id=1, source_target_pairs={{0,12},{4,8},{8,4},{12,0},{1,13},{5,9},{9,5},{13,1},{2,14},{6,10},... | collective-permute-start | bytes 196616 | tf_op jit(solution)/shard_map/ppermute | solution.py:302
  39.3 8.9 %collective-permute-start.16 = (bf16[2,512,256]{2,1,0:T(8,128)(2,1)S(1)}, bf16[2,512,256]{2,1,0:T(8,128)(2,1)S(1)}, u32[]{:S(2)}, u32[]{:S(2)}) collective-permute-start(bf16[2,512,256]{2,1,0:T(8,128)(2,1)S(1)} %pad_maximum_fusion), channel_id=1, source_target_pairs={{0,1},{1,0},{2,3},{3,2},{4,5},{5,4},{6,7},{7,6},{8,9},{9,8},{10,11... | collective-permute-start | bytes 1572872 | tf_op jit(solution)/shard_map/ppermute | solution.py:305
  39.4 6.9 %collective-permute-start.19 = (bf16[2,64,256]{2,1,0:T(8,128)(2,1)S(1)}, bf16[2,64,256]{2,1,0:T(8,128)(2,1)S(1)}, u32[]{:S(2)}, u32[]{:S(2)}) collective-permute-start(bf16[2,64,256]{2,1,0:T(8,128)(2,1)S(1)} %add_sums.5.refs_3_), channel_id=1, source_target_pairs={{0,12},{4,8},{8,4},{12,0},{1,13},{5,9},{9,5},{13,1},{2,14},{6,10},... | collective-permute-start | bytes 196616 | tf_op jit(solution)/shard_map/ppermute | solution.py:302
  40.3 7.9 %collective-permute-start.18 = (bf16[2,64,256]{2,1,0:T(8,128)(2,1)S(1)}, bf16[2,64,256]{2,1,0:T(8,128)(2,1)S(1)}, u32[]{:S(2)}, u32[]{:S(2)}) collective-permute-start(bf16[2,64,256]{2,1,0:T(8,128)(2,1)S(1)} %add_sums.5.refs_3_), channel_id=1, source_target_pairs={{0,8},{4,12},{8,0},{12,4},{1,9},{5,13},{9,1},{13,5},{2,10},{6,14},... | collective-permute-start | bytes 196616 | tf_op jit(solution)/shard_map/ppermute | solution.py:302
  40.3 7.9 %collective-permute-start.17 = (bf16[2,64,256]{2,1,0:T(8,128)(2,1)S(1)}, bf16[2,64,256]{2,1,0:T(8,128)(2,1)S(1)}, u32[]{:S(2)}, u32[]{:S(2)}) collective-permute-start(bf16[2,64,256]{2,1,0:T(8,128)(2,1)S(1)} %add_sums.5.refs_3_), channel_id=1, source_target_pairs={{0,4},{4,0},{8,12},{12,8},{1,5},{5,1},{9,13},{13,9},{2,6},{6,2},{1... | collective-permute-start | bytes 196616 | tf_op jit(solution)/shard_map/ppermute | solution.py:302

commit v5 on v4

--- a/solution.py
+++ b/solution.py
@@ -80,9 +80,11 @@
         prob = jnp.exp2(scores * (scale * math.log2(math.e)) - offset)
         dprob = lax.dot_general(values, go, NT, preferred_element_type=F32)
         dscore = ((prob * scale) * (dprob - delta)).astype(BF16)
-        dq = lax.dot_general(dscore, keys, TN, preferred_element_type=F32).astype(BF16)
+        turned = jnp.dot(jnp.transpose(keys), dscore, preferred_element_type=F32).astype(BF16)
         for h in range(per_kv):
-            dq_ref[:, g * span + h * HD : g * span + (h + 1) * HD] = dq[h * tokens : (h + 1) * tokens]
+            dq_ref[:, g * span + h * HD : g * span + (h + 1) * HD] = jnp.transpose(
+                turned[:, h * tokens : (h + 1) * tokens]
+            )
         dk = jnp.dot(dscore, q, preferred_element_type=F32)
         dv = jnp.dot(prob.astype(BF16), go, preferred_element_type=F32)
         for c in range(pieces):

time: 50.7 us -> 50.6 us (level)
  transfers between devices with their start and end apart: 20 -> 20, of which waited for: 8 -> 8; matrix products, arithmetic and copies ran while one was open for 0% -> 0% of each run, Pallas kernels for 19% -> 18%
where the time goes in v5:
time: 50.6 us; the launch traced here: 50.4 us
  starting transfers between devices  23.6 us (47%)
  waiting for transfers between devices  11.9 us (24%)
  Pallas kernels  11.6 us (23%)
  local copies, waits for them, and re-layouts  2.23 us (4%)
  between operations  0.92 us (2%)
    ppermute x12, starting transfers between devices, to_ctx(): return lax.ppermute(x, 'ctx', xor_pairs(ctx_count, offset))  19 us
    ppermute x12, waiting for transfers between devices, to_ctx(): return lax.ppermute(x, 'ctx', xor_pairs(ctx_count, offset))  8.44 us
    pallas_call x4, Pallas kernels, head_block(): pl.pallas_call(functools.partial(heads_kernel, per_kv, off), in_specs=[WH...  6.86 us
    ppermute x8, starting transfers between devices, to_roll(): return lax.ppermute(x, 'roll', xor_pairs(roll_count, offset))  4.59 us
    ppermute x8, waiting for transfers between devices, to_roll(): return lax.ppermute(x, 'roll', xor_pairs(roll_count, offset))  3.46 us
    pallas_call x1, Pallas kernels, weight_grads(): pl.pallas_call(kernel, in_specs=[WHOLE] * (len(shares) + len(low)), out_s...  2.34 us
    unnamed x20, local copies, waits for them, and re-layouts  2.2 us
    pallas_call x1, Pallas kernels, finish(): pl.pallas_call(kernel, in_specs=[anywhere] * count + [WHOLE] * (1 + len(r...  1.4 us
  transfers between devices with their start and end apart: 20, of which 8 were waited for; matrix products, arithmetic and copies ran while one was open for 0% of the time, Pallas kernels for 18%

profile of v5, /device:TPU:0, one launch (start us, length us, event | category | flops | bytes accessed | tf_op | source)
XLA Modules:
  0.0 50.4 jit_solution(2487938641553229340)
XLA Ops:
  0.7 0.9 %copy-done = bf16[2,64,1024]{2,1,0:T(8,128)(2,1)S(1)} copy-done((bf16[2,64,1024]{2,1,0:T(8,128)(2,1)S(1)}, bf16[2,64,1024]{2,1,0:T(8,128)(2,1)}, u32[]{:S(2)}) %copy-start) | copy-done | bytes 262168
  1.6 4.1 %collective-permute-start.1 = (bf16[2,64,256]{2,1,0:T(8,128)(2,1)S(1)}, bf16[2,64,256]{2,1,0:T(8,128)(2,1)S(1)}, u32[]{:S(2)}, u32[]{:S(2)}) collective-permute-start(bf16[2,64,256]{2,1,0:T(8,128)(2,1)S(1)} %constant_dynamic-slice_fusion), channel_id=1, source_target_pairs={{0,8},{4,12},{8,0},{12,4},{1,9},{5,13},{9,1},{13,5},{2,10},{6,14},... | collective-permute-start | bytes 196616 | tf_op jit(solution)/shard_map/ppermute | solution.py:304
  5.7 1.6 %collective-permute-start = (bf16[2,64,256]{2,1,0:T(8,128)(2,1)S(1)}, bf16[2,64,256]{2,1,0:T(8,128)(2,1)S(1)}, u32[]{:S(2)}, u32[]{:S(2)}) collective-permute-start(bf16[2,64,256]{2,1,0:T(8,128)(2,1)S(1)} %constant_dynamic-slice_fusion), channel_id=1, source_target_pairs={{0,4},{4,0},{8,12},{12,8},{1,5},{5,1},{9,13},{13,9},{2,6},{6,2},{1... | collective-permute-start | bytes 196616 | tf_op jit(solution)/shard_map/ppermute | solution.py:304
  7.3 1.2 %copy-done.3 = bf16[64,8192]{1,0:T(8,128)(2,1)S(1)} copy-done((bf16[64,8192]{1,0:T(8,128)(2,1)S(1)}, bf16[64,8192]{1,0:T(8,128)(2,1)}, u32[]{:S(2)}) %copy-start.3) | copy-done | bytes 1048600
  8.6 0.1 cut_hidden.1
  8.6 1.0 %collective-permute-start.12 = (bf16[64,512]{1,0:T(8,128)(2,1)S(1)}, bf16[64,512]{1,0:T(8,128)(2,1)S(1)}, u32[]{:S(2)}, u32[]{:S(2)}) collective-permute-start(bf16[64,512]{1,0:T(8,128)(2,1)S(1)} %get-tuple-element.72), channel_id=1, source_target_pairs={{0,4},{4,0},{8,12},{12,8},{1,5},{5,1},{9,13},{13,9},{2,6},{6,2},{1... | collective-permute-start | bytes 196616 | tf_op jit(solution)/shard_map/ppermute | solution.py:304
  9.6 3.5 %collective-permute-start.13 = (bf16[64,512]{1,0:T(8,128)(2,1)S(1)}, bf16[64,512]{1,0:T(8,128)(2,1)S(1)}, u32[]{:S(2)}, u32[]{:S(2)}) collective-permute-start(bf16[64,512]{1,0:T(8,128)(2,1)S(1)} %get-tuple-element.73), channel_id=1, source_target_pairs={{0,8},{4,12},{8,0},{12,4},{1,9},{5,13},{9,1},{13,5},{2,10},{6,14},... | collective-permute-start | bytes 196616 | tf_op jit(solution)/shard_map/ppermute | solution.py:304
  13.2 0.7 %prep.1 = (f32[128,128]{1,0:T(8,128)S(1)}, f32[64,128]{1,0:T(8,128)S(1)}, f32[64,128]{1,0:T(8,128)S(1)}) custom-call(s32[4]{0:T(128)S(1)} %copy-done.6, s32[16]{0:T(128)S(1)} %copy-done.7, f32[16]{0:T(128)S(1)} %copy-done.8, s32[16]{0:T(128)S(1)} %copy-done.9, f32[64,128]{1,0:T(8,128)S(1)} %bitcast.11, f32[64,128]{1,0:T(8,128)S(1)} %bitcast.12), custom_call_target="tpu_custom_call" | custom-call | flops 1073741824 | tf_op jit(solution)/shard_map/prep/pallas_call | solution.py:46
  14.0 0.2 collective-permute-done.2
  14.2 1.6 %collective-permute-start.5 = (bf16[4,2,64,256]{3,2,1,0:T(8,128)(2,1)S(1)}, bf16[4,2,64,256]{3,2,1,0:T(8,128)(2,1)S(1)}, u32[]{:S(2)}, u32[]{:S(2)}) collective-permute-start(bf16[4,2,64,256]{3,2,1,0:T(8,128)(2,1)S(1)} %pad_maximum_fusion.1.kv_ref), channel_id=1, source_target_pairs={{0,2},{1,3},{2,0},{3,1},{4,6},{5,7},{6,4},{7,5},{8,10},{9,11},{10,... | collective-permute-start | bytes 786440 | tf_op jit(solution)/shard_map/ppermute | solution.py:307
  15.8 1.7 %head_block.4 = (bf16[128,2048]{1,0:T(8,128)(2,1)S(1)}, bf16[4,2,64,256]{3,2,1,0:T(8,128)(2,1)S(1)}) custom-call(bf16[128,8192]{1,0:T(8,128)(2,1)S(1)} %copy-done.1, bf16[128,8192]{1,0:T(8,128)(2,1)S(1)} %copy-done.2, f32[128,128]{1,0:T(8,128)S(1)} %get-tuple-element.47.w_ref, f32[64,128]{1,0:T(8,128)S(1)} %get-tuple-element.48.o_ref, ...), custom_call_target="tpu_custom_call" | custom-call | flops 5368709120 | tf_op jit(solution)/shard_map/head_block/pallas_call | solution.py:101
  17.5 0.6 %collective-permute-start.4 = (bf16[4,2,64,256]{3,2,1,0:T(8,128)(2,1)S(1)}, bf16[4,2,64,256]{3,2,1,0:T(8,128)(2,1)S(1)}, u32[]{:S(2)}, u32[]{:S(2)}) collective-permute-start(bf16[4,2,64,256]{3,2,1,0:T(8,128)(2,1)S(1)} %get-tuple-element.53), channel_id=1, source_target_pairs={{0,1},{1,0},{2,3},{3,2},{4,5},{5,4},{6,7},{7,6},{8,9},{9,8},{10,11... | collective-permute-start | bytes 786440 | tf_op jit(solution)/shard_map/ppermute | solution.py:307
  18.1 1.7 %head_block.5 = (bf16[128,2048]{1,0:T(8,128)(2,1)S(1)}, f32[4,2,64,256]{3,2,1,0:T(8,128)S(1)}) custom-call(bf16[128,8192]{1,0:T(8,128)(2,1)S(1)} %copy-done.1, bf16[128,8192]{1,0:T(8,128)(2,1)S(1)} %copy-done.2, f32[128,128]{1,0:T(8,128)S(1)} %get-tuple-element.47.w_ref, f32[64,128]{1,0:T(8,128)S(1)} %get-tuple-element.48.o_ref, ...), custom_call_target="tpu_custom_call" | custom-call | flops 5368709120 | tf_op jit(solution)/shard_map/head_block/pallas_call | solution.py:101
  19.9 0.7 %collective-permute-start.8 = (bf16[4,2,64,256]{3,2,1,0:T(8,128)(2,1)S(1)}, bf16[4,2,64,256]{3,2,1,0:T(8,128)(2,1)S(1)}, u32[]{:S(2)}, u32[]{:S(2)}) collective-permute-start(bf16[4,2,64,256]{3,2,1,0:T(8,128)(2,1)S(1)} %add_sums.3), channel_id=1, source_target_pairs={{0,2},{1,3},{2,0},{3,1},{4,6},{5,7},{6,4},{7,5},{8,10},{9,11},{10,... | collective-permute-start | bytes 786440 | tf_op jit(solution)/shard_map/ppermute | solution.py:307
  20.6 0.2 collective-permute-done.5.kv_ref
  20.8 1.7 %head_block.6 = (bf16[128,2048]{1,0:T(8,128)(2,1)S(1)}, bf16[4,2,64,256]{3,2,1,0:T(8,128)(2,1)S(1)}) custom-call(bf16[128,8192]{1,0:T(8,128)(2,1)S(1)} %copy-done.1, bf16[128,8192]{1,0:T(8,128)(2,1)S(1)} %copy-done.2, f32[128,128]{1,0:T(8,128)S(1)} %get-tuple-element.47.w_ref, f32[64,128]{1,0:T(8,128)S(1)} %get-tuple-element.48.o_ref, ...), custom_call_target="tpu_custom_call" | custom-call | flops 5368709120 | tf_op jit(solution)/shard_map/head_block/pallas_call | solution.py:101
  22.5 0.5 %collective-permute-start.7 = (bf16[4,2,64,256]{3,2,1,0:T(8,128)(2,1)S(1)}, bf16[4,2,64,256]{3,2,1,0:T(8,128)(2,1)S(1)}, u32[]{:S(2)}, u32[]{:S(2)}) collective-permute-start(bf16[4,2,64,256]{3,2,1,0:T(8,128)(2,1)S(1)} %get-tuple-element.58), channel_id=1, source_target_pairs={{0,1},{1,0},{2,3},{3,2},{4,5},{5,4},{6,7},{7,6},{8,9},{9,8},{10,11... | collective-permute-start | bytes 786440 | tf_op jit(solution)/shard_map/ppermute | solution.py:307
  23.0 0.1 turn_hidden.1
  23.2 1.7 %head_block.7 = (bf16[128,2048]{1,0:T(8,128)(2,1)S(1)}, f32[4,2,64,256]{3,2,1,0:T(8,128)S(1)}) custom-call(bf16[128,8192]{1,0:T(8,128)(2,1)S(1)} %copy-done.1, bf16[128,8192]{1,0:T(8,128)(2,1)S(1)} %copy-done.2, f32[128,128]{1,0:T(8,128)S(1)} %get-tuple-element.47.w_ref, f32[64,128]{1,0:T(8,128)S(1)} %get-tuple-element.48.o_ref, ...), custom_call_target="tpu_custom_call" | custom-call | flops 5368709120 | tf_op jit(solution)/shard_map/head_block/pallas_call | solution.py:101
  24.9 3.3 %collective-permute-done.8.refs_1_ = bf16[4,2,64,256]{3,2,1,0:T(8,128)(2,1)S(1)} collective-permute-done((bf16[4,2,64,256]{3,2,1,0:T(8,128)(2,1)S(1)}, bf16[4,2,64,256]{3,2,1,0:T(8,128)(2,1)S(1)}, u32[]{:S(2)}, u32[]{:S(2)}) %collective-permute-start.8) | collective-permute-done | bytes 262176 | tf_op jit(solution)/shard_map/ppermute | solution.py:307
  28.3 1.1 %collective-permute-start.15 = (bf16[1,512,256]{2,1,0:T(8,128)(2,1)S(1)}, bf16[1,512,256]{2,1,0:T(8,128)(2,1)S(1)}, u32[]{:S(2)}, u32[]{:S(2)}) collective-permute-start(bf16[1,512,256]{2,1,0:T(8,128)(2,1)S(1)} %bitcast.8), channel_id=1, source_target_pairs={{0,2},{1,3},{2,0},{3,1},{4,6},{5,7},{6,4},{7,5},{8,10},{9,11},{10,... | collective-permute-start | bytes 786440 | tf_op jit(solution)/shard_map/ppermute | solution.py:307
  29.5 3.5 %collective-permute-start.10 = (bf16[2,64,256]{2,1,0:T(8,128)(2,1)S(1)}, bf16[2,64,256]{2,1,0:T(8,128)(2,1)S(1)}, u32[]{:S(2)}, u32[]{:S(2)}) collective-permute-start(bf16[2,64,256]{2,1,0:T(8,128)(2,1)S(1)} %get-tuple-element.62), channel_id=1, source_target_pairs={{0,8},{4,12},{8,0},{12,4},{1,9},{5,13},{9,1},{13,5},{2,10},{6,14},... | collective-permute-start | bytes 196616 | tf_op jit(solution)/shard_map/ppermute | solution.py:304
  33.0 0.8 %collective-permute-start.11 = (bf16[2,64,256]{2,1,0:T(8,128)(2,1)S(1)}, bf16[2,64,256]{2,1,0:T(8,128)(2,1)S(1)}, u32[]{:S(2)}, u32[]{:S(2)}) collective-permute-start(bf16[2,64,256]{2,1,0:T(8,128)(2,1)S(1)} %get-tuple-element.63), channel_id=1, source_target_pairs={{0,12},{4,8},{8,4},{12,0},{1,13},{5,9},{9,5},{13,1},{2,14},{6,10},... | collective-permute-start | bytes 196616 | tf_op jit(solution)/shard_map/ppermute | solution.py:304
  33.8 0.1 collective-permute-done.9.refs_0_.refs_5_
  33.9 3.2 %collective-permute-done.10.refs_1_.refs_6_ = bf16[2,64,256]{2,1,0:T(8,128)(2,1)S(1)} collective-permute-done((bf16[2,64,256]{2,1,0:T(8,128)(2,1)S(1)}, bf16[2,64,256]{2,1,0:T(8,128)(2,1)S(1)}, u32[]{:S(2)}, u32[]{:S(2)}) %collective-permute-start.10) | collective-permute-done | bytes 65568 | tf_op jit(solution)/shard_map/ppermute | solution.py:304
  37.0 2.0 %collective-permute-done.11.refs_2_.refs_7_ = bf16[2,64,256]{2,1,0:T(8,128)(2,1)S(1)} collective-permute-done((bf16[2,64,256]{2,1,0:T(8,128)(2,1)S(1)}, bf16[2,64,256]{2,1,0:T(8,128)(2,1)S(1)}, u32[]{:S(2)}, u32[]{:S(2)}) %collective-permute-start.11) | collective-permute-done | bytes 65568 | tf_op jit(solution)/shard_map/ppermute | solution.py:304
  39.3 0.9 %collective-permute-start.19 = (bf16[2,64,256]{2,1,0:T(8,128)(2,1)S(1)}, bf16[2,64,256]{2,1,0:T(8,128)(2,1)S(1)}, u32[]{:S(2)}, u32[]{:S(2)}) collective-permute-start(bf16[2,64,256]{2,1,0:T(8,128)(2,1)S(1)} %add_sums.5.refs_3_), channel_id=1, source_target_pairs={{0,12},{4,8},{8,4},{12,0},{1,13},{5,9},{9,5},{13,1},{2,14},{6,10},... | collective-permute-start | bytes 196616 | tf_op jit(solution)/shard_map/ppermute | solution.py:304
  40.2 3.5 %collective-permute-start.17 = (bf16[2,64,256]{2,1,0:T(8,128)(2,1)S(1)}, bf16[2,64,256]{2,1,0:T(8,128)(2,1)S(1)}, u32[]{:S(2)}, u32[]{:S(2)}) collective-permute-start(bf16[2,64,256]{2,1,0:T(8,128)(2,1)S(1)} %add_sums.5.refs_3_), channel_id=1, source_target_pairs={{0,4},{4,0},{8,12},{12,8},{1,5},{5,1},{9,13},{13,9},{2,6},{6,2},{1... | collective-permute-start | bytes 196616 | tf_op jit(solution)/shard_map/ppermute | solution.py:304
  43.7 1.4 %finish.1 = (bf16[128,8192]{1,0:T(8,128)(2,1)}, f32[2,64,256]{2,1,0:T(8,128)}) custom-call(bf16[128,2048]{1,0:T(8,128)(2,1)S(1)} %get-tuple-element.64.refs_0_, bf16[128,2048]{1,0:T(8,128)(2,1)S(1)} %get-tuple-element.65.refs_1_, bf16[128,2048]{1,0:T(8,128)(2,1)S(1)} %get-tuple-element.66.refs_2_, bf16[128,2048]{1,0:T(8,128)(2,1)S(1)} %get-tuple-element.67.refs_3_, ...), custom_call_target="tpu_custom_call" | custom-call | flops 1073741824 | tf_op jit(solution)/shard_map/finish/pallas_call | solution.py:146
  45.1 1.0 %collective-permute-done.19.refs_6_ = bf16[2,64,256]{2,1,0:T(8,128)(2,1)S(1)} collective-permute-done((bf16[2,64,256]{2,1,0:T(8,128)(2,1)S(1)}, bf16[2,64,256]{2,1,0:T(8,128)(2,1)S(1)}, u32[]{:S(2)}, u32[]{:S(2)}) %collective-permute-start.19) | collective-permute-done | bytes 65568 | tf_op jit(solution)/shard_map/ppermute | solution.py:304
  46.1 1.9 %collective-permute-done.18.refs_5_ = bf16[2,64,256]{2,1,0:T(8,128)(2,1)S(1)} collective-permute-done((bf16[2,64,256]{2,1,0:T(8,128)(2,1)S(1)}, bf16[2,64,256]{2,1,0:T(8,128)(2,1)S(1)}, u32[]{:S(2)}, u32[]{:S(2)}) %collective-permute-start.18) | collective-permute-done | bytes 65568 | tf_op jit(solution)/shard_map/ppermute | solution.py:304
  48.1 2.3 %weight_grads.1 = f32[2,2048,256]{2,1,0:T(8,128)} custom-call(bf16[1,512,256]{2,1,0:T(8,128)(2,1)S(1)} %bitcast.10, bf16[1,512,256]{2,1,0:T(8,128)(2,1)S(1)} %collective-permute-done.15.refs_1_, bf16[2,512,256]{2,1,0:T(8,128)(2,1)S(1)} %collective-permute-done.16.refs_2_, bf16[2,64,256]{2,1,0:T(8,128)(2,1)S(1)} %add_sums.5.refs_3_, ...), custom_call_target="tpu_custom_call" | custom-call | flops 2147483648 | tf_op jit(solution)/shard_map/weight_grads/pallas_call | solution.py:269
  (44 shorter events, 0.6 us)
Async XLA Ops:
  0.6 1.0 %copy-start = (bf16[2,64,1024]{2,1,0:T(8,128)(2,1)S(1)}, bf16[2,64,1024]{2,1,0:T(8,128)(2,1)}, u32[]{:S(2)}) copy-start(bf16[2,64,1024]{2,1,0:T(8,128)(2,1)} %param.14) | copy-start | bytes 786436
  1.6 11.5 %copy-start.4 = (f32[128,64]{0,1:T(8,128)S(1)}, f32[128,64]{0,1:T(8,128)}, u32[]{:S(2)}) copy-start(f32[128,64]{0,1:T(8,128)} %param.12) | copy-start | bytes 98308
  1.6 11.5 %copy-start.5 = (f32[128,64]{0,1:T(8,128)S(1)}, f32[128,64]{0,1:T(8,128)}, u32[]{:S(2)}) copy-start(f32[128,64]{0,1:T(8,128)} %param.13) | copy-start | bytes 98308
  1.6 11.5 %copy-start.6 = (s32[4]{0:T(128)S(1)}, s32[4]{0:T(128)}, u32[]{:S(2)}) copy-start(s32[4]{0:T(128)} %ids.1) | copy-start | bytes 52
  1.6 11.5 %copy-start.7 = (s32[16]{0:T(128)S(1)}, s32[16]{0:T(128)}, u32[]{:S(2)}) copy-start(s32[16]{0:T(128)} %lengths.1) | copy-start | bytes 196
  1.6 11.6 %copy-start.8 = (f32[16]{0:T(128)S(1)}, f32[16]{0:T(128)}, u32[]{:S(2)}) copy-start(f32[16]{0:T(128)} %advantages.1) | copy-start | bytes 196
  1.6 11.6 %copy-start.9 = (s32[16]{0:T(128)S(1)}, s32[16]{0:T(128)}, u32[]{:S(2)}) copy-start(s32[16]{0:T(128)} %adv_index.1) | copy-start | bytes 196
  1.6 12.2 %collective-permute-start.1 = (bf16[2,64,256]{2,1,0:T(8,128)(2,1)S(1)}, bf16[2,64,256]{2,1,0:T(8,128)(2,1)S(1)}, u32[]{:S(2)}, u32[]{:S(2)}) collective-permute-start(bf16[2,64,256]{2,1,0:T(8,128)(2,1)S(1)} %constant_dynamic-slice_fusion), channel_id=1, source_target_pairs={{0,8},{4,12},{8,0},{12,4},{1,9},{5,13},{9,1},{13,5},{2,10},{6,14},... | collective-permute-start | bytes 196616 | tf_op jit(solution)/shard_map/ppermute | solution.py:304
  5.7 8.2 %collective-permute-start = (bf16[2,64,256]{2,1,0:T(8,128)(2,1)S(1)}, bf16[2,64,256]{2,1,0:T(8,128)(2,1)S(1)}, u32[]{:S(2)}, u32[]{:S(2)}) collective-permute-start(bf16[2,64,256]{2,1,0:T(8,128)(2,1)S(1)} %constant_dynamic-slice_fusion), channel_id=1, source_target_pairs={{0,4},{4,0},{8,12},{12,8},{1,5},{5,1},{9,13},{13,9},{2,6},{6,2},{1... | collective-permute-start | bytes 196616 | tf_op jit(solution)/shard_map/ppermute | solution.py:304
  7.3 6.9 %collective-permute-start.2 = (bf16[2,64,256]{2,1,0:T(8,128)(2,1)S(1)}, bf16[2,64,256]{2,1,0:T(8,128)(2,1)S(1)}, u32[]{:S(2)}, u32[]{:S(2)}) collective-permute-start(bf16[2,64,256]{2,1,0:T(8,128)(2,1)S(1)} %constant_dynamic-slice_fusion), channel_id=1, source_target_pairs={{0,12},{4,8},{8,4},{12,0},{1,13},{5,9},{9,5},{13,1},{2,14},{6,10},... | collective-permute-start | bytes 196616 | tf_op jit(solution)/shard_map/ppermute | solution.py:304
  7.3 1.2 %copy-start.3 = (bf16[64,8192]{1,0:T(8,128)(2,1)S(1)}, bf16[64,8192]{1,0:T(8,128)(2,1)}, u32[]{:S(2)}) copy-start(bf16[64,8192]{1,0:T(8,128)(2,1)} %x_ref.1) | copy-start | bytes 3145732
  8.6 13.9 %collective-permute-start.12 = (bf16[64,512]{1,0:T(8,128)(2,1)S(1)}, bf16[64,512]{1,0:T(8,128)(2,1)S(1)}, u32[]{:S(2)}, u32[]{:S(2)}) collective-permute-start(bf16[64,512]{1,0:T(8,128)(2,1)S(1)} %get-tuple-element.72), channel_id=1, source_target_pairs={{0,4},{4,0},{8,12},{12,8},{1,5},{5,1},{9,13},{13,9},{2,6},{6,2},{1... | collective-permute-start | bytes 196616 | tf_op jit(solution)/shard_map/ppermute | solution.py:304
  9.6 13.4 %collective-permute-start.13 = (bf16[64,512]{1,0:T(8,128)(2,1)S(1)}, bf16[64,512]{1,0:T(8,128)(2,1)S(1)}, u32[]{:S(2)}, u32[]{:S(2)}) collective-permute-start(bf16[64,512]{1,0:T(8,128)(2,1)S(1)} %get-tuple-element.73), channel_id=1, source_target_pairs={{0,8},{4,12},{8,0},{12,4},{1,9},{5,13},{9,1},{13,5},{2,10},{6,14},... | collective-permute-start | bytes 196616 | tf_op jit(solution)/shard_map/ppermute | solution.py:304
  13.2 2.6 %copy-start.1 = (bf16[128,8192]{1,0:T(8,128)(2,1)S(1)}, bf16[128,8192]{1,0:T(8,128)(2,1)}, u32[]{:S(2)}) copy-start(bf16[128,8192]{1,0:T(8,128)(2,1)} %q_ref.7) | copy-start | bytes 6291460
  13.2 2.6 %copy-start.2 = (bf16[128,8192]{1,0:T(8,128)(2,1)S(1)}, bf16[128,8192]{1,0:T(8,128)(2,1)}, u32[]{:S(2)}) copy-start(bf16[128,8192]{1,0:T(8,128)(2,1)} %ct_ref.7) | copy-start | bytes 6291460
  13.9 9.2 %collective-permute-start.14 = (bf16[64,512]{1,0:T(8,128)(2,1)S(1)}, bf16[64,512]{1,0:T(8,128)(2,1)S(1)}, u32[]{:S(2)}, u32[]{:S(2)}) collective-permute-start(bf16[64,512]{1,0:T(8,128)(2,1)S(1)} %get-tuple-element.74), channel_id=1, source_target_pairs={{0,12},{4,8},{8,4},{12,0},{1,13},{5,9},{9,5},{13,1},{2,14},{6,10},... | collective-permute-start | bytes 196616 | tf_op jit(solution)/shard_map/ppermute | solution.py:304
  14.2 6.5 %collective-permute-start.5 = (bf16[4,2,64,256]{3,2,1,0:T(8,128)(2,1)S(1)}, bf16[4,2,64,256]{3,2,1,0:T(8,128)(2,1)S(1)}, u32[]{:S(2)}, u32[]{:S(2)}) collective-permute-start(bf16[4,2,64,256]{3,2,1,0:T(8,128)(2,1)S(1)} %pad_maximum_fusion.1.kv_ref), channel_id=1, source_target_pairs={{0,2},{1,3},{2,0},{3,1},{4,6},{5,7},{6,4},{7,5},{8,10},{9,11},{10,... | collective-permute-start | bytes 786440 | tf_op jit(solution)/shard_map/ppermute | solution.py:307
  15.8 1.7 %collective-permute-start.3 = (bf16[4,2,64,256]{3,2,1,0:T(8,128)(2,1)S(1)}, bf16[4,2,64,256]{3,2,1,0:T(8,128)(2,1)S(1)}, u32[]{:S(2)}, u32[]{:S(2)}) collective-permute-start(bf16[4,2,64,256]{3,2,1,0:T(8,128)(2,1)S(1)} %pad_maximum_fusion.1.kv_ref), channel_id=1, source_target_pairs={{0,1},{1,0},{2,3},{3,2},{4,5},{5,4},{6,7},{7,6},{8,9},{9,8},{10,11... | collective-permute-start | bytes 786440 | tf_op jit(solution)/shard_map/ppermute | solution.py:307
  17.5 2.3 %collective-permute-start.4 = (bf16[4,2,64,256]{3,2,1,0:T(8,128)(2,1)S(1)}, bf16[4,2,64,256]{3,2,1,0:T(8,128)(2,1)S(1)}, u32[]{:S(2)}, u32[]{:S(2)}) collective-permute-start(bf16[4,2,64,256]{3,2,1,0:T(8,128)(2,1)S(1)} %get-tuple-element.53), channel_id=1, source_target_pairs={{0,1},{1,0},{2,3},{3,2},{4,5},{5,4},{6,7},{7,6},{8,9},{9,8},{10,11... | collective-permute-start | bytes 786440 | tf_op jit(solution)/shard_map/ppermute | solution.py:307
  19.9 8.3 %collective-permute-start.8 = (bf16[4,2,64,256]{3,2,1,0:T(8,128)(2,1)S(1)}, bf16[4,2,64,256]{3,2,1,0:T(8,128)(2,1)S(1)}, u32[]{:S(2)}, u32[]{:S(2)}) collective-permute-start(bf16[4,2,64,256]{3,2,1,0:T(8,128)(2,1)S(1)} %add_sums.3), channel_id=1, source_target_pairs={{0,2},{1,3},{2,0},{3,1},{4,6},{5,7},{6,4},{7,5},{8,10},{9,11},{10,... | collective-permute-start | bytes 786440 | tf_op jit(solution)/shard_map/ppermute | solution.py:307
  20.7 2.4 %collective-permute-start.6 = (bf16[4,2,64,256]{3,2,1,0:T(8,128)(2,1)S(1)}, bf16[4,2,64,256]{3,2,1,0:T(8,128)(2,1)S(1)}, u32[]{:S(2)}, u32[]{:S(2)}) collective-permute-start(bf16[4,2,64,256]{3,2,1,0:T(8,128)(2,1)S(1)} %collective-permute-done.5.kv_ref), channel_id=1, source_target_pairs={{0,1},{1,0},{2,3},{3,2},{4,5},{5,4},{6,7},{7,6},{8,9},{9,8},{10,11... | collective-permute-start | bytes 786440 | tf_op jit(solution)/shard_map/ppermute | solution.py:307
  22.5 5.7 %collective-permute-start.7 = (bf16[4,2,64,256]{3,2,1,0:T(8,128)(2,1)S(1)}, bf16[4,2,64,256]{3,2,1,0:T(8,128)(2,1)S(1)}, u32[]{:S(2)}, u32[]{:S(2)}) collective-permute-start(bf16[4,2,64,256]{3,2,1,0:T(8,128)(2,1)S(1)} %get-tuple-element.58), channel_id=1, source_target_pairs={{0,1},{1,0},{2,3},{3,2},{4,5},{5,4},{6,7},{7,6},{8,9},{9,8},{10,11... | collective-permute-start | bytes 786440 | tf_op jit(solution)/shard_map/ppermute | solution.py:307
  28.3 10.9 %collective-permute-start.15 = (bf16[1,512,256]{2,1,0:T(8,128)(2,1)S(1)}, bf16[1,512,256]{2,1,0:T(8,128)(2,1)S(1)}, u32[]{:S(2)}, u32[]{:S(2)}) collective-permute-start(bf16[1,512,256]{2,1,0:T(8,128)(2,1)S(1)} %bitcast.8), channel_id=1, source_target_pairs={{0,2},{1,3},{2,0},{3,1},{4,6},{5,7},{6,4},{7,5},{8,10},{9,11},{10,... | collective-permute-start | bytes 786440 | tf_op jit(solution)/shard_map/ppermute | solution.py:307
  29.4 4.5 %collective-permute-start.9 = (bf16[2,64,256]{2,1,0:T(8,128)(2,1)S(1)}, bf16[2,64,256]{2,1,0:T(8,128)(2,1)S(1)}, u32[]{:S(2)}, u32[]{:S(2)}) collective-permute-start(bf16[2,64,256]{2,1,0:T(8,128)(2,1)S(1)} %get-tuple-element.61), channel_id=1, source_target_pairs={{0,4},{4,0},{8,12},{12,8},{1,5},{5,1},{9,13},{13,9},{2,6},{6,2},{1... | collective-permute-start | bytes 196616 | tf_op jit(solution)/shard_map/ppermute | solution.py:304
  29.5 7.5 %collective-permute-start.10 = (bf16[2,64,256]{2,1,0:T(8,128)(2,1)S(1)}, bf16[2,64,256]{2,1,0:T(8,128)(2,1)S(1)}, u32[]{:S(2)}, u32[]{:S(2)}) collective-permute-start(bf16[2,64,256]{2,1,0:T(8,128)(2,1)S(1)} %get-tuple-element.62), channel_id=1, source_target_pairs={{0,8},{4,12},{8,0},{12,4},{1,9},{5,13},{9,1},{13,5},{2,10},{6,14},... | collective-permute-start | bytes 196616 | tf_op jit(solution)/shard_map/ppermute | solution.py:304
  33.0 6.1 %collective-permute-start.11 = (bf16[2,64,256]{2,1,0:T(8,128)(2,1)S(1)}, bf16[2,64,256]{2,1,0:T(8,128)(2,1)S(1)}, u32[]{:S(2)}, u32[]{:S(2)}) collective-permute-start(bf16[2,64,256]{2,1,0:T(8,128)(2,1)S(1)} %get-tuple-element.63), channel_id=1, source_target_pairs={{0,12},{4,8},{8,4},{12,0},{1,13},{5,9},{9,5},{13,1},{2,14},{6,10},... | collective-permute-start | bytes 196616 | tf_op jit(solution)/shard_map/ppermute | solution.py:304
  39.2 8.9 %collective-permute-start.16 = (bf16[2,512,256]{2,1,0:T(8,128)(2,1)S(1)}, bf16[2,512,256]{2,1,0:T(8,128)(2,1)S(1)}, u32[]{:S(2)}, u32[]{:S(2)}) collective-permute-start(bf16[2,512,256]{2,1,0:T(8,128)(2,1)S(1)} %pad_maximum_fusion), channel_id=1, source_target_pairs={{0,1},{1,0},{2,3},{3,2},{4,5},{5,4},{6,7},{7,6},{8,9},{9,8},{10,11... | collective-permute-start | bytes 1572872 | tf_op jit(solution)/shard_map/ppermute | solution.py:307
  39.3 6.9 %collective-permute-start.19 = (bf16[2,64,256]{2,1,0:T(8,128)(2,1)S(1)}, bf16[2,64,256]{2,1,0:T(8,128)(2,1)S(1)}, u32[]{:S(2)}, u32[]{:S(2)}) collective-permute-start(bf16[2,64,256]{2,1,0:T(8,128)(2,1)S(1)} %add_sums.5.refs_3_), channel_id=1, source_target_pairs={{0,12},{4,8},{8,4},{12,0},{1,13},{5,9},{9,5},{13,1},{2,14},{6,10},... | collective-permute-start | bytes 196616 | tf_op jit(solution)/shard_map/ppermute | solution.py:304
  40.2 7.9 %collective-permute-start.18 = (bf16[2,64,256]{2,1,0:T(8,128)(2,1)S(1)}, bf16[2,64,256]{2,1,0:T(8,128)(2,1)S(1)}, u32[]{:S(2)}, u32[]{:S(2)}) collective-permute-start(bf16[2,64,256]{2,1,0:T(8,128)(2,1)S(1)} %add_sums.5.refs_3_), channel_id=1, source_target_pairs={{0,8},{4,12},{8,0},{12,4},{1,9},{5,13},{9,1},{13,5},{2,10},{6,14},... | collective-permute-start | bytes 196616 | tf_op jit(solution)/shard_map/ppermute | solution.py:304
  40.2 7.9 %collective-permute-start.17 = (bf16[2,64,256]{2,1,0:T(8,128)(2,1)S(1)}, bf16[2,64,256]{2,1,0:T(8,128)(2,1)S(1)}, u32[]{:S(2)}, u32[]{:S(2)}) collective-permute-start(bf16[2,64,256]{2,1,0:T(8,128)(2,1)S(1)} %add_sums.5.refs_3_), channel_id=1, source_target_pairs={{0,4},{4,0},{8,12},{12,8},{1,5},{5,1},{9,13},{13,9},{2,6},{6,2},{1... | collective-permute-start | bytes 196616 | tf_op jit(solution)/shard_map/ppermute | solution.py:304

commit v6 on v4

--- a/solution.py
+++ b/solution.py
@@ -343,7 +343,7 @@
             delta, total = lax.optimization_barrier((delta, total))
             arrived.append(to_roll(total, off))
     sums = list(add(grads, [sibling] + arrived, [F32] + [BF16] * (ctx_count - 1), True))
-    received = [to_ctx(sums[k], k) for k in range(1, ctx_count)]
+    received = [to_ctx(sums[k], k) for k in reversed(range(1, ctx_count))]
 
     (owned_low,) = add(sums[0], received, [BF16], False)
     x_share = lax.optimization_barrier((x_share, sums[0]))[0]
@@ -356,7 +356,7 @@
         bit //= 2
         if bit:
             x_parts[-1] = lax.optimization_barrier((x_parts[-1], owned_low))[0]
-    low = [owned_low] + [to_ctx(owned_low, k) for k in range(1, ctx_count)]
+    low = [owned_low] + [to_ctx(owned_low, k) for k in reversed(range(1, ctx_count))][::-1]
     dq, sums[0], owned_low = lax.optimization_barrier((dq, sums[0], owned_low))
     query_grad, owned = finish(order, dq, sums[0], received)
     return (query_grad, owned, weight_grads(offsets, x_parts, low))

time: 50.7 us -> 49.8 us (0.982)
  waiting for transfers between devices: 11.8 us -> 10.9 us
    ppermute x12, waiting for transfers between devices: 8.44 us -> 7.54 us  [to_ctx(): return lax.ppermute(x, 'ctx', xor_pairs(ctx_count, offset))]
where the time goes in v6:
time: 49.8 us; the launch traced here: 49.6 us
  starting transfers between devices  23.6 us (47%)
  Pallas kernels  11.9 us (24%)
  waiting for transfers between devices  10.9 us (22%)
  local copies, waits for them, and re-layouts  2.23 us (4%)
  between operations  0.91 us (2%)
    ppermute x12, starting transfers between devices, to_ctx(): return lax.ppermute(x, 'ctx', xor_pairs(ctx_count, offset))  19 us
    ppermute x12, waiting for transfers between devices, to_ctx(): return lax.ppermute(x, 'ctx', xor_pairs(ctx_count, offset))  7.54 us
    pallas_call x4, Pallas kernels, head_block(): pl.pallas_call(functools.partial(heads_kernel, per_kv, off), in_specs=[WH...  7.09 us
    ppermute x8, starting transfers between devices, to_roll(): return lax.ppermute(x, 'roll', xor_pairs(roll_count, offset))  4.59 us
    ppermute x8, waiting for transfers between devices, to_roll(): return lax.ppermute(x, 'roll', xor_pairs(roll_count, offset))  3.35 us
    pallas_call x1, Pallas kernels, weight_grads(): pl.pallas_call(kernel, in_specs=[WHOLE] * (len(shares) + len(low)), out_s...  2.34 us
    unnamed x20, local copies, waits for them, and re-layouts  2.2 us
    pallas_call x1, Pallas kernels, finish(): pl.pallas_call(kernel, in_specs=[anywhere] * count + [WHOLE] * (1 + len(r...  1.4 us
  transfers between devices with their start and end apart: 20, of which 8 were waited for; matrix products, arithmetic and copies ran while one was open for 0% of the time, Pallas kernels for 19%

profile of v6, /device:TPU:0, one launch (start us, length us, event | category | flops | bytes accessed | tf_op | source)
XLA Modules:
  0.0 49.6 jit_solution(2882954701029351824)
XLA Ops:
  0.7 0.9 %copy-done = bf16[2,64,1024]{2,1,0:T(8,128)(2,1)S(1)} copy-done((bf16[2,64,1024]{2,1,0:T(8,128)(2,1)S(1)}, bf16[2,64,1024]{2,1,0:T(8,128)(2,1)}, u32[]{:S(2)}) %copy-start) | copy-done | bytes 262168
  1.6 4.1 %collective-permute-start.1 = (bf16[2,64,256]{2,1,0:T(8,128)(2,1)S(1)}, bf16[2,64,256]{2,1,0:T(8,128)(2,1)S(1)}, u32[]{:S(2)}, u32[]{:S(2)}) collective-permute-start(bf16[2,64,256]{2,1,0:T(8,128)(2,1)S(1)} %constant_dynamic-slice_fusion), channel_id=1, source_target_pairs={{0,8},{4,12},{8,0},{12,4},{1,9},{5,13},{9,1},{13,5},{2,10},{6,14},... | collective-permute-start | bytes 196616 | tf_op jit(solution)/shard_map/ppermute | solution.py:302
  5.7 1.6 %collective-permute-start = (bf16[2,64,256]{2,1,0:T(8,128)(2,1)S(1)}, bf16[2,64,256]{2,1,0:T(8,128)(2,1)S(1)}, u32[]{:S(2)}, u32[]{:S(2)}) collective-permute-start(bf16[2,64,256]{2,1,0:T(8,128)(2,1)S(1)} %constant_dynamic-slice_fusion), channel_id=1, source_target_pairs={{0,4},{4,0},{8,12},{12,8},{1,5},{5,1},{9,13},{13,9},{2,6},{6,2},{1... | collective-permute-start | bytes 196616 | tf_op jit(solution)/shard_map/ppermute | solution.py:302
  7.3 1.2 %copy-done.3 = bf16[64,8192]{1,0:T(8,128)(2,1)S(1)} copy-done((bf16[64,8192]{1,0:T(8,128)(2,1)S(1)}, bf16[64,8192]{1,0:T(8,128)(2,1)}, u32[]{:S(2)}) %copy-start.3) | copy-done | bytes 1048600
  8.6 0.1 cut_hidden.1
  8.6 1.0 %collective-permute-start.12 = (bf16[64,512]{1,0:T(8,128)(2,1)S(1)}, bf16[64,512]{1,0:T(8,128)(2,1)S(1)}, u32[]{:S(2)}, u32[]{:S(2)}) collective-permute-start(bf16[64,512]{1,0:T(8,128)(2,1)S(1)} %get-tuple-element.72), channel_id=1, source_target_pairs={{0,4},{4,0},{8,12},{12,8},{1,5},{5,1},{9,13},{13,9},{2,6},{6,2},{1... | collective-permute-start | bytes 196616 | tf_op jit(solution)/shard_map/ppermute | solution.py:302
  9.6 3.5 %collective-permute-start.13 = (bf16[64,512]{1,0:T(8,128)(2,1)S(1)}, bf16[64,512]{1,0:T(8,128)(2,1)S(1)}, u32[]{:S(2)}, u32[]{:S(2)}) collective-permute-start(bf16[64,512]{1,0:T(8,128)(2,1)S(1)} %get-tuple-element.73), channel_id=1, source_target_pairs={{0,8},{4,12},{8,0},{12,4},{1,9},{5,13},{9,1},{13,5},{2,10},{6,14},... | collective-permute-start | bytes 196616 | tf_op jit(solution)/shard_map/ppermute | solution.py:302
  13.2 0.7 %prep.1 = (f32[128,128]{1,0:T(8,128)S(1)}, f32[64,128]{1,0:T(8,128)S(1)}, f32[64,128]{1,0:T(8,128)S(1)}) custom-call(s32[4]{0:T(128)S(1)} %copy-done.6, s32[16]{0:T(128)S(1)} %copy-done.7, f32[16]{0:T(128)S(1)} %copy-done.8, s32[16]{0:T(128)S(1)} %copy-done.9, f32[64,128]{1,0:T(8,128)S(1)} %bitcast.11, f32[64,128]{1,0:T(8,128)S(1)} %bitcast.12), custom_call_target="tpu_custom_call" | custom-call | flops 1073741824 | tf_op jit(solution)/shard_map/prep/pallas_call | solution.py:46
  14.0 0.2 collective-permute-done.2
  14.2 1.6 %collective-permute-start.5 = (bf16[4,2,64,256]{3,2,1,0:T(8,128)(2,1)S(1)}, bf16[4,2,64,256]{3,2,1,0:T(8,128)(2,1)S(1)}, u32[]{:S(2)}, u32[]{:S(2)}) collective-permute-start(bf16[4,2,64,256]{3,2,1,0:T(8,128)(2,1)S(1)} %pad_maximum_fusion.1.kv_ref), channel_id=1, source_target_pairs={{0,2},{1,3},{2,0},{3,1},{4,6},{5,7},{6,4},{7,5},{8,10},{9,11},{10,... | collective-permute-start | bytes 786440 | tf_op jit(solution)/shard_map/ppermute | solution.py:305
  15.8 1.8 %head_block.4 = (bf16[128,2048]{1,0:T(8,128)(2,1)S(1)}, bf16[4,2,64,256]{3,2,1,0:T(8,128)(2,1)S(1)}) custom-call(bf16[128,8192]{1,0:T(8,128)(2,1)S(1)} %copy-done.1, bf16[128,8192]{1,0:T(8,128)(2,1)S(1)} %copy-done.2, f32[128,128]{1,0:T(8,128)S(1)} %get-tuple-element.47.w_ref, f32[64,128]{1,0:T(8,128)S(1)} %get-tuple-element.48.o_ref, ...), custom_call_target="tpu_custom_call" | custom-call | flops 5368709120 | tf_op jit(solution)/shard_map/head_block/pallas_call | solution.py:99
  17.6 0.6 %collective-permute-start.4 = (bf16[4,2,64,256]{3,2,1,0:T(8,128)(2,1)S(1)}, bf16[4,2,64,256]{3,2,1,0:T(8,128)(2,1)S(1)}, u32[]{:S(2)}, u32[]{:S(2)}) collective-permute-start(bf16[4,2,64,256]{3,2,1,0:T(8,128)(2,1)S(1)} %get-tuple-element.53), channel_id=1, source_target_pairs={{0,1},{1,0},{2,3},{3,2},{4,5},{5,4},{6,7},{7,6},{8,9},{9,8},{10,11... | collective-permute-start | bytes 786440 | tf_op jit(solution)/shard_map/ppermute | solution.py:305
  18.2 1.8 %head_block.5 = (bf16[128,2048]{1,0:T(8,128)(2,1)S(1)}, f32[4,2,64,256]{3,2,1,0:T(8,128)S(1)}) custom-call(bf16[128,8192]{1,0:T(8,128)(2,1)S(1)} %copy-done.1, bf16[128,8192]{1,0:T(8,128)(2,1)S(1)} %copy-done.2, f32[128,128]{1,0:T(8,128)S(1)} %get-tuple-element.47.w_ref, f32[64,128]{1,0:T(8,128)S(1)} %get-tuple-element.48.o_ref, ...), custom_call_target="tpu_custom_call" | custom-call | flops 5368709120 | tf_op jit(solution)/shard_map/head_block/pallas_call | solution.py:99
  20.0 0.7 %collective-permute-start.8 = (bf16[4,2,64,256]{3,2,1,0:T(8,128)(2,1)S(1)}, bf16[4,2,64,256]{3,2,1,0:T(8,128)(2,1)S(1)}, u32[]{:S(2)}, u32[]{:S(2)}) collective-permute-start(bf16[4,2,64,256]{3,2,1,0:T(8,128)(2,1)S(1)} %add_sums.3), channel_id=1, source_target_pairs={{0,2},{1,3},{2,0},{3,1},{4,6},{5,7},{6,4},{7,5},{8,10},{9,11},{10,... | collective-permute-start | bytes 786440 | tf_op jit(solution)/shard_map/ppermute | solution.py:305
  20.7 0.2 collective-permute-start.6
  20.9 1.8 %head_block.6 = (bf16[128,2048]{1,0:T(8,128)(2,1)S(1)}, bf16[4,2,64,256]{3,2,1,0:T(8,128)(2,1)S(1)}) custom-call(bf16[128,8192]{1,0:T(8,128)(2,1)S(1)} %copy-done.1, bf16[128,8192]{1,0:T(8,128)(2,1)S(1)} %copy-done.2, f32[128,128]{1,0:T(8,128)S(1)} %get-tuple-element.47.w_ref, f32[64,128]{1,0:T(8,128)S(1)} %get-tuple-element.48.o_ref, ...), custom_call_target="tpu_custom_call" | custom-call | flops 5368709120 | tf_op jit(solution)/shard_map/head_block/pallas_call | solution.py:99
  22.7 0.4 collective-permute-start.7
  23.1 0.1 turn_hidden.1
  23.2 1.8 %head_block.7 = (bf16[128,2048]{1,0:T(8,128)(2,1)S(1)}, f32[4,2,64,256]{3,2,1,0:T(8,128)S(1)}) custom-call(bf16[128,8192]{1,0:T(8,128)(2,1)S(1)} %copy-done.1, bf16[128,8192]{1,0:T(8,128)(2,1)S(1)} %copy-done.2, f32[128,128]{1,0:T(8,128)S(1)} %get-tuple-element.47.w_ref, f32[64,128]{1,0:T(8,128)S(1)} %get-tuple-element.48.o_ref, ...), custom_call_target="tpu_custom_call" | custom-call | flops 5368709120 | tf_op jit(solution)/shard_map/head_block/pallas_call | solution.py:99
  25.0 3.3 %collective-permute-done.8.refs_1_ = bf16[4,2,64,256]{3,2,1,0:T(8,128)(2,1)S(1)} collective-permute-done((bf16[4,2,64,256]{3,2,1,0:T(8,128)(2,1)S(1)}, bf16[4,2,64,256]{3,2,1,0:T(8,128)(2,1)S(1)}, u32[]{:S(2)}, u32[]{:S(2)}) %collective-permute-start.8) | collective-permute-done | bytes 262176 | tf_op jit(solution)/shard_map/ppermute | solution.py:305
  28.4 1.1 %collective-permute-start.15 = (bf16[1,512,256]{2,1,0:T(8,128)(2,1)S(1)}, bf16[1,512,256]{2,1,0:T(8,128)(2,1)S(1)}, u32[]{:S(2)}, u32[]{:S(2)}) collective-permute-start(bf16[1,512,256]{2,1,0:T(8,128)(2,1)S(1)} %bitcast.8), channel_id=1, source_target_pairs={{0,2},{1,3},{2,0},{3,1},{4,6},{5,7},{6,4},{7,5},{8,10},{9,11},{10,... | collective-permute-start | bytes 786440 | tf_op jit(solution)/shard_map/ppermute | solution.py:305
  29.5 3.0 %collective-permute-start.9 = (bf16[2,64,256]{2,1,0:T(8,128)(2,1)S(1)}, bf16[2,64,256]{2,1,0:T(8,128)(2,1)S(1)}, u32[]{:S(2)}, u32[]{:S(2)}) collective-permute-start(bf16[2,64,256]{2,1,0:T(8,128)(2,1)S(1)} %get-tuple-element.61), channel_id=1, source_target_pairs={{0,12},{4,8},{8,4},{12,0},{1,13},{5,9},{9,5},{13,1},{2,14},{6,10},... | collective-permute-start | bytes 196616 | tf_op jit(solution)/shard_map/ppermute | solution.py:302
  32.6 1.3 %collective-permute-start.11 = (bf16[2,64,256]{2,1,0:T(8,128)(2,1)S(1)}, bf16[2,64,256]{2,1,0:T(8,128)(2,1)S(1)}, u32[]{:S(2)}, u32[]{:S(2)}) collective-permute-start(bf16[2,64,256]{2,1,0:T(8,128)(2,1)S(1)} %get-tuple-element.63), channel_id=1, source_target_pairs={{0,4},{4,0},{8,12},{12,8},{1,5},{5,1},{9,13},{13,9},{2,6},{6,2},{1... | collective-permute-start | bytes 196616 | tf_op jit(solution)/shard_map/ppermute | solution.py:302
  33.9 1.7 %collective-permute-done.9.refs_0_.refs_5_ = bf16[2,64,256]{2,1,0:T(8,128)(2,1)S(1)} collective-permute-done((bf16[2,64,256]{2,1,0:T(8,128)(2,1)S(1)}, bf16[2,64,256]{2,1,0:T(8,128)(2,1)S(1)}, u32[]{:S(2)}, u32[]{:S(2)}) %collective-permute-start.9) | collective-permute-done | bytes 65568 | tf_op jit(solution)/shard_map/ppermute | solution.py:302
  35.6 2.2 %collective-permute-done.10.refs_1_.refs_6_ = bf16[2,64,256]{2,1,0:T(8,128)(2,1)S(1)} collective-permute-done((bf16[2,64,256]{2,1,0:T(8,128)(2,1)S(1)}, bf16[2,64,256]{2,1,0:T(8,128)(2,1)S(1)}, u32[]{:S(2)}, u32[]{:S(2)}) %collective-permute-start.10) | collective-permute-done | bytes 65568 | tf_op jit(solution)/shard_map/ppermute | solution.py:302
  37.8 0.2 collective-permute-done.11.refs_2_.refs_7_
  38.1 2.2 %collective-permute-start.19 = (bf16[2,64,256]{2,1,0:T(8,128)(2,1)S(1)}, bf16[2,64,256]{2,1,0:T(8,128)(2,1)S(1)}, u32[]{:S(2)}, u32[]{:S(2)}) collective-permute-start(bf16[2,64,256]{2,1,0:T(8,128)(2,1)S(1)} %add_sums.5.refs_3_), channel_id=1, source_target_pairs={{0,12},{4,8},{8,4},{12,0},{1,13},{5,9},{9,5},{13,1},{2,14},{6,10},... | collective-permute-start | bytes 196616 | tf_op jit(solution)/shard_map/ppermute | solution.py:302
  40.3 2.3 %collective-permute-start.17 = (bf16[2,64,256]{2,1,0:T(8,128)(2,1)S(1)}, bf16[2,64,256]{2,1,0:T(8,128)(2,1)S(1)}, u32[]{:S(2)}, u32[]{:S(2)}) collective-permute-start(bf16[2,64,256]{2,1,0:T(8,128)(2,1)S(1)} %add_sums.5.refs_3_), channel_id=1, source_target_pairs={{0,4},{4,0},{8,12},{12,8},{1,5},{5,1},{9,13},{13,9},{2,6},{6,2},{1... | collective-permute-start | bytes 196616 | tf_op jit(solution)/shard_map/ppermute | solution.py:302
  42.6 1.4 %finish.1 = (bf16[128,8192]{1,0:T(8,128)(2,1)}, f32[2,64,256]{2,1,0:T(8,128)}) custom-call(bf16[128,2048]{1,0:T(8,128)(2,1)S(1)} %get-tuple-element.64.refs_0_, bf16[128,2048]{1,0:T(8,128)(2,1)S(1)} %get-tuple-element.65.refs_1_, bf16[128,2048]{1,0:T(8,128)(2,1)S(1)} %get-tuple-element.66.refs_2_, bf16[128,2048]{1,0:T(8,128)(2,1)S(1)} %get-tuple-element.67.refs_3_, ...), custom_call_target="tpu_custom_call" | custom-call | flops 1073741824 | tf_op jit(solution)/shard_map/finish/pallas_call | solution.py:144
  44.0 1.0 %collective-permute-done.19.refs_6_ = bf16[2,64,256]{2,1,0:T(8,128)(2,1)S(1)} collective-permute-done((bf16[2,64,256]{2,1,0:T(8,128)(2,1)S(1)}, bf16[2,64,256]{2,1,0:T(8,128)(2,1)S(1)}, u32[]{:S(2)}, u32[]{:S(2)}) %collective-permute-start.19) | collective-permute-done | bytes 65568 | tf_op jit(solution)/shard_map/ppermute | solution.py:302
  45.0 2.3 %collective-permute-done.18.refs_5_ = bf16[2,64,256]{2,1,0:T(8,128)(2,1)S(1)} collective-permute-done((bf16[2,64,256]{2,1,0:T(8,128)(2,1)S(1)}, bf16[2,64,256]{2,1,0:T(8,128)(2,1)S(1)}, u32[]{:S(2)}, u32[]{:S(2)}) %collective-permute-start.18) | collective-permute-done | bytes 65568 | tf_op jit(solution)/shard_map/ppermute | solution.py:302
  47.3 2.3 %weight_grads.1 = f32[2,2048,256]{2,1,0:T(8,128)} custom-call(bf16[1,512,256]{2,1,0:T(8,128)(2,1)S(1)} %bitcast.10, bf16[1,512,256]{2,1,0:T(8,128)(2,1)S(1)} %collective-permute-done.15.refs_1_, bf16[2,512,256]{2,1,0:T(8,128)(2,1)S(1)} %collective-permute-done.16.refs_2_, bf16[2,64,256]{2,1,0:T(8,128)(2,1)S(1)} %add_sums.5.refs_3_, ...), custom_call_target="tpu_custom_call" | custom-call | flops 2147483648 | tf_op jit(solution)/shard_map/weight_grads/pallas_call | solution.py:267
  (44 shorter events, 0.6 us)
Async XLA Ops:
  0.6 1.0 %copy-start = (bf16[2,64,1024]{2,1,0:T(8,128)(2,1)S(1)}, bf16[2,64,1024]{2,1,0:T(8,128)(2,1)}, u32[]{:S(2)}) copy-start(bf16[2,64,1024]{2,1,0:T(8,128)(2,1)} %param.14) | copy-start | bytes 786436
  1.6 11.5 %copy-start.4 = (f32[128,64]{0,1:T(8,128)S(1)}, f32[128,64]{0,1:T(8,128)}, u32[]{:S(2)}) copy-start(f32[128,64]{0,1:T(8,128)} %param.12) | copy-start | bytes 98308
  1.6 11.5 %copy-start.5 = (f32[128,64]{0,1:T(8,128)S(1)}, f32[128,64]{0,1:T(8,128)}, u32[]{:S(2)}) copy-start(f32[128,64]{0,1:T(8,128)} %param.13) | copy-start | bytes 98308
  1.6 11.5 %copy-start.6 = (s32[4]{0:T(128)S(1)}, s32[4]{0:T(128)}, u32[]{:S(2)}) copy-start(s32[4]{0:T(128)} %ids.1) | copy-start | bytes 52
  1.6 11.5 %copy-start.7 = (s32[16]{0:T(128)S(1)}, s32[16]{0:T(128)}, u32[]{:S(2)}) copy-start(s32[16]{0:T(128)} %lengths.1) | copy-start | bytes 196
  1.6 11.6 %copy-start.8 = (f32[16]{0:T(128)S(1)}, f32[16]{0:T(128)}, u32[]{:S(2)}) copy-start(f32[16]{0:T(128)} %advantages.1) | copy-start | bytes 196
  1.6 11.6 %copy-start.9 = (s32[16]{0:T(128)S(1)}, s32[16]{0:T(128)}, u32[]{:S(2)}) copy-start(s32[16]{0:T(128)} %adv_index.1) | copy-start | bytes 196
  1.6 12.2 %collective-permute-start.1 = (bf16[2,64,256]{2,1,0:T(8,128)(2,1)S(1)}, bf16[2,64,256]{2,1,0:T(8,128)(2,1)S(1)}, u32[]{:S(2)}, u32[]{:S(2)}) collective-permute-start(bf16[2,64,256]{2,1,0:T(8,128)(2,1)S(1)} %constant_dynamic-slice_fusion), channel_id=1, source_target_pairs={{0,8},{4,12},{8,0},{12,4},{1,9},{5,13},{9,1},{13,5},{2,10},{6,14},... | collective-permute-start | bytes 196616 | tf_op jit(solution)/shard_map/ppermute | solution.py:302
  5.7 8.2 %collective-permute-start = (bf16[2,64,256]{2,1,0:T(8,128)(2,1)S(1)}, bf16[2,64,256]{2,1,0:T(8,128)(2,1)S(1)}, u32[]{:S(2)}, u32[]{:S(2)}) collective-permute-start(bf16[2,64,256]{2,1,0:T(8,128)(2,1)S(1)} %constant_dynamic-slice_fusion), channel_id=1, source_target_pairs={{0,4},{4,0},{8,12},{12,8},{1,5},{5,1},{9,13},{13,9},{2,6},{6,2},{1... | collective-permute-start | bytes 196616 | tf_op jit(solution)/shard_map/ppermute | solution.py:302
  7.3 6.9 %collective-permute-start.2 = (bf16[2,64,256]{2,1,0:T(8,128)(2,1)S(1)}, bf16[2,64,256]{2,1,0:T(8,128)(2,1)S(1)}, u32[]{:S(2)}, u32[]{:S(2)}) collective-permute-start(bf16[2,64,256]{2,1,0:T(8,128)(2,1)S(1)} %constant_dynamic-slice_fusion), channel_id=1, source_target_pairs={{0,12},{4,8},{8,4},{12,0},{1,13},{5,9},{9,5},{13,1},{2,14},{6,10},... | collective-permute-start | bytes 196616 | tf_op jit(solution)/shard_map/ppermute | solution.py:302
  7.3 1.2 %copy-start.3 = (bf16[64,8192]{1,0:T(8,128)(2,1)S(1)}, bf16[64,8192]{1,0:T(8,128)(2,1)}, u32[]{:S(2)}) copy-start(bf16[64,8192]{1,0:T(8,128)(2,1)} %x_ref.1) | copy-start | bytes 3145732
  8.6 14.0 %collective-permute-start.12 = (bf16[64,512]{1,0:T(8,128)(2,1)S(1)}, bf16[64,512]{1,0:T(8,128)(2,1)S(1)}, u32[]{:S(2)}, u32[]{:S(2)}) collective-permute-start(bf16[64,512]{1,0:T(8,128)(2,1)S(1)} %get-tuple-element.72), channel_id=1, source_target_pairs={{0,4},{4,0},{8,12},{12,8},{1,5},{5,1},{9,13},{13,9},{2,6},{6,2},{1... | collective-permute-start | bytes 196616 | tf_op jit(solution)/shard_map/ppermute | solution.py:302
  9.6 13.5 %collective-permute-start.13 = (bf16[64,512]{1,0:T(8,128)(2,1)S(1)}, bf16[64,512]{1,0:T(8,128)(2,1)S(1)}, u32[]{:S(2)}, u32[]{:S(2)}) collective-permute-start(bf16[64,512]{1,0:T(8,128)(2,1)S(1)} %get-tuple-element.73), channel_id=1, source_target_pairs={{0,8},{4,12},{8,0},{12,4},{1,9},{5,13},{9,1},{13,5},{2,10},{6,14},... | collective-permute-start | bytes 196616 | tf_op jit(solution)/shard_map/ppermute | solution.py:302
  13.2 2.6 %copy-start.1 = (bf16[128,8192]{1,0:T(8,128)(2,1)S(1)}, bf16[128,8192]{1,0:T(8,128)(2,1)}, u32[]{:S(2)}) copy-start(bf16[128,8192]{1,0:T(8,128)(2,1)} %q_ref.7) | copy-start | bytes 6291460
  13.2 2.6 %copy-start.2 = (bf16[128,8192]{1,0:T(8,128)(2,1)S(1)}, bf16[128,8192]{1,0:T(8,128)(2,1)}, u32[]{:S(2)}) copy-start(bf16[128,8192]{1,0:T(8,128)(2,1)} %ct_ref.7) | copy-start | bytes 6291460
  13.9 9.2 %collective-permute-start.14 = (bf16[64,512]{1,0:T(8,128)(2,1)S(1)}, bf16[64,512]{1,0:T(8,128)(2,1)S(1)}, u32[]{:S(2)}, u32[]{:S(2)}) collective-permute-start(bf16[64,512]{1,0:T(8,128)(2,1)S(1)} %get-tuple-element.74), channel_id=1, source_target_pairs={{0,12},{4,8},{8,4},{12,0},{1,13},{5,9},{9,5},{13,1},{2,14},{6,10},... | collective-permute-start | bytes 196616 | tf_op jit(solution)/shard_map/ppermute | solution.py:302
  14.2 6.5 %collective-permute-start.5 = (bf16[4,2,64,256]{3,2,1,0:T(8,128)(2,1)S(1)}, bf16[4,2,64,256]{3,2,1,0:T(8,128)(2,1)S(1)}, u32[]{:S(2)}, u32[]{:S(2)}) collective-permute-start(bf16[4,2,64,256]{3,2,1,0:T(8,128)(2,1)S(1)} %pad_maximum_fusion.1.kv_ref), channel_id=1, source_target_pairs={{0,2},{1,3},{2,0},{3,1},{4,6},{5,7},{6,4},{7,5},{8,10},{9,11},{10,... | collective-permute-start | bytes 786440 | tf_op jit(solution)/shard_map/ppermute | solution.py:305
  15.8 1.8 %collective-permute-start.3 = (bf16[4,2,64,256]{3,2,1,0:T(8,128)(2,1)S(1)}, bf16[4,2,64,256]{3,2,1,0:T(8,128)(2,1)S(1)}, u32[]{:S(2)}, u32[]{:S(2)}) collective-permute-start(bf16[4,2,64,256]{3,2,1,0:T(8,128)(2,1)S(1)} %pad_maximum_fusion.1.kv_ref), channel_id=1, source_target_pairs={{0,1},{1,0},{2,3},{3,2},{4,5},{5,4},{6,7},{7,6},{8,9},{9,8},{10,11... | collective-permute-start | bytes 786440 | tf_op jit(solution)/shard_map/ppermute | solution.py:305
  17.6 2.3 %collective-permute-start.4 = (bf16[4,2,64,256]{3,2,1,0:T(8,128)(2,1)S(1)}, bf16[4,2,64,256]{3,2,1,0:T(8,128)(2,1)S(1)}, u32[]{:S(2)}, u32[]{:S(2)}) collective-permute-start(bf16[4,2,64,256]{3,2,1,0:T(8,128)(2,1)S(1)} %get-tuple-element.53), channel_id=1, source_target_pairs={{0,1},{1,0},{2,3},{3,2},{4,5},{5,4},{6,7},{7,6},{8,9},{9,8},{10,11... | collective-permute-start | bytes 786440 | tf_op jit(solution)/shard_map/ppermute | solution.py:305
  20.0 8.3 %collective-permute-start.8 = (bf16[4,2,64,256]{3,2,1,0:T(8,128)(2,1)S(1)}, bf16[4,2,64,256]{3,2,1,0:T(8,128)(2,1)S(1)}, u32[]{:S(2)}, u32[]{:S(2)}) collective-permute-start(bf16[4,2,64,256]{3,2,1,0:T(8,128)(2,1)S(1)} %add_sums.3), channel_id=1, source_target_pairs={{0,2},{1,3},{2,0},{3,1},{4,6},{5,7},{6,4},{7,5},{8,10},{9,11},{10,... | collective-permute-start | bytes 786440 | tf_op jit(solution)/shard_map/ppermute | solution.py:305
  20.7 2.5 %collective-permute-start.6 = (bf16[4,2,64,256]{3,2,1,0:T(8,128)(2,1)S(1)}, bf16[4,2,64,256]{3,2,1,0:T(8,128)(2,1)S(1)}, u32[]{:S(2)}, u32[]{:S(2)}) collective-permute-start(bf16[4,2,64,256]{3,2,1,0:T(8,128)(2,1)S(1)} %collective-permute-done.5.kv_ref), channel_id=1, source_target_pairs={{0,1},{1,0},{2,3},{3,2},{4,5},{5,4},{6,7},{7,6},{8,9},{9,8},{10,11... | collective-permute-start | bytes 786440 | tf_op jit(solution)/shard_map/ppermute | solution.py:305
  22.7 5.6 %collective-permute-start.7 = (bf16[4,2,64,256]{3,2,1,0:T(8,128)(2,1)S(1)}, bf16[4,2,64,256]{3,2,1,0:T(8,128)(2,1)S(1)}, u32[]{:S(2)}, u32[]{:S(2)}) collective-permute-start(bf16[4,2,64,256]{3,2,1,0:T(8,128)(2,1)S(1)} %get-tuple-element.58), channel_id=1, source_target_pairs={{0,1},{1,0},{2,3},{3,2},{4,5},{5,4},{6,7},{7,6},{8,9},{9,8},{10,11... | collective-permute-start | bytes 786440 | tf_op jit(solution)/shard_map/ppermute | solution.py:305
  28.4 9.6 %collective-permute-start.15 = (bf16[1,512,256]{2,1,0:T(8,128)(2,1)S(1)}, bf16[1,512,256]{2,1,0:T(8,128)(2,1)S(1)}, u32[]{:S(2)}, u32[]{:S(2)}) collective-permute-start(bf16[1,512,256]{2,1,0:T(8,128)(2,1)S(1)} %bitcast.8), channel_id=1, source_target_pairs={{0,2},{1,3},{2,0},{3,1},{4,6},{5,7},{6,4},{7,5},{8,10},{9,11},{10,... | collective-permute-start | bytes 786440 | tf_op jit(solution)/shard_map/ppermute | solution.py:305
  29.5 6.1 %collective-permute-start.9 = (bf16[2,64,256]{2,1,0:T(8,128)(2,1)S(1)}, bf16[2,64,256]{2,1,0:T(8,128)(2,1)S(1)}, u32[]{:S(2)}, u32[]{:S(2)}) collective-permute-start(bf16[2,64,256]{2,1,0:T(8,128)(2,1)S(1)} %get-tuple-element.61), channel_id=1, source_target_pairs={{0,12},{4,8},{8,4},{12,0},{1,13},{5,9},{9,5},{13,1},{2,14},{6,10},... | collective-permute-start | bytes 196616 | tf_op jit(solution)/shard_map/ppermute | solution.py:302
  32.6 5.2 %collective-permute-start.10 = (bf16[2,64,256]{2,1,0:T(8,128)(2,1)S(1)}, bf16[2,64,256]{2,1,0:T(8,128)(2,1)S(1)}, u32[]{:S(2)}, u32[]{:S(2)}) collective-permute-start(bf16[2,64,256]{2,1,0:T(8,128)(2,1)S(1)} %get-tuple-element.62), channel_id=1, source_target_pairs={{0,8},{4,12},{8,0},{12,4},{1,9},{5,13},{9,1},{13,5},{2,10},{6,14},... | collective-permute-start | bytes 196616 | tf_op jit(solution)/shard_map/ppermute | solution.py:302
  32.6 5.4 %collective-permute-start.11 = (bf16[2,64,256]{2,1,0:T(8,128)(2,1)S(1)}, bf16[2,64,256]{2,1,0:T(8,128)(2,1)S(1)}, u32[]{:S(2)}, u32[]{:S(2)}) collective-permute-start(bf16[2,64,256]{2,1,0:T(8,128)(2,1)S(1)} %get-tuple-element.63), channel_id=1, source_target_pairs={{0,4},{4,0},{8,12},{12,8},{1,5},{5,1},{9,13},{13,9},{2,6},{6,2},{1... | collective-permute-start | bytes 196616 | tf_op jit(solution)/shard_map/ppermute | solution.py:302
  38.1 9.2 %collective-permute-start.16 = (bf16[2,512,256]{2,1,0:T(8,128)(2,1)S(1)}, bf16[2,512,256]{2,1,0:T(8,128)(2,1)S(1)}, u32[]{:S(2)}, u32[]{:S(2)}) collective-permute-start(bf16[2,512,256]{2,1,0:T(8,128)(2,1)S(1)} %pad_maximum_fusion), channel_id=1, source_target_pairs={{0,1},{1,0},{2,3},{3,2},{4,5},{5,4},{6,7},{7,6},{8,9},{9,8},{10,11... | collective-permute-start | bytes 1572872 | tf_op jit(solution)/shard_map/ppermute | solution.py:305
  38.1 6.9 %collective-permute-start.19 = (bf16[2,64,256]{2,1,0:T(8,128)(2,1)S(1)}, bf16[2,64,256]{2,1,0:T(8,128)(2,1)S(1)}, u32[]{:S(2)}, u32[]{:S(2)}) collective-permute-start(bf16[2,64,256]{2,1,0:T(8,128)(2,1)S(1)} %add_sums.5.refs_3_), channel_id=1, source_target_pairs={{0,12},{4,8},{8,4},{12,0},{1,13},{5,9},{9,5},{13,1},{2,14},{6,10},... | collective-permute-start | bytes 196616 | tf_op jit(solution)/shard_map/ppermute | solution.py:302
  40.3 6.9 %collective-permute-start.18 = (bf16[2,64,256]{2,1,0:T(8,128)(2,1)S(1)}, bf16[2,64,256]{2,1,0:T(8,128)(2,1)S(1)}, u32[]{:S(2)}, u32[]{:S(2)}) collective-permute-start(bf16[2,64,256]{2,1,0:T(8,128)(2,1)S(1)} %add_sums.5.refs_3_), channel_id=1, source_target_pairs={{0,8},{4,12},{8,0},{12,4},{1,9},{5,13},{9,1},{13,5},{2,10},{6,14},... | collective-permute-start | bytes 196616 | tf_op jit(solution)/shard_map/ppermute | solution.py:302
  40.3 6.9 %collective-permute-start.17 = (bf16[2,64,256]{2,1,0:T(8,128)(2,1)S(1)}, bf16[2,64,256]{2,1,0:T(8,128)(2,1)S(1)}, u32[]{:S(2)}, u32[]{:S(2)}) collective-permute-start(bf16[2,64,256]{2,1,0:T(8,128)(2,1)S(1)} %add_sums.5.refs_3_), channel_id=1, source_target_pairs={{0,4},{4,0},{8,12},{12,8},{1,5},{5,1},{9,13},{13,9},{2,6},{6,2},{1... | collective-permute-start | bytes 196616 | tf_op jit(solution)/shard_map/ppermute | solution.py:302
